TPU v7x, 256 devices: a whole 4x4x8 slice. The times are simulated.
256 devices in a mesh: step: 32 (over y, x, z_hi), seq: 8 (over z_lo, core).
Axes of the slice: x: 4, y: 4, z: 8 (z_hi: 2, z_lo: 4; z = z_hi * 4 + z_lo), core: 2. Of those that a mesh axis runs over, the one named last changes fastest.
Arguments:
- trajectory: float32 [32, 4, 256, 3072], P('step', None, 'seq'), may hold values from -6 to 6
- timesteps: int32 [33], replicated, may hold values from 0 to 65, as said below
- offset: int32 [4], replicated, may hold values from 0 to 31, as said below
- mod_table: float32 [66, 3, 3072], replicated, may hold values from -4 to 4
- w_qkv: bfloat16 [3072, 6144], P('step', 'seq'), may hold values from -0.109375 to 0.109375
- w_out: bfloat16 [2048, 3072], P('seq', 'step'), may hold values from -0.25 to 0.25
- query_gain: float32 [128], replicated, may hold values from 1 to 3
- k_gain: float32 [128], replicated, may hold values from 1 to 3
Outputs:
- next_states: float32 [32, 4, 256, 3072], P('step', None, 'seq')
Inputs may be any that keep to these rules, and one draw needn't show every extreme that they name: `timesteps`: strictly rising; first entry 0, last entry 65. Some sequence has offset 0 and another has offset 32 - 1.
All inputs are finite; a program needn't handle non-finite values.
Results may differ from a plain program's by a relative error of at most 0.0065.
Values may be sent and summed in bfloat16 or wider, within the bound.
No kernel may reach another device: no remote copies, remote signals or barrier semaphores. Data moves between devices by JAX's collectives and lax.ppermute only.
A program may use at most 128 MiB of HBM per device.

v0:
```python
import math

import jax
import jax.numpy as jnp
from jax import lax
from jax.sharding import PartitionSpec as P

eps = 1e-06


def entering(x, axis, combine, identity):
    devices, mine = (lax.axis_size(axis), lax.axis_index(axis))
    everything = lax.all_gather(x.astype(jnp.bfloat16), axis)
    start = jnp.broadcast_to(jnp.asarray(identity, x.dtype), x.shape)

    def turn(k, before):
        reached = k < mine
        new = combine(before, everything[k].astype(x.dtype))
        return jnp.where(reached, new, before)

    return lax.fori_loop(0, devices, turn, start)


def spread(x, axis, root):
    mine = lax.axis_index(axis) == root
    return lax.psum(jnp.where(mine, x, jnp.zeros_like(x)), axis)


def normalize(values):
    mean = jnp.mean(values, axis=-1, keepdims=True)
    centered = values - mean
    variance = jnp.mean(centered * centered, axis=-1, keepdims=True)
    return centered * lax.rsqrt(variance + eps)


def rms_norm(values):
    return values * lax.rsqrt(jnp.mean(values * values, axis=-1, keepdims=True) + eps)


def add_terms(earlier, later):
    return earlier + later


def body(trajectory, timesteps, offset, mod_table, w_qkv, w_out, query_gain, k_gain):
    token_place = lax.axis_index("step")
    current = trajectory[0]
    t_now = lax.dynamic_index_in_dim(timesteps, token_place, 0, keepdims=False)
    t_next = lax.dynamic_index_in_dim(timesteps, token_place + 1, 0, keepdims=False)
    total = mod_table.shape[0]
    indicator_rows = (jnp.arange(total, dtype=jnp.int32) == t_now).astype(jnp.float32)
    modulation = jnp.einsum("t,tcd->cd", indicator_rows, mod_table, precision=lax.Precision.HIGHEST)
    hidden = (normalize(current) * (1.0 + modulation[1]) + modulation[0]).astype(jnp.bfloat16)
    w_cols = lax.all_gather(w_qkv, "step", axis=0, tiled=True)
    qkv = jnp.einsum(
        "fvx,xy->fvy",
        lax.all_gather(hidden, "seq", axis=1, tiled=True),
        w_cols,
        preferred_element_type=jnp.float32,
    )
    seqs, length, width = qkv.shape
    head_dim = query_gain.shape[0]
    local_heads = width // (3 * head_dim)
    qkv = qkv.reshape(seqs, length, local_heads, 3, head_dim)
    queries = (rms_norm(qkv[:, :, :, 0, :]) * query_gain).astype(jnp.bfloat16)
    keys = (rms_norm(qkv[:, :, :, 1, :]) * k_gain).astype(jnp.bfloat16)
    values = qkv[:, :, :, 2, :].astype(jnp.bfloat16)
    scores = jnp.einsum(
        "sqhd,skhd->shqk", queries, keys, preferred_element_type=jnp.float32
    ) / math.sqrt(head_dim)
    weights = jax.nn.softmax(scores, axis=-1).astype(jnp.bfloat16)
    attended = jnp.einsum("shqk,skhd->sqhd", weights, values, preferred_element_type=jnp.float32)
    attended = attended.astype(jnp.bfloat16).reshape(seqs, length, local_heads * head_dim)
    w_rows = lax.all_gather(w_out, "step", axis=1, tiled=True)
    returned_value = lax.all_to_all(attended, "seq", split_axis=1, concat_axis=2, tiled=True)
    complete_weight = lax.all_gather(w_rows, "seq", axis=0, tiled=True)
    projected_rows = jnp.einsum(
        "gnf,fe->gne", returned_value, complete_weight, preferred_element_type=jnp.float32
    )
    drift = current + modulation[2] * projected_rows
    step_size = (t_now - t_next).astype(jnp.float32) / total
    increment = step_size * drift
    live = (token_place >= offset)[:, None, None]
    term = jnp.where(live, increment, jnp.float32(0.0))
    before = entering(term, "step", add_terms, jnp.zeros_like(term))
    anchors = []
    for member in range(current.shape[0]):
        anchors.append(spread(current[member], "step", offset[member]))
    anchor = jnp.stack(anchors, axis=0)
    earlier = (token_place < offset)[:, None, None]
    result = jnp.where(earlier, current + increment, anchor + (before + term))
    return result[None]


def solution(mesh):
    return jax.shard_map(
        body,
        mesh=mesh,
        in_specs=(
            P("step", None, "seq", None),
            P(),
            P(),
            P(),
            P("step", "seq"),
            P("seq", "step"),
            P(),
            P(),
        ),
        out_specs=P("step", None, "seq", None),
        check_vma=False,
    )
```

profile of v0, /device:TPU:33, one launch (start us, length us, event | category | flops | bytes accessed | tf_op | source)
XLA Modules:
  0.0 1199.4 jit_solution(9965293334458123162)
XLA Ops:
  6.5 0.7 all-gather.11.cloned.1.call-update
  7.3 0.7 all-gather.9.cloned.1.call-update
  8.1 1.4 fusion.39
  9.4 1.6 fusion.29
  11.0 1.7 reduce_sum.45
  12.7 0.2 copy-done.2
  12.9 0.3 multiply_reduce_fusion.1
  13.3 1.2 add_convert_fusion
  14.5 82.9 %all-gather.11.cloned.1.call-done = bf16[256,3072]{0,1:T(8,128)(2,1)} async-done(((bf16[256,96]{0,1:T(8,128)(2,1)}), bf16[256,3072]{0,1:T(8,128)(2,1)}) %all-gather.11.cloned.1.call-update) | async-done | bytes 1572880 | tf_op jit(solution)/shard_map/all_gather | solution.py:73
  97.5 2.6 copy.31
  100.1 111.7 %all-gather.9.cloned.1.call-done = bf16[3072,768]{1,0:T(8,128)(2,1)} async-done(((bf16[96,768]{1,0:T(8,128)(2,1)}), bf16[3072,768]{1,0:T(8,128)(2,1)}) %all-gather.9.cloned.1.call-update) | async-done | bytes 4718608 | tf_op jit(solution)/shard_map/all_gather | solution.py:53
  211.8 70.6 %all-gather.7.cloned.1.call-done = bf16[4,256,3072]{2,1,0:T(8,128)(2,1)} async-done(((bf16[4,32,3072]{2,1,0:T(8,128)(2,1)}), bf16[4,256,3072]{2,1,0:T(8,128)(2,1)}) %all-gather.7.cloned.1.call-update) | async-done | bytes 6291472 | tf_op jit(solution)/shard_map/all_gather | solution.py:56
  282.4 8.6 fusion.3
  291.1 0.2 multiply_reduce_fusion.3
  291.3 0.5 copy-done.6
  291.8 0.6 fusion.18
  292.3 0.3 copy-done.3
  292.7 1.3 copy-done.4
  294.0 0.6 fusion.41
  294.5 3.0 convolution_convert_fusion
  297.5 1.1 copy.28
  298.6 5.8 all-to-all-start
  305.7 18.9 %all-to-all-done = bf16[4,256,256]{2,0,1:T(4,128)(2,1)S(1)} async-done(((bf16[4,256,256]{2,0,1:T(4,128)(2,1)}), bf16[4,256,256]{2,0,1:T(4,128)(2,1)S(1)}, u32[]{:S(2)}, u32[]{:S(2)}) %all-to-all-start) | async-done | bytes 524320 | tf_op jit(solution)/shard_map/all_to_all | solution.py:74
  324.6 0.1 copy.29
  324.7 102.9 %all-gather.13.cloned.1.call-done = bf16[2048,3072]{1,0:T(8,128)(2,1)} async-done(((bf16[256,3072]{1,0:T(8,128)(2,1)}), bf16[2048,3072]{1,0:T(8,128)(2,1)}) %all-gather.13.cloned.1.call-update) | async-done | bytes 12582928 | tf_op jit(solution)/shard_map/all_gather | solution.py:75
  427.6 8.0 select_convert_fusion
  435.7 0.6 fusion.40
  438.7 1.2 select_bitcast_fusion.3
  439.9 330.1 %all-gather.15.cloned.1.call-done = bf16[128,32,3072]{2,1,0:T(8,128)(2,1)} async-done(((bf16[4,32,3072]{2,1,0:T(8,128)(2,1)}), bf16[128,32,3072]{2,1,0:T(8,128)(2,1)}) %all-gather.15.cloned.1.call-update) | async-done | bytes 25165840 | tf_op jit(solution)/shard_map/all_gather | solution.py:13
  770.1 96.6 %while.14 = (s32[]{:T(128)}, f32[4,32,3072]{2,1,0:T(8,128)}, s32[]{:T(128)}, bf16[32,4,32,3072]{3,2,1,0:T(8,128)(2,1)}, s32[]{:T(128)}, /*index=5*/s32[]{:T(128)}) while((s32[]{:T(128)}, f32[4,32,3072]{2,1,0:T(8,128)}, s32[]{:T(128)}, bf16[32,4,32,3072]{3,2,1,0:T(8,128)(2,1)}, s32[]{:T(128)}, /*index=5*/s32[]{:T(128)}) %tuple.61), condition=%wide.region_11.12_spmd.clone, body=%wide.region_10.11_spmd.clone.sunk | while | flops 1572868 | bytes 3932253 | solution.py:21
  770.1 2.6 add_select_fusion.2
  772.6 3.0 add_select_fusion.2
  775.6 3.0 add_select_fusion.2
  778.7 3.0 add_select_fusion.2
  781.7 3.0 add_select_fusion.2
  784.7 3.0 add_select_fusion.2
  787.8 3.0 add_select_fusion.2
  790.8 3.0 add_select_fusion.2
  793.8 3.0 add_select_fusion.2
  796.9 3.0 add_select_fusion.2
  799.9 3.0 add_select_fusion.2
  802.9 3.1 add_select_fusion.2
  806.0 3.0 add_select_fusion.2
  809.0 3.0 add_select_fusion.2
  812.1 3.0 add_select_fusion.2
  815.1 3.0 add_select_fusion.2
  818.1 3.0 add_select_fusion.2
  821.2 3.0 add_select_fusion.2
  824.2 3.0 add_select_fusion.2
  827.2 3.0 add_select_fusion.2
  830.3 3.0 add_select_fusion.2
  833.3 3.0 add_select_fusion.2
  836.3 3.0 add_select_fusion.2
  839.4 3.0 add_select_fusion.2
  842.4 3.0 add_select_fusion.2
  845.4 3.0 add_select_fusion.2
  848.5 3.0 add_select_fusion.2
  851.5 3.0 add_select_fusion.2
  854.5 3.0 add_select_fusion.2
  857.6 3.0 add_select_fusion.2
  860.6 3.0 add_select_fusion.2
  863.6 3.0 add_select_fusion.2
  866.7 321.2 %all-reduce.3.cloned.1.call-done = (f32[1,32,3072]{2,1,0:T(8,128)}, f32[1,32,3072]{2,1,0:T(8,128)}, f32[1,32,3072]{2,1,0:T(8,128)}, f32[1,32,3072]{2,1,0:T(8,128)}) async-done(((f32[1,32,3072]{2,1,0:T(8,128)}, f32[1,32,3072]{2,1,0:T(8,128)}, f32[1,32,3072]{2,1,0:T(8,128)}, f32[1,32,3072]{2,1,0:T(8,128)}), (f32[1,32,3072]{2,1,0:T(8,128)}, f32[1,32,3072]{2,1,0:T(8,128)}, f32[1,32,3072]{2,1,0:T(8,128)}, ...) | async-done | bytes 1572880 | tf_op jit(solution)/shard_map/psum | solution.py:26
  1187.8 4.7 fusion.16
  (30 shorter events, 0.5 us)
Async XLA Ops:
  6.5 2.9 copy-start
  6.5 90.9 %all-gather.11.cloned.1.call-start = ((), (), s32[]{:S(2)}) async-start(), calls=%async_computation.3 | async-start | bytes 1622016 | tf_op jit(solution)/shard_map/all_gather | solution.py:73
  7.3 204.5 %all-gather.9.cloned.1.call-start = ((), (), s32[]{:S(2)}) async-start(), calls=%async_computation.2 | async-start | bytes 4866048 | tf_op jit(solution)/shard_map/all_gather | solution.py:53
  8.0 274.4 %all-gather.7.cloned.1.call-start = ((), (), s32[]{:S(2)}) async-start(), calls=%async_computation.1 | async-start | bytes 7077888 | tf_op jit(solution)/shard_map/all_gather | solution.py:56
  11.0 1.9 copy-start.2
  14.5 413.1 %all-gather.13.cloned.1.call-start = ((), (), s32[]{:S(2)}) async-start(), calls=%async_computation.4 | async-start | bytes 14155776 | tf_op jit(solution)/shard_map/all_gather | solution.py:75
  291.0 1.6 copy-start.3
  291.0 0.7 copy-start.6
  291.0 0.7 copy-start.7
  292.7 1.3 copy-start.4
  297.5 8.1 copy-start.5
  298.6 26.0 %all-to-all-start = ((bf16[4,256,256]{2,0,1:T(4,128)(2,1)}), bf16[4,256,256]{2,0,1:T(4,128)(2,1)S(1)}, u32[]{:S(2)}, u32[]{:S(2)}) async-start(bf16[4,256,256]{2,0,1:T(4,128)(2,1)} %copy.28), calls=%async_computation | async-start | bytes 1048576 | tf_op jit(solution)/shard_map/all_to_all | solution.py:74
  304.4 465.7 %all-gather.15.cloned.1.call-start = ((), (), s32[]{:S(2)}) async-start(), calls=%async_computation.5 | async-start | bytes 25952256 | tf_op jit(solution)/shard_map/all_gather | solution.py:13
  435.6 752.2 %all-reduce.3.cloned.1.call-start = ((), (), s32[]{:S(2)}) async-start(), calls=%async_computation.6 | async-start | bytes 3145728 | tf_op jit(solution)/shard_map/psum | solution.py:26
  1187.8 4.7 copy-start.1
Sparse Core Ops, SparseCore 0:
  10.8 86.5 all-gather.10
  101.0 110.7 all-gather.8
  213.6 68.7 all-gather.6
  284.0 143.5 all-gather.12
  435.7 334.2 all-gather.14
  772.8 415.0 all-reduce.2
where the time goes:
time: 1220 us; the launch traced here: 1200 us
  waiting for transfers between devices  1040 us (85%)
  other arithmetic  107 us (9%)
  matrix products  21.7 us (2%)
  between operations  17.3 us (1%)
    all_gather x1, waiting for transfers between devices, entering(): everything = lax.all_gather(x.astype(jnp.bfloat16), axis)  330 us
    psum x1, waiting for transfers between devices, spread(): return lax.psum(jnp.where(mine, x, jnp.zeros_like(x)), axis)  321 us
    all_gather x1, waiting for transfers between devices, body(): w_cols = lax.all_gather(w_qkv, 'step', axis=0, tiled=True)  112 us
    all_gather x1, waiting for transfers between devices, body(): complete_weight = lax.all_gather(w_rows, 'seq', axis=0, tiled=True)  103 us
    select_n x32, other arithmetic, turn(): return jnp.where(reached, new, before)  96.6 us
    all_gather x1, waiting for transfers between devices, body(): w_rows = lax.all_gather(w_out, 'step', axis=1, tiled=True)  82.9 us
    all_gather x1, waiting for transfers between devices, body(): lax.all_gather(hidden, 'seq', axis=1, tiled=True)  70.6 us
  transfers between devices with their start and end apart: 7, of which 7 were waited for; matrix products, arithmetic and copies ran while one was open for 10% of the time, Pallas kernels for 0%

commit v1 on v0

v1 whole, which is shorter than its diff:
```python
import math

import jax
import jax.numpy as jnp
import numpy as np
from jax import lax
from jax.experimental import pallas as pl
from jax.experimental.pallas import tpu as pltpu
from jax.sharding import Mesh, PartitionSpec as P

eps = 1e-06
AXES = ("y", "x", "h", "z", "c")
NY, NX, NH, NZ, NC = 4, 4, 2, 4, 2
D = 3072
SEQS = 4
ROWS = 32
HEAD = 128
COLS = D // (NX * NC)
TS = 4
BF = jnp.bfloat16
F32 = jnp.float32
VMEM_LIMIT = 48 * 1024 * 1024


def flat(y, x, h, z, c):
    return (((y * NX + x) * NH + h) * NZ + z) * NC + c


def every():
    for y in range(NY):
        for x in range(NX):
            for h in range(NH):
                for z in range(NZ):
                    for c in range(NC):
                        yield y, x, h, z, c


SWAP_XZ = [(flat(*d), flat(d[0], d[3], d[2], d[1], d[4])) for d in every()]
SWAP_YX = [(flat(*d), flat(d[1], d[0], d[2], d[3], d[4])) for d in every()]


def spread(v, axes, parts):
    copies = jnp.broadcast_to(v[None], (parts,) + v.shape)
    return lax.all_to_all(copies, axes, 0, 0)


def other_core(v):
    return lax.ppermute(v, "c", [(0, 1), (1, 0)])


def call(kernel, out_shape, **rest):
    return pl.pallas_call(
        kernel,
        out_shape=out_shape,
        compiler_params=pltpu.CompilerParams(vmem_limit_bytes=VMEM_LIMIT),
        **rest,
    )


def enter_kernel(cur_ref, mod_ref, hidden_ref, state_ref):
    values = cur_ref[0]
    mean = jnp.mean(values, axis=-1, keepdims=True)
    centered = values - mean
    variance = jnp.mean(centered * centered, axis=-1, keepdims=True)
    normal = centered * lax.rsqrt(variance + eps)
    hidden = normal * (1.0 + mod_ref[1:2, :]) + mod_ref[0:1, :]
    hidden_ref[0] = hidden.astype(BF)
    for x in range(NX):
        for c in range(NC):
            at = (x * NC + c) * COLS
            state_ref[x, 0, c] = values[:, at : at + COLS].astype(BF)


def enter(cur, mod):
    return call(
        enter_kernel,
        (
            jax.ShapeDtypeStruct((SEQS, ROWS, D), BF),
            jax.ShapeDtypeStruct((NX, SEQS, NC, ROWS, COLS), BF),
        ),
        grid=(SEQS,),
        in_specs=[
            pl.BlockSpec((1, ROWS, D), lambda s: (s, 0, 0)),
            pl.BlockSpec((3, D), lambda s: (0, 0)),
        ],
        out_specs=(
            pl.BlockSpec((1, ROWS, D), lambda s: (s, 0, 0)),
            pl.BlockSpec((NX, 1, NC, ROWS, COLS), lambda s: (0, s, 0, 0, 0)),
        ),
    )(cur, mod)


def dot(a, b):
    return lax.dot_general(a, b, (((1,), (0,)), ((), ())), preferred_element_type=F32)


def dot_t(a, b):
    return lax.dot_general(a, b, (((1,), (1,)), ((), ())), preferred_element_type=F32)


def rms(values, gain):
    scale = lax.rsqrt(jnp.mean(values * values, axis=-1, keepdims=True) + eps)
    return (values * scale * gain).astype(BF)


def attend_kernel(mine_ref, other_ref, wa_ref, wb_ref, qg_ref, kg_ref, att_ref):
    count, rows = mine_ref.shape[0], mine_ref.shape[1]
    halves = []
    for ref in (mine_ref, other_ref):
        tokens = ref[...].reshape(count * rows, D)
        halves.append((dot(tokens, wa_ref[...]), dot(tokens, wb_ref[...])))

    def part(index, column):
        side = 0 if column < 4 else 1
        at = (column - 4 * side) * HEAD
        here = slice(index * rows, (index + 1) * rows)
        return jnp.concatenate([half[side][here, at : at + HEAD] for half in halves], 0)

    for index in range(count):
        for head in range(2):
            queries = rms(part(index, 3 * head), qg_ref[...])
            keys = rms(part(index, 3 * head + 1), kg_ref[...])
            values = part(index, 3 * head + 2).astype(BF)
            scores = dot_t(queries, keys) * (1.0 / math.sqrt(HEAD))
            scores = jnp.exp(scores - jnp.max(scores, axis=-1, keepdims=True))
            weights = scores / jnp.sum(scores, axis=-1, keepdims=True)
            result = dot(weights.astype(BF), values).astype(BF)
            at = head * HEAD
            att_ref[0, index, :, at : at + HEAD] = result[:rows]
            att_ref[1, index, :, at : at + HEAD] = result[rows:]


def attend(mine, other, wa, wb, qg, kg):
    rows = NZ * ROWS
    step = 2
    whole = lambda *shape: pl.BlockSpec(shape, lambda i: (0,) * len(shape))
    return call(
        attend_kernel,
        jax.ShapeDtypeStruct((2, TS, rows, 2 * HEAD), BF),
        grid=(TS // step,),
        in_specs=[
            pl.BlockSpec((step, rows, D), lambda i: (i, 0, 0)),
            pl.BlockSpec((step, rows, D), lambda i: (i, 0, 0)),
            whole(D, 4 * HEAD),
            whole(D, 2 * HEAD),
            whole(1, HEAD),
            whole(1, HEAD),
        ],
        out_specs=pl.BlockSpec((2, step, rows, 2 * HEAD), lambda i: (0, i, 0, 0)),
    )(mine, other, wa, wb, qg, kg)


def project_kernel(
    ints_ref, floats_ref, att_ref, sib_ref, wm_ref, ws_ref, state_ref, gate_ref, perm_ref, out_ref
):
    rows = NZ * ROWS
    core = ints_ref[0]
    for half in range(2):
        total = None
        for group in range(NX):
            a = att_ref[group, half].reshape(TS * rows, 2 * HEAD)
            b = sib_ref[group, 1 - half].reshape(TS * rows, 2 * HEAD)
            term = dot_t(a, wm_ref[group]) + dot_t(b, ws_ref[group])
            total = term if total is None else total + term
        token_core = core if half == 0 else 1 - core
        values = []
        for t in range(TS):
            projected = total[t * rows : (t + 1) * rows]
            state = state_ref[t, :, token_core].reshape(rows, COLS).astype(F32)
            step, first = floats_ref[t], floats_ref[TS + t]
            increment = step * (state + gate_ref[t : t + 1, :] * projected)
            values.append((increment + first * state).astype(BF).reshape(NZ, ROWS, COLS))
        for z in range(NZ):
            block = jnp.concatenate([v[z] for v in values], 0)
            moved = dot(perm_ref[...], block).astype(BF)
            out_ref[:, z, token_core] = moved.reshape(NY * NH, TS * 4, COLS)


def prefix_kernel(lower_ref, terms_ref, out_ref):
    for c in range(NC):
        terms = terms_ref[:, c].reshape(NY * NH * SEQS * 16, COLS)
        total = dot(lower_ref[...], terms).astype(BF)
        out_ref[:, :, c * COLS : (c + 1) * COLS] = total.reshape(32, 16, COLS)


def leave_kernel(early_ref, got_ref, cur_ref, perm_ref, out_ref):
    got = got_ref[:, 0].reshape(NY * NH * 16, 2 * COLS)
    total = dot(perm_ref[...], got).reshape(SEQS, ROWS, 2 * COLS)
    for s in range(SEQS):
        out_ref[0, s] = total[s] + jnp.where(early_ref[s] > 0, cur_ref[0, s], 0.0)


def row_orders():
    out = np.zeros((128, 128), np.float32)
    back = np.zeros((128, 128), np.float32)
    for part in range(8):
        for a in range(4):
            for t in range(4):
                out[part * 16 + a * 4 + t, a * 32 + part * 4 + t] = 1
                back[a * 32 + part * 4 + t, part * 16 + a * 4 + t] = 1
    return jnp.asarray(out, BF), jnp.asarray(back, BF)


def lower_matrix(offset):
    row, col = np.arange(512), np.arange(512)
    k, s, t = row // 16, (row // 4) % 4, row % 4
    y, h, s2, x, t2 = col // 128, (col // 64) % 2, (col // 16) % 4, (col // 4) % 4, col % 4
    j = (y * NX + x) * NH + h
    same = (s[:, None] == s2[None]) & (t[:, None] == t2[None])
    start = jnp.tile(jnp.repeat(offset, 4), 32)[:, None]
    kk, jj = jnp.asarray(k)[:, None], jnp.asarray(j)[None]
    late = (jj >= start) & (jj <= kk)
    taken = jnp.where(kk >= start, late, jj == kk)
    return (taken & jnp.asarray(same)).astype(BF)


def body(trajectory, timesteps, offset, mod_table, w_qkv, w_out, query_gain, k_gain):
    y, x, h, z, c = (lax.axis_index(a) for a in AXES)
    total = mod_table.shape[0]
    step_of = lambda index: lax.dynamic_index_in_dim(timesteps, index, 0, keepdims=False)
    row_of = lambda index: lax.dynamic_index_in_dim(mod_table, step_of(index), 0, keepdims=False)
    mine = (y * NX + x) * NH + h

    wq = lax.ppermute(w_qkv, AXES, SWAP_XZ)
    hidden, state = enter(trajectory[0], row_of(mine))
    tokens = lax.all_to_all(hidden, "z", 0, 0)

    wa = spread(wq[:, : 4 * HEAD], ("z", "h"), NZ * NH).reshape(-1, 4 * HEAD)
    wa = spread(wa, "y", NY).reshape(D, 4 * HEAD)
    wb = spread(wq[:, 4 * HEAD :], "y", NY)
    wb = lax.all_gather(wb, ("z", "h"), axis=1).reshape(D, 2 * HEAD)

    gathered = spread(tokens.reshape(NZ * ROWS, D), "x", NX)
    other = other_core(gathered)

    state = lax.all_to_all(
        state.reshape(NX * SEQS * NC, ROWS, COLS), ("x", "z", "c"), 0, 0
    ).reshape(NX, NZ, NC, ROWS, COLS)

    wo = lax.ppermute(w_out.T, AXES, SWAP_YX)
    wo = spread(wo, ("z", "h"), NZ * NH).reshape(NZ * NH * 96, 2 * HEAD)
    wo = spread(wo, "y", NY).reshape(NY, NZ, NH, 96, 2 * HEAD)
    pick = lambda core: (
        lax.dynamic_slice_in_dim(wo, 2 * core, 2, 0)
        .transpose(1, 0, 2, 3, 4)
        .reshape(NZ, COLS, 2 * HEAD)
    )
    wo_mine = pick(c)
    wo_other = other_core(pick(1 - c))

    attended = attend(gathered, other, wa, wb, query_gain[None], k_gain[None])
    attended = spread(attended, "x", NX)
    sibling = other_core(attended)

    ks = (y * NX + jnp.arange(TS, dtype=jnp.int32)) * NH + h
    sizes = (timesteps[ks] - timesteps[ks + 1]).astype(F32) / total
    first = (ks == offset[z]).astype(F32)
    gates = lax.dynamic_slice_in_dim(
        jnp.stack([row_of(ks[t])[2] for t in range(TS)]), (x * NC + c) * COLS, COLS, 1
    )
    outward, back = row_orders()
    smem = pl.BlockSpec(memory_space=pltpu.SMEM)
    vmem = pl.BlockSpec(memory_space=pltpu.VMEM)
    terms = call(
        project_kernel,
        jax.ShapeDtypeStruct((NY * NH, NZ, NC, TS * 4, COLS), BF),
        in_specs=[smem, smem] + [vmem] * 7,
        out_specs=vmem,
    )(
        c.astype(jnp.int32)[None],
        jnp.concatenate([sizes, first]),
        attended,
        sibling,
        wo_mine,
        wo_other,
        state,
        gates,
        outward,
    )
    terms = lax.all_to_all(terms.reshape(64, TS * 4, COLS), ("y", "h", "z", "c"), 0, 0)
    sums = call(
        prefix_kernel,
        jax.ShapeDtypeStruct((32, 16, 2 * COLS), BF),
        in_specs=[vmem, vmem],
        out_specs=vmem,
    )(lower_matrix(offset), terms.reshape(32, NC, 16, COLS))
    got = lax.all_to_all(sums, ("y", "x", "h"), 0, 0)
    early = (mine < offset).astype(jnp.int32)
    return call(
        leave_kernel,
        jax.ShapeDtypeStruct((1, SEQS, ROWS, D), F32),
        grid=(NX,),
        in_specs=[
            smem,
            pl.BlockSpec((NY, 1, NH, 16, 2 * COLS), lambda i: (0, i, 0, 0, 0)),
            pl.BlockSpec((1, SEQS, ROWS, 2 * COLS), lambda i: (0, 0, 0, i)),
            pl.BlockSpec((128, 128), lambda i: (0, 0)),
        ],
        out_specs=pl.BlockSpec((1, SEQS, ROWS, 2 * COLS), lambda i: (0, 0, 0, i)),
    )(early, got.reshape(NY, NX, NH, 16, 2 * COLS), trajectory, back)


def solution(mesh):
    fine = Mesh(mesh.devices.reshape(NY, NX, NH, NZ, NC), AXES)
    steps, places = ("y", "x", "h"), ("z", "c")
    return jax.shard_map(
        body,
        mesh=fine,
        in_specs=(
            P(steps, None, places, None),
            P(),
            P(),
            P(),
            P(steps, places),
            P(places, steps),
            P(),
            P(),
        ),
        out_specs=P(steps, None, places, None),
        check_vma=False,
    )
```

time: 1220 us -> 415 us (0.34); the launches traced: 1200 us -> 413 us
  waiting for transfers between devices: 1040 us -> 216 us
  other arithmetic: 107 us -> 1.28 us
  starting transfers between devices: 5.92 us -> 65.1 us
  blocking collectives: 0 us -> 51.3 us
  matrix products: 21.7 us -> 0 us
  local copies, waits for them, and re-layouts: 8.12 us -> 29 us
  Pallas kernels: 0 us -> 19.5 us
  between operations: 17.3 us -> 31.1 us
    all_gather x5 -> x1, waiting for transfers between devices: 698 us -> 58.5 us  [body(): wb = lax.all_gather(wb, ('z', 'h'), axis=1).reshape(D, 2 * HEAD)]
    psum x1 -> x0, waiting for transfers between devices: 321 us -> none  [spread(): return lax.psum(jnp.where(mine, x, jnp.zeros_like(x)), axis)]
    all_to_all x1 -> x9, waiting for transfers between devices: 18.9 us -> 157 us  [the longest x6 105 us: spread(): return lax.all_to_all(copies, axes, 0, 0)]
    select_n x32 -> x1, other arithmetic: 96.6 us -> 0.01 us  [body(): sizes = (timesteps[ks] - timesteps[ks + 1]).astype(F32) / total]
    all_to_all x0 -> x2, blocking collectives: none -> 51.3 us  [the longest x1 28.6 us: spread(): return lax.all_to_all(copies, axes, 0, 0)]
    all_to_all x1 -> x9, starting transfers between devices: 5.75 us -> 55.3 us  [the longest x6 31.1 us: spread(): return lax.all_to_all(copies, axes, 0, 0)]
    dot_general x5 -> x0, matrix products: 21.7 us -> none  [the longest x1 8.61 us: body(): jnp.einsum('fvx,xy->fvy', lax.all_gather(hidden, 'seq', axis=1, tiled=Tru...]
    pallas_call x0 -> x5, Pallas kernels: none -> 19.5 us  [the longest x1 9.21 us: attend(): call(attend_kernel, jax.ShapeDtypeStruct((2, TS, rows, 2 * HEAD), BF), gr...]
  transfers between devices with their start and end apart: 7 -> 15, of which waited for: 7 -> 9; matrix products, arithmetic and copies ran while one was open for 10% -> 4% of each run, Pallas kernels for 0% -> 3%
where the time goes in v1:
time: 415 us; the launch traced here: 413 us
  waiting for transfers between devices  216 us (52%)
  starting transfers between devices  65.1 us (16%)
  blocking collectives  51.3 us (12%)
  between operations  31.1 us (7%)
  local copies, waits for them, and re-layouts  29 us (7%)
  Pallas kernels  19.5 us (5%)
    all_to_all x6, waiting for transfers between devices, spread(): return lax.all_to_all(copies, axes, 0, 0)  105 us
    all_gather x1, waiting for transfers between devices, body(): wb = lax.all_gather(wb, ('z', 'h'), axis=1).reshape(D, 2 * HEAD)  58.5 us
    all_to_all x6, starting transfers between devices, spread(): return lax.all_to_all(copies, axes, 0, 0)  31.1 us
    all_to_all x1, blocking collectives, spread(): return lax.all_to_all(copies, axes, 0, 0)  28.6 us
    all_to_all x1, waiting for transfers between devices, body(): got = lax.all_to_all(sums, ('y', 'x', 'h'), 0, 0)  27.8 us
    all_to_all x1, blocking collectives, body(): tokens = lax.all_to_all(hidden, 'z', 0, 0)  22.7 us
    all_to_all x1, waiting for transfers between devices, body(): lax.all_to_all(terms.reshape(64, TS * 4, COLS), ('y', 'h', 'z', 'c'), 0, 0)  21.4 us
    all_to_all x1, starting transfers between devices, body(): lax.all_to_all(terms.reshape(64, TS * 4, COLS), ('y', 'h', 'z', 'c'), 0, 0)  10.5 us
  transfers between devices with their start and end apart: 15, of which 9 were waited for; matrix products, arithmetic and copies ran while one was open for 4% of the time, Pallas kernels for 3%

profile of v1, /device:TPU:33, one launch (start us, length us, event | category | flops | bytes accessed | tf_op | source)
XLA Modules:
  0.0 413.3 jit_solution(3555742885850049841)
XLA Ops:
  6.5 2.7 collective-permute-start.1
  9.2 1.2 dynamic_slice.44
  10.4 0.7 compare_convert_fusion
  11.1 0.6 fusion.6
  19.3 1.5 fusion.5
  22.8 0.7 broadcast_in_dim.77
  23.5 4.2 %all-to-all-start.4 = ((bf16[4,96,256]{2,1,0:T(8,128)(2,1)}), bf16[4,96,256]{2,1,0:T(8,128)(2,1)S(1)}, u32[]{:S(2)}, u32[]{:S(2)}) async-start(bf16[4,96,256]{2,1,0:T(8,128)(2,1)} %broadcast_in_dim.77), calls=%async_computation.4 | async-start | bytes 393216 | tf_op jit(solution)/shard_map/all_to_all | solution.py:44
  27.7 1.0 constant_dynamic-slice_fusion
  28.7 0.0 copy-start
  28.7 1.4 copy-done
  30.1 1.3 shard_map.127
  31.4 0.9 copy-done.6
  32.3 0.6 all-to-all-done.4
  32.9 22.7 %all_to_all.55 = bf16[4,32,3072]{2,1,0:T(8,128)(2,1)S(1)} all-to-all(bf16[4,32,3072]{2,1,0:T(8,128)(2,1)S(1)} %get-tuple-element.7), channel_id=1, replica_groups=mesh['y'=4,'x'=4,'h'=2,'z'=4,'c'=2] {'z'}, dimensions={0} | all-to-all | bytes 1572864 | tf_op jit(solution)/shard_map/all_to_all | solution.py:226
  55.6 2.0 broadcast_in_dim.73
  57.6 3.9 all-to-all-start.1
  61.5 34.9 %all-to-all-done.1.mine_ref = bf16[4,128,3072]{2,1,0:T(8,128)(2,1)S(1)} async-done(((bf16[4,128,3072]{2,1,0:T(8,128)(2,1)}), bf16[4,128,3072]{2,1,0:T(8,128)(2,1)S(1)}, u32[]{:S(2)}, u32[]{:S(2)}) %all-to-all-start.1) | async-done | bytes 3145760 | tf_op jit(solution)/shard_map/all_to_all | solution.py:44
  96.3 0.9 broadcast_in_dim.74
  97.3 10.5 %all-to-all-start.2 = ((bf16[8,96,512]{2,1,0:T(8,128)(2,1)}), bf16[8,96,512]{2,1,0:T(8,128)(2,1)}, u32[]{:S(2)}, u32[]{:S(2)}) async-start(bf16[8,96,512]{2,1,0:T(8,128)(2,1)} %broadcast_in_dim.74), calls=%async_computation.2 | async-start | bytes 1572864 | tf_op jit(solution)/shard_map/all_to_all | solution.py:44
  107.8 3.6 collective-permute-start
  111.3 17.9 %all-to-all-done.2 = bf16[8,96,512]{2,1,0:T(8,128)(2,1)} async-done(((bf16[8,96,512]{2,1,0:T(8,128)(2,1)}), bf16[8,96,512]{2,1,0:T(8,128)(2,1)}, u32[]{:S(2)}, u32[]{:S(2)}) %all-to-all-start.2) | async-done | bytes 786464 | tf_op jit(solution)/shard_map/all_to_all | solution.py:44
  129.2 3.1 broadcast_in_dim.76
  132.3 4.8 %all-to-all-start.3 = ((bf16[4,768,512]{2,1,0:T(8,128)(2,1)}), bf16[4,768,512]{2,1,0:T(8,128)(2,1)}, u32[]{:S(2)}, u32[]{:S(2)}) async-start(bf16[4,768,512]{2,1,0:T(8,128)(2,1)} %broadcast_in_dim.76), calls=%async_computation.3 | async-start | bytes 6291456 | tf_op jit(solution)/shard_map/all_to_all | solution.py:44
  137.1 0.0 all-gather.3.cloned.1.call-start
  137.1 0.7 all-gather.3.cloned.1.call-update
  137.8 0.7 collective-permute-start.3
  138.5 35.8 %all-to-all-done.3 = bf16[4,768,512]{2,1,0:T(8,128)(2,1)} async-done(((bf16[4,768,512]{2,1,0:T(8,128)(2,1)}), bf16[4,768,512]{2,1,0:T(8,128)(2,1)}, u32[]{:S(2)}, u32[]{:S(2)}) %all-to-all-start.3) | async-done | bytes 3145760 | tf_op jit(solution)/shard_map/all_to_all | solution.py:44
  174.3 0.8 broadcast_in_dim.81
  175.1 3.4 all-to-all-start.6
  178.5 58.5 %all-gather.3.cloned.1.call-done = bf16[4,768,256]{2,1,0:T(8,128)(2,1)} async-done(((bf16[4,96,256]{2,1,0:T(8,128)(2,1)}), bf16[4,768,256]{2,1,0:T(8,128)(2,1)}) %all-gather.3.cloned.1.call-update) | async-done | bytes 1572880 | tf_op jit(solution)/shard_map/all_gather | solution.py:231
  237.1 1.4 copy-done.5
  238.5 9.2 %shard_map.128 = bf16[2,4,128,256]{3,2,1,0:T(8,128)(2,1)S(1)} custom-call(bf16[4,128,3072]{2,1,0:T(8,128)(2,1)S(1)} %all-to-all-done.1.mine_ref, bf16[4,128,3072]{2,1,0:T(8,128)(2,1)} %collective-permute-done.other_ref, bf16[3072,512]{1,0:T(8,128)(2,1)} %bitcast.8.wa_ref, bf16[3072,256]{1,0:T(8,128)(2,1)S(1)} %bitcast.53, f32[1,128]{1,0:T(1,128)S(1)} %bitcast.56, ...), custom_call_target="tpu_custom_call" | custom-call | tf_op jit(solution)/shard_map/pallas_call | solution.py:137
  247.7 0.8 copy-done.4
  248.5 1.3 broadcast_in_dim.80
  249.8 28.6 %all_to_all.56.att_ref = bf16[4,2,4,128,256]{4,3,2,1,0:T(8,128)(2,1)S(1)} all-to-all(bf16[4,2,4,128,256]{4,3,2,1,0:T(8,128)(2,1)S(1)} %broadcast_in_dim.80), channel_id=1, replica_groups=mesh['y'=4,'x'=4,'h'=2,'z'=4,'c'=2] {'x'}, dimensions={0} | all-to-all | bytes 4194304 | tf_op jit(solution)/shard_map/all_to_all | solution.py:44
  278.4 1.2 broadcast_in_dim.83
  279.6 4.4 %all-to-all-start.7 = ((bf16[4,768,256]{2,1,0:T(8,128)(2,1)}), bf16[4,768,256]{2,1,0:T(8,128)(2,1)}, u32[]{:S(2)}, u32[]{:S(2)}) async-start(bf16[4,768,256]{2,1,0:T(8,128)(2,1)} %broadcast_in_dim.83), calls=%async_computation.7 | async-start | bytes 3145728 | tf_op jit(solution)/shard_map/all_to_all | solution.py:44
  284.0 2.6 collective-permute-start.2
  286.6 15.8 %all-to-all-done.7 = bf16[4,768,256]{2,1,0:T(8,128)(2,1)} async-done(((bf16[4,768,256]{2,1,0:T(8,128)(2,1)}), bf16[4,768,256]{2,1,0:T(8,128)(2,1)}, u32[]{:S(2)}, u32[]{:S(2)}) %all-to-all-start.7) | async-done | bytes 1572896 | tf_op jit(solution)/shard_map/all_to_all | solution.py:44
  302.3 7.1 %all-to-all-start.8 = ((bf16[32,32,384]{2,1,0:T(8,128)(2,1)}), bf16[32,32,384]{2,1,0:T(8,128)(2,1)S(1)}, u32[]{:S(2)}, u32[]{:S(2)}) async-start(bf16[32,32,384]{2,1,0:T(8,128)(2,1)} %bitcast.54), calls=%async_computation.8 | async-start | bytes 1572864 | tf_op jit(solution)/shard_map/all_to_all | solution.py:236
  314.7 2.4 dynamic-slice_bitcast_fusion
  317.1 0.9 copy.15
  318.1 0.4 collective-permute-start.4
  318.4 0.6 gather_fusion
  319.1 0.6 gather_fusion.1
  322.4 0.1 pad_maximum_fusion.floats_ref
  322.4 1.1 dynamic-slice_bitcast_fusion.2
  323.5 0.1 fusion.2.gate_ref
  323.6 2.1 copy.14
  325.7 2.6 all-to-all-done.8
  328.3 1.1 copy-done.3
  329.4 4.7 %shard_map.129 = bf16[8,4,2,16,384]{4,3,2,1,0:T(8,128)(2,1)S(1)} custom-call(s32[1]{0:T(128)} %bitcast.ints_ref, f32[8]{0:T(128)S(1)} %pad_maximum_fusion.floats_ref, bf16[4,2,4,128,256]{4,3,2,1,0:T(8,128)(2,1)S(1)} %all_to_all.56.att_ref, bf16[4,2,4,128,256]{4,3,2,1,0:T(8,128)(2,1)} %collective-permute-done.2.sib_ref, bf16[4,384,256]{2,1,0:T(8,128)(2,1)S(1)} %bitcast.52, ...), custom_call_target="tpu_custom_call" | custom-call | tf_op jit(solution)/shard_map/pallas_call | solution.py:264
  334.1 0.9 copy-done.2
  335.0 10.5 %all-to-all-start.9 = ((bf16[64,16,384]{2,1,0:T(8,128)(2,1)}), bf16[64,16,384]{2,1,0:T(8,128)(2,1)S(1)}, u32[]{:S(2)}, u32[]{:S(2)}) async-start(bf16[64,16,384]{2,1,0:T(8,128)(2,1)} %bitcast.51), calls=%async_computation.9 | async-start | bytes 1572864 | tf_op jit(solution)/shard_map/all_to_all | solution.py:280
  345.5 0.1 broadcast_in_dim.33
  345.6 0.1 tile.7
  345.7 0.1 broadcast_in_dim_tile.3
  345.8 0.0 copy-start.7
  345.8 0.4 and_convert_fusion.lower_ref
  346.3 21.4 %all-to-all-done.9 = bf16[64,16,384]{2,1,0:T(8,128)(2,1)S(1)} async-done(((bf16[64,16,384]{2,1,0:T(8,128)(2,1)}), bf16[64,16,384]{2,1,0:T(8,128)(2,1)S(1)}, u32[]{:S(2)}, u32[]{:S(2)}) %all-to-all-start.9) | async-done | bytes 786464 | tf_op jit(solution)/shard_map/all_to_all | solution.py:280
  367.7 1.6 shard_map.130
  369.3 6.6 %all-to-all-start.10 = ((bf16[32,16,768]{2,1,0:T(8,128)(2,1)}), bf16[32,16,768]{2,1,0:T(8,128)(2,1)S(1)}, u32[]{:S(2)}, u32[]{:S(2)}) async-start(bf16[32,16,768]{2,1,0:T(8,128)(2,1)} %shard_map.130), calls=%async_computation.10 | async-start | bytes 1572864 | tf_op jit(solution)/shard_map/all_to_all | solution.py:287
  375.9 27.8 %all-to-all-done.10 = bf16[32,16,768]{2,1,0:T(8,128)(2,1)S(1)} async-done(((bf16[32,16,768]{2,1,0:T(8,128)(2,1)}), bf16[32,16,768]{2,1,0:T(8,128)(2,1)S(1)}, u32[]{:S(2)}, u32[]{:S(2)}) %all-to-all-start.10) | async-done | bytes 786464 | tf_op jit(solution)/shard_map/all_to_all | solution.py:287
  403.7 2.7 shard_map.131
  (44 shorter events, 0.1 us)
Async XLA Ops:
  6.5 16.3 %collective-permute-start.1 = (bf16[96,768]{1,0:T(8,128)(2,1)}, bf16[96,768]{1,0:T(8,128)(2,1)S(1)}, u32[]{:S(2)}, u32[]{:S(2)}) collective-permute-start(bf16[96,768]{1,0:T(8,128)(2,1)} %param.17), channel_id=1, source_target_pairs={{0,0},{1,1},{2,16},{3,17},{4,32},{5,33},{6,48},{7,49},{8,8},{9,9},... | collective-permute-start | bytes 442376 | tf_op jit(solution)/shard_map/ppermute | solution.py:224
  23.5 9.4 %all-to-all-start.4 = ((bf16[4,96,256]{2,1,0:T(8,128)(2,1)}), bf16[4,96,256]{2,1,0:T(8,128)(2,1)S(1)}, u32[]{:S(2)}, u32[]{:S(2)}) async-start(bf16[4,96,256]{2,1,0:T(8,128)(2,1)} %broadcast_in_dim.77), calls=%async_computation.4 | async-start | bytes 393216 | tf_op jit(solution)/shard_map/all_to_all | solution.py:44
  28.7 1.4 copy-start
  31.4 0.9 copy-start.6
  32.9 24.7 %copy-start.12 = (bf16[4,96,256]{2,1,0:T(8,128)(2,1)}, bf16[4,96,256]{2,1,0:T(8,128)(2,1)S(1)}, u32[]{:S(2)}) copy-start(bf16[4,96,256]{2,1,0:T(8,128)(2,1)S(1)} %all-to-all-done.4) | copy-start | bytes 589828
  57.6 38.8 %all-to-all-start.1 = ((bf16[4,128,3072]{2,1,0:T(8,128)(2,1)}), bf16[4,128,3072]{2,1,0:T(8,128)(2,1)S(1)}, u32[]{:S(2)}, u32[]{:S(2)}) async-start(bf16[4,128,3072]{2,1,0:T(8,128)(2,1)} %broadcast_in_dim.73), calls=%async_computation.1 | async-start | bytes 6291456 | tf_op jit(solution)/shard_map/all_to_all | solution.py:44
  97.3 31.9 %all-to-all-start.2 = ((bf16[8,96,512]{2,1,0:T(8,128)(2,1)}), bf16[8,96,512]{2,1,0:T(8,128)(2,1)}, u32[]{:S(2)}, u32[]{:S(2)}) async-start(bf16[8,96,512]{2,1,0:T(8,128)(2,1)} %broadcast_in_dim.74), calls=%async_computation.2 | async-start | bytes 1572864 | tf_op jit(solution)/shard_map/all_to_all | solution.py:44
  107.8 129.3 %collective-permute-start = (bf16[4,128,3072]{2,1,0:T(8,128)(2,1)S(1)}, bf16[4,128,3072]{2,1,0:T(8,128)(2,1)}, u32[]{:S(2)}, u32[]{:S(2)}) collective-permute-start(bf16[4,128,3072]{2,1,0:T(8,128)(2,1)S(1)} %all-to-all-done.1.mine_ref), channel_id=1, source_target_pairs={{0,1},{1,0},{2,3},{3,2},{4,5},{5,4},{6,7},{7,6},{8,9},{9,8},{10,11... | collective-permute-start | bytes 9437192 | tf_op jit(solution)/shard_map/ppermute | solution.py:48
  132.3 5.5 %copy-start.17 = (bf16[256,96]{0,1:T(8,128)(2,1)S(1)}, bf16[256,96]{0,1:T(8,128)(2,1)}, u32[]{:S(2)}) copy-start(bf16[256,96]{0,1:T(8,128)(2,1)} %param.18) | copy-start | bytes 147460
  132.3 104.7 %copy-start.9 = (f32[128]{0:T(128)S(1)}, f32[128]{0:T(128)}, u32[]{:S(2)}) copy-start(f32[128]{0:T(128)} %param.19) | copy-start | bytes 1540
  132.3 104.8 %copy-start.10 = (f32[128]{0:T(128)S(1)}, f32[128]{0:T(128)}, u32[]{:S(2)}) copy-start(f32[128]{0:T(128)} %param.20) | copy-start | bytes 1540
  132.3 42.0 %all-to-all-start.3 = ((bf16[4,768,512]{2,1,0:T(8,128)(2,1)}), bf16[4,768,512]{2,1,0:T(8,128)(2,1)}, u32[]{:S(2)}, u32[]{:S(2)}) async-start(bf16[4,768,512]{2,1,0:T(8,128)(2,1)} %broadcast_in_dim.76), calls=%async_computation.3 | async-start | bytes 6291456 | tf_op jit(solution)/shard_map/all_to_all | solution.py:44
  137.1 100.0 %all-gather.3.cloned.1.call-start = ((), (), s32[]{:S(2)}) async-start(), calls=%async_computation.11 | async-start | bytes 1769472 | tf_op jit(solution)/shard_map/all_gather | solution.py:231
  137.8 0.7 collective-permute-start.3
  175.1 73.4 %all-to-all-start.6 = ((bf16[8,96,256]{2,1,0:T(8,128)(2,1)}), bf16[8,96,256]{2,1,0:T(8,128)(2,1)S(1)}, u32[]{:S(2)}, u32[]{:S(2)}) async-start(bf16[8,96,256]{2,1,0:T(8,128)(2,1)} %broadcast_in_dim.81), calls=%async_computation.6 | async-start | bytes 786432 | tf_op jit(solution)/shard_map/all_to_all | solution.py:44
  237.0 1.4 copy-start.5
  247.7 0.8 copy-start.4
  279.6 22.7 %all-to-all-start.7 = ((bf16[4,768,256]{2,1,0:T(8,128)(2,1)}), bf16[4,768,256]{2,1,0:T(8,128)(2,1)}, u32[]{:S(2)}, u32[]{:S(2)}) async-start(bf16[4,768,256]{2,1,0:T(8,128)(2,1)} %broadcast_in_dim.83), calls=%async_computation.7 | async-start | bytes 3145728 | tf_op jit(solution)/shard_map/all_to_all | solution.py:44
  284.0 44.3 %collective-permute-start.2 = (bf16[4,2,4,128,256]{4,3,2,1,0:T(8,128)(2,1)S(1)}, bf16[4,2,4,128,256]{4,3,2,1,0:T(8,128)(2,1)}, u32[]{:S(2)}, u32[]{:S(2)}) collective-permute-start(bf16[4,2,4,128,256]{4,3,2,1,0:T(8,128)(2,1)S(1)} %all_to_all.56.att_ref), channel_id=1, source_target_pairs={{0,1},{1,0},{2,3},{3,2},{4,5},{5,4},{6,7},{7,6},{8,9},{9,8},{10,11... | collective-permute-start | bytes 6291464 | tf_op jit(solution)/shard_map/ppermute | solution.py:48
  302.3 25.9 %all-to-all-start.8 = ((bf16[32,32,384]{2,1,0:T(8,128)(2,1)}), bf16[32,32,384]{2,1,0:T(8,128)(2,1)S(1)}, u32[]{:S(2)}, u32[]{:S(2)}) async-start(bf16[32,32,384]{2,1,0:T(8,128)(2,1)} %bitcast.54), calls=%async_computation.8 | async-start | bytes 1572864 | tf_op jit(solution)/shard_map/all_to_all | solution.py:236
  314.7 3.7 copy-start.11
  317.1 11.1 %copy-start.8 = (bf16[128,128]{1,0:T(8,128)(2,1)S(1)}, bf16[128,128]{1,0:T(8,128)(2,1)}, u32[]{:S(2)}) copy-start(bf16[128,128]{1,0:T(8,128)(2,1)} %constant.76.clone.perm_ref) | copy-start | bytes 98308
  318.1 10.2 %collective-permute-start.4 = (bf16[4,384,256]{2,1,0:T(8,128)(2,1)}, bf16[4,384,256]{2,1,0:T(8,128)(2,1)}, u32[]{:S(2)}, u32[]{:S(2)}) collective-permute-start(bf16[4,384,256]{2,1,0:T(8,128)(2,1)} %bitcast.18), channel_id=1, source_target_pairs={{0,1},{1,0},{2,3},{3,2},{4,5},{5,4},{6,7},{7,6},{8,9},{9,8},{10,11... | collective-permute-start | bytes 2359304 | tf_op jit(solution)/shard_map/ppermute | solution.py:48
  328.3 1.1 copy-start.3
  329.4 16.1 %copy-start.16 = (s32[4]{0:T(128)S(1)}, s32[4]{0:T(128)}, u32[]{:S(2)}) copy-start(s32[4]{0:T(128)} %param.15) | copy-start | bytes 52
  329.4 16.4 %copy-start.14 = (s32[512]{0:T(512)S(1)}, s32[512]{0:T(512)}, u32[]{:S(2)}) copy-start(s32[512]{0:T(512)} %constant.78.clone) | copy-start | bytes 6148
  329.4 16.4 %copy-start.13 = (pred[512,512]{1,0:T(32,128)(4,1)S(1)}, pred[512,512]{1,0:T(32,128)(4,1)}, u32[]{:S(2)}) copy-start(pred[512,512]{1,0:T(32,128)(4,1)} %constant.80.clone) | copy-start | bytes 786436
  329.4 16.4 %copy-start.15 = (s32[512]{0:T(512)S(1)}, s32[512]{0:T(512)}, u32[]{:S(2)}) copy-start(s32[512]{0:T(512)} %constant.79.clone) | copy-start | bytes 6148
  334.1 0.9 copy-start.2
  335.0 32.7 %all-to-all-start.9 = ((bf16[64,16,384]{2,1,0:T(8,128)(2,1)}), bf16[64,16,384]{2,1,0:T(8,128)(2,1)S(1)}, u32[]{:S(2)}, u32[]{:S(2)}) async-start(bf16[64,16,384]{2,1,0:T(8,128)(2,1)} %bitcast.51), calls=%async_computation.9 | async-start | bytes 1572864 | tf_op jit(solution)/shard_map/all_to_all | solution.py:280
  345.8 57.8 %copy-start.1 = (f32[1,4,32,3072]{3,2,1,0:T(8,128)S(1)}, f32[1,4,32,3072]{3,2,1,0:T(8,128)}, u32[]{:S(2)}) copy-start(f32[1,4,32,3072]{3,2,1,0:T(8,128)} %cur_ref.1) | copy-start | bytes 4718596
  345.8 57.8 %copy-start.7 = (bf16[128,128]{1,0:T(8,128)(2,1)S(1)}, bf16[128,128]{1,0:T(8,128)(2,1)}, u32[]{:S(2)}) copy-start(bf16[128,128]{1,0:T(8,128)(2,1)} %constant.77.clone.perm_ref) | copy-start | bytes 98308
  369.3 34.4 %all-to-all-start.10 = ((bf16[32,16,768]{2,1,0:T(8,128)(2,1)}), bf16[32,16,768]{2,1,0:T(8,128)(2,1)S(1)}, u32[]{:S(2)}, u32[]{:S(2)}) async-start(bf16[32,16,768]{2,1,0:T(8,128)(2,1)} %shard_map.130), calls=%async_computation.10 | async-start | bytes 1572864 | tf_op jit(solution)/shard_map/all_to_all | solution.py:287
Sparse Core Ops, SparseCore 0:
  139.7 97.2 all-gather.2

commit v2 on v1

--- a/solution.py
+++ b/solution.py
@@ -20,6 +20,7 @@
 BF = jnp.bfloat16
 F32 = jnp.float32
 VMEM_LIMIT = 48 * 1024 * 1024
+AWAY = (0, 3, 1, 2)
 
 
 def flat(y, x, h, z, c):
@@ -46,6 +47,30 @@
 
 def other_core(v):
     return lax.ppermute(v, "c", [(0, 1), (1, 0)])
+
+
+def shift(v, axis, size, away):
+    return lax.ppermute(v, axis, [(i, (i + away) % size) for i in range(size)])
+
+
+def ring(v, axis, size, first, second):
+    before = shift(v, axis, size, 1)
+    after = shift(v, axis, size, -1)
+    far = (shift(first(before), axis, size, 1), shift(second(after), axis, size, -1))
+    return (v, before, after) + far
+
+
+def halves(v):
+    n = v.shape[0] // 2
+    return v[:n], v[n:]
+
+
+def ring_rows(v, axis, size):
+    return ring(v, axis, size, lambda b: halves(b)[0], lambda b: halves(b)[1])
+
+
+def after(v, other):
+    return lax.optimization_barrier((v, other))[0]
 
 
 def call(kernel, out_shape, **rest):
@@ -103,76 +128,101 @@
     return (values * scale * gain).astype(BF)
 
 
-def attend_kernel(mine_ref, other_ref, wa_ref, wb_ref, qg_ref, kg_ref, att_ref):
-    count, rows = mine_ref.shape[0], mine_ref.shape[1]
-    halves = []
-    for ref in (mine_ref, other_ref):
-        tokens = ref[...].reshape(count * rows, D)
-        halves.append((dot(tokens, wa_ref[...]), dot(tokens, wb_ref[...])))
+def attend_kernel(ints_ref, *refs):
+    mine, others, weights = refs[0:5], refs[5:10], refs[10:15]
+    qg_ref, kg_ref, att_ref, tokens_ref, qkv_ref = refs[15:]
+    rows = NZ * ROWS
+    half = rows // 2
+    for side, pieces in enumerate((mine, others)):
+        for place in range(3):
+            tokens_ref[side * TS + place] = pieces[place][...]
+        tokens_ref[side * TS + 3, :half] = pieces[3][...]
+        tokens_ref[side * TS + 3, half:] = pieces[4][...]
+    y = ints_ref[0]
+    wide = D // NY
+    starts = [y * wide]
+    for away in (NY - 1, 1):
+        starts.append(lax.rem(y + away, NY) * wide)
+    starts.append(lax.rem(y + 2, NY) * wide)
+    starts.append(starts[3] + wide // 2)
+    for place, weight in enumerate(weights):
+        depth = weight.shape[0]
+        columns = pl.ds(pl.multiple_of(starts[place], HEAD), depth)
+        term = dot(tokens_ref[:, :, columns].reshape(2 * TS * rows, depth), weight[...])
+        if place == 0:
+            qkv_ref[...] = term
+        else:
+            qkv_ref[...] += term
 
     def part(index, column):
-        side = 0 if column < 4 else 1
-        at = (column - 4 * side) * HEAD
-        here = slice(index * rows, (index + 1) * rows)
-        return jnp.concatenate([half[side][here, at : at + HEAD] for half in halves], 0)
-
-    for index in range(count):
+        at = column * HEAD
+        first, second = index * rows, (TS + index) * rows
+        return jnp.concatenate(
+            [qkv_ref[first : first + rows, at : at + HEAD], qkv_ref[second : second + rows, at : at + HEAD]], 0
+        )
+
+    for index in range(TS):
         for head in range(2):
             queries = rms(part(index, 3 * head), qg_ref[...])
             keys = rms(part(index, 3 * head + 1), kg_ref[...])
             values = part(index, 3 * head + 2).astype(BF)
             scores = dot_t(queries, keys) * (1.0 / math.sqrt(HEAD))
             scores = jnp.exp(scores - jnp.max(scores, axis=-1, keepdims=True))
-            weights = scores / jnp.sum(scores, axis=-1, keepdims=True)
-            result = dot(weights.astype(BF), values).astype(BF)
+            share = scores / jnp.sum(scores, axis=-1, keepdims=True)
+            result = dot(share.astype(BF), values).astype(BF)
             at = head * HEAD
             att_ref[0, index, :, at : at + HEAD] = result[:rows]
             att_ref[1, index, :, at : at + HEAD] = result[rows:]
 
 
-def attend(mine, other, wa, wb, qg, kg):
+def attend(y, mine, others, weights, qg, kg):
     rows = NZ * ROWS
-    step = 2
-    whole = lambda *shape: pl.BlockSpec(shape, lambda i: (0,) * len(shape))
+    smem = pl.BlockSpec(memory_space=pltpu.SMEM)
+    vmem = pl.BlockSpec(memory_space=pltpu.VMEM)
     return call(
         attend_kernel,
         jax.ShapeDtypeStruct((2, TS, rows, 2 * HEAD), BF),
-        grid=(TS // step,),
-        in_specs=[
-            pl.BlockSpec((step, rows, D), lambda i: (i, 0, 0)),
-            pl.BlockSpec((step, rows, D), lambda i: (i, 0, 0)),
-            whole(D, 4 * HEAD),
-            whole(D, 2 * HEAD),
-            whole(1, HEAD),
-            whole(1, HEAD),
+        in_specs=[smem] + [vmem] * 17,
+        out_specs=vmem,
+        scratch_shapes=[
+            pltpu.VMEM((2 * TS, rows, D), BF),
+            pltpu.VMEM((2 * TS * rows, 6 * HEAD), F32),
         ],
-        out_specs=pl.BlockSpec((2, step, rows, 2 * HEAD), lambda i: (0, i, 0, 0)),
-    )(mine, other, wa, wb, qg, kg)
-
-
-def project_kernel(
-    ints_ref, floats_ref, att_ref, sib_ref, wm_ref, ws_ref, state_ref, gate_ref, perm_ref, out_ref
-):
+    )(y[None], *mine, *others, *weights, qg, kg)
+
+
+def project_kernel(ints_ref, floats_ref, *refs):
+    att, sib = refs[0:5], refs[5:10]
+    wm_ref, ws_ref, state_ref, gate_ref, perm_ref, out_ref = refs[10:]
     rows = NZ * ROWS
-    core = ints_ref[0]
+    core, x = ints_ref[0], ints_ref[1]
+
+    def block(pieces, place, half):
+        if place < 3:
+            return pieces[place][half].reshape(TS * rows, 2 * HEAD)
+        return pieces[3 + half][...].reshape(TS * rows, 2 * HEAD)
+
     for half in range(2):
-        total = None
-        for group in range(NX):
-            a = att_ref[group, half].reshape(TS * rows, 2 * HEAD)
-            b = sib_ref[group, 1 - half].reshape(TS * rows, 2 * HEAD)
+        totals = [None] * TS
+        for place, away in enumerate(AWAY):
+            group = lax.rem(x + away, NX)
+            a = block(att, place, half)
+            b = block(sib, place, 1 - half)
             term = dot_t(a, wm_ref[group]) + dot_t(b, ws_ref[group])
-            total = term if total is None else total + term
+            for j in range(TS):
+                at = AWAY.index((j - away) % NX) * rows
+                piece = term[at : at + rows]
+                totals[j] = piece if totals[j] is None else totals[j] + piece
         token_core = core if half == 0 else 1 - core
         values = []
-        for t in range(TS):
-            projected = total[t * rows : (t + 1) * rows]
-            state = state_ref[t, :, token_core].reshape(rows, COLS).astype(F32)
-            step, first = floats_ref[t], floats_ref[TS + t]
-            increment = step * (state + gate_ref[t : t + 1, :] * projected)
+        for j in range(TS):
+            state = state_ref[lax.rem(x + j, NX), :, token_core].reshape(rows, COLS).astype(F32)
+            step, first = floats_ref[j], floats_ref[TS + j]
+            increment = step * (state + gate_ref[j : j + 1, :] * totals[j])
             values.append((increment + first * state).astype(BF).reshape(NZ, ROWS, COLS))
         for z in range(NZ):
-            block = jnp.concatenate([v[z] for v in values], 0)
-            moved = dot(perm_ref[...], block).astype(BF)
+            stacked = jnp.concatenate([v[z] for v in values], 0)
+            moved = dot(perm_ref[...], stacked).astype(BF)
             out_ref[:, z, token_core] = moved.reshape(NY * NH, TS * 4, COLS)
 
 
@@ -201,14 +251,14 @@
     return jnp.asarray(out, BF), jnp.asarray(back, BF)
 
 
-def lower_matrix(offset):
+def lower_matrix(offset, here):
     row, col = np.arange(512), np.arange(512)
     k, s, t = row // 16, (row // 4) % 4, row % 4
     y, h, s2, x, t2 = col // 128, (col // 64) % 2, (col // 16) % 4, (col // 4) % 4, col % 4
-    j = (y * NX + x) * NH + h
+    j = (jnp.asarray(y) * NX + lax.rem(jnp.asarray(x) + here, NX)) * NH + jnp.asarray(h)
     same = (s[:, None] == s2[None]) & (t[:, None] == t2[None])
     start = jnp.tile(jnp.repeat(offset, 4), 32)[:, None]
-    kk, jj = jnp.asarray(k)[:, None], jnp.asarray(j)[None]
+    kk, jj = jnp.asarray(k)[:, None], j[None]
     late = (jj >= start) & (jj <= kk)
     taken = jnp.where(kk >= start, late, jj == kk)
     return (taken & jnp.asarray(same)).astype(BF)
@@ -222,37 +272,39 @@
     mine = (y * NX + x) * NH + h
 
     wq = lax.ppermute(w_qkv, AXES, SWAP_XZ)
+    wo = lax.ppermute(w_out.T, AXES, SWAP_YX)
     hidden, state = enter(trajectory[0], row_of(mine))
     tokens = lax.all_to_all(hidden, "z", 0, 0)
 
-    wa = spread(wq[:, : 4 * HEAD], ("z", "h"), NZ * NH).reshape(-1, 4 * HEAD)
-    wa = spread(wa, "y", NY).reshape(D, 4 * HEAD)
-    wb = spread(wq[:, 4 * HEAD :], "y", NY)
-    wb = lax.all_gather(wb, ("z", "h"), axis=1).reshape(D, 2 * HEAD)
-
-    gathered = spread(tokens.reshape(NZ * ROWS, D), "x", NX)
-    other = other_core(gathered)
-
+    wq = spread(after(wq, tokens), ("z", "h"), NZ * NH).reshape(-1, 6 * HEAD)
+    weights = ring_rows(wq, "y", NY)
+
+    tokens = ring_rows(tokens.reshape(NZ * ROWS, D), "x", NX)
+    others = [other_core(v) for v in tokens]
+
+    wo = spread(after(wo, wq), ("z", "h"), NZ * NH).reshape(NZ * NH * 96, 2 * HEAD)
     state = lax.all_to_all(
-        state.reshape(NX * SEQS * NC, ROWS, COLS), ("x", "z", "c"), 0, 0
+        after(state, wo).reshape(NX * SEQS * NC, ROWS, COLS), ("x", "z", "c"), 0, 0
     ).reshape(NX, NZ, NC, ROWS, COLS)
 
-    wo = lax.ppermute(w_out.T, AXES, SWAP_YX)
-    wo = spread(wo, ("z", "h"), NZ * NH).reshape(NZ * NH * 96, 2 * HEAD)
-    wo = spread(wo, "y", NY).reshape(NY, NZ, NH, 96, 2 * HEAD)
-    pick = lambda core: (
-        lax.dynamic_slice_in_dim(wo, 2 * core, 2, 0)
-        .transpose(1, 0, 2, 3, 4)
-        .reshape(NZ, COLS, 2 * HEAD)
-    )
+    attended = attend(after(y, state), tokens, others, weights, query_gain[None], k_gain[None])
+
+    wo = ring_rows(wo, "y", NY)
+    wo = jnp.stack(wo[:3] + (jnp.concatenate(wo[3:], 0),))
+    wo = wo.reshape(NY, NZ, NH, 96, 2 * HEAD)
+    place = jnp.array([AWAY.index(i) for i in range(NY)], jnp.int32)
+
+    def pick(core):
+        both = [wo[place[lax.rem(2 * core + i - y + NY, NY)]] for i in range(2)]
+        return jnp.stack(both, 1).reshape(NZ, COLS, 2 * HEAD)
+
     wo_mine = pick(c)
     wo_other = other_core(pick(1 - c))
 
-    attended = attend(gathered, other, wa, wb, query_gain[None], k_gain[None])
-    attended = spread(attended, "x", NX)
-    sibling = other_core(attended)
-
-    ks = (y * NX + jnp.arange(TS, dtype=jnp.int32)) * NH + h
+    attended = ring(attended, "x", NX, lambda b: b[0], lambda b: b[1])
+    sibling = [other_core(v) for v in attended]
+
+    ks = (y * NX + lax.rem(x + jnp.arange(TS, dtype=jnp.int32), NX)) * NH + h
     sizes = (timesteps[ks] - timesteps[ks + 1]).astype(F32) / total
     first = (ks == offset[z]).astype(F32)
     gates = lax.dynamic_slice_in_dim(
@@ -264,13 +316,13 @@
     terms = call(
         project_kernel,
         jax.ShapeDtypeStruct((NY * NH, NZ, NC, TS * 4, COLS), BF),
-        in_specs=[smem, smem] + [vmem] * 7,
+        in_specs=[smem, smem] + [vmem] * 15,
         out_specs=vmem,
     )(
-        c.astype(jnp.int32)[None],
+        jnp.stack([c, x]).astype(jnp.int32),
         jnp.concatenate([sizes, first]),
-        attended,
-        sibling,
+        *attended,
+        *sibling,
         wo_mine,
         wo_other,
         state,
@@ -283,7 +335,7 @@
         jax.ShapeDtypeStruct((32, 16, 2 * COLS), BF),
         in_specs=[vmem, vmem],
         out_specs=vmem,
-    )(lower_matrix(offset), terms.reshape(32, NC, 16, COLS))
+    )(lower_matrix(offset, x), terms.reshape(32, NC, 16, COLS))
     got = lax.all_to_all(sums, ("y", "x", "h"), 0, 0)
     early = (mine < offset).astype(jnp.int32)
     return call(

time: 415 us -> 287 us (0.69)
  waiting for transfers between devices: 216 us -> 119 us
  blocking collectives: 51.3 us -> 0 us
  starting transfers between devices: 65.1 us -> 94.1 us
  local copies, waits for them, and re-layouts: 29 us -> 17.1 us
  between operations: 31.1 us -> 24.4 us
  Pallas kernels: 19.5 us -> 24.9 us
  other arithmetic: 1.28 us -> 6.27 us
    all_to_all x6 -> x2, waiting for transfers between devices: 105 us -> 28.9 us  [spread(): return lax.all_to_all(copies, axes, 0, 0)]
    all_gather x1 -> x0, waiting for transfers between devices: 58.5 us -> none  [body(): wb = lax.all_gather(wb, ('z', 'h'), axis=1).reshape(D, 2 * HEAD)]
    all_to_all x2 -> x0, blocking collectives: 51.3 us -> none  [the longest x1 28.6 us: spread(): return lax.all_to_all(copies, axes, 0, 0)]
    ppermute x0 -> x16, starting transfers between devices: none -> 28.8 us  [shift(): return lax.ppermute(v, axis, [(i, (i + away) % size) for i in range(size)])]
    ppermute x0 -> x16, waiting for transfers between devices: none -> 26.9 us  [shift(): return lax.ppermute(v, axis, [(i, (i + away) % size) for i in range(size)])]
    all_to_all x6 -> x2, starting transfers between devices: 31.1 us -> 15.5 us  [spread(): return lax.all_to_all(copies, axes, 0, 0)]
    ppermute x1, waiting for transfers between devices: 0.01 us -> 14.2 us  [body(): wq = lax.ppermute(w_qkv, AXES, SWAP_XZ)]
    all_to_all x1 -> x2, starting transfers between devices: 7.09 us -> 15.4 us  [the longest x1 9.96 us: body(): lax.all_to_all(after(state, wo).reshape(NX * SEQS * NC, ROWS, COLS), ('x'...]
  transfers between devices with their start and end apart: 15 -> 35, of which waited for: 9 -> 9; matrix products, arithmetic and copies ran while one was open for 4% -> 5% of each run, Pallas kernels for 3% -> 0%
where the time goes in v2:
time: 287 us; the launch traced here: 286 us
  waiting for transfers between devices  119 us (41%)
  starting transfers between devices  94.1 us (33%)
  Pallas kernels  24.9 us (9%)
  between operations  24.4 us (9%)
  local copies, waits for them, and re-layouts  17.1 us (6%)
  other arithmetic  6.27 us (2%)
    all_to_all x2, waiting for transfers between devices, spread(): return lax.all_to_all(copies, axes, 0, 0)  28.9 us
    ppermute x16, starting transfers between devices, shift(): return lax.ppermute(v, axis, [(i, (i + away) % size) for i in range(size)])  28.8 us
    all_to_all x1, waiting for transfers between devices, body(): got = lax.all_to_all(sums, ('y', 'x', 'h'), 0, 0)  27.8 us
    ppermute x16, waiting for transfers between devices, shift(): return lax.ppermute(v, axis, [(i, (i + away) % size) for i in range(size)])  26.9 us
    all_to_all x1, waiting for transfers between devices, body(): lax.all_to_all(terms.reshape(64, TS * 4, COLS), ('y', 'h', 'z', 'c'), 0, 0)  21.4 us
    all_to_all x2, starting transfers between devices, spread(): return lax.all_to_all(copies, axes, 0, 0)  15.5 us
    ppermute x1, waiting for transfers between devices, body(): wq = lax.ppermute(w_qkv, AXES, SWAP_XZ)  14.2 us
    ppermute x11, starting transfers between devices, other_core(): return lax.ppermute(v, 'c', [(0, 1), (1, 0)])  12.9 us
  transfers between devices with their start and end apart: 35, of which 9 were waited for; matrix products, arithmetic and copies ran while one was open for 5% of the time, Pallas kernels for 0%

profile of v2, /device:TPU:33, one launch (start us, length us, event | category | flops | bytes accessed | tf_op | source)
XLA Modules:
  0.0 286.0 jit_solution(12504081392172748815)
XLA Ops:
  0.0 1.2 dynamic_slice.62
  1.2 0.7 compare_convert_fusion
  1.9 0.6 fusion.19
  10.1 1.5 fusion.18
  13.6 1.0 constant_dynamic-slice_fusion
  14.6 1.4 copy-done
  16.0 2.4 shard_map.154
  18.5 5.4 %all-to-all-start = ((bf16[4,32,3072]{2,1,0:T(8,128)(2,1)}), bf16[4,32,3072]{2,1,0:T(8,128)(2,1)S(1)}, u32[]{:S(2)}, u32[]{:S(2)}) async-start(bf16[4,32,3072]{2,1,0:T(8,128)(2,1)} %get-tuple-element.12), calls=%async_computation | async-start | bytes 1572864 | tf_op jit(solution)/shard_map/all_to_all | solution.py:277
  23.9 3.0 %collective-permute-start.1 = (bf16[96,768]{1,0:T(8,128)(2,1)S(1)}, bf16[96,768]{1,0:T(8,128)(2,1)S(1)}, u32[]{:S(2)}, u32[]{:S(2)}) collective-permute-start(bf16[96,768]{1,0:T(8,128)(2,1)S(1)} %copy-done.24), channel_id=1, source_target_pairs={{0,0},{1,1},{2,16},{3,17},{4,32},{5,33},{6,48},{7,49},{8,8},{9,9},... | collective-permute-start | bytes 442376 | tf_op jit(solution)/shard_map/ppermute | solution.py:274
  26.9 14.2 %collective-permute-done.1 = bf16[96,768]{1,0:T(8,128)(2,1)S(1)} collective-permute-done((bf16[96,768]{1,0:T(8,128)(2,1)S(1)}, bf16[96,768]{1,0:T(8,128)(2,1)S(1)}, u32[]{:S(2)}, u32[]{:S(2)}) %collective-permute-start.1) | collective-permute-done | bytes 147488 | tf_op jit(solution)/shard_map/ppermute | solution.py:274
  41.1 1.1 broadcast_in_dim.38
  42.2 12.0 %all-to-all-start.1 = ((bf16[8,96,768]{2,1,0:T(8,128)(2,1)}), bf16[8,96,768]{2,1,0:T(8,128)(2,1)}, u32[]{:S(2)}, u32[]{:S(2)}) async-start(bf16[8,96,768]{2,1,0:T(8,128)(2,1)} %broadcast_in_dim.38), calls=%async_computation.1 | async-start | bytes 2359296 | tf_op jit(solution)/shard_map/all_to_all | solution.py:45
  54.2 3.7 %collective-permute-start.2 = (bf16[128,3072]{1,0:T(8,128)(2,1)S(1)}, bf16[128,3072]{1,0:T(8,128)(2,1)S(1)}, u32[]{:S(2)}, u32[]{:S(2)}) collective-permute-start(bf16[128,3072]{1,0:T(8,128)(2,1)S(1)} %bitcast.63), channel_id=1, source_target_pairs={{0,16},{16,32},{32,48},{48,0},{1,17},{17,33},{33,49},{49,1},{2,18}... | collective-permute-start | bytes 2359304 | tf_op jit(solution)/shard_map/ppermute | solution.py:53
  57.8 0.7 collective-permute-start
  58.5 24.6 %all-to-all-done.1 = bf16[8,96,768]{2,1,0:T(8,128)(2,1)} async-done(((bf16[8,96,768]{2,1,0:T(8,128)(2,1)}), bf16[8,96,768]{2,1,0:T(8,128)(2,1)}, u32[]{:S(2)}, u32[]{:S(2)}) %all-to-all-start.1) | async-done | bytes 1179680 | tf_op jit(solution)/shard_map/all_to_all | solution.py:45
  83.1 0.8 broadcast_in_dim.39
  83.9 3.5 %all-to-all-start.2 = ((bf16[8,96,256]{2,1,0:T(8,128)(2,1)}), bf16[8,96,256]{2,1,0:T(8,128)(2,1)S(1)}, u32[]{:S(2)}, u32[]{:S(2)}) async-start(bf16[8,96,256]{2,1,0:T(8,128)(2,1)} %broadcast_in_dim.39), calls=%async_computation.2 | async-start | bytes 786432 | tf_op jit(solution)/shard_map/all_to_all | solution.py:45
  87.4 2.6 collective-permute-start.3
  90.0 2.4 collective-permute-start.6
  92.3 1.3 collective-permute-start.11
  93.6 1.4 collective-permute-start.12
  95.1 1.1 collective-permute-start.4
  96.2 4.3 %all-to-all-done.2 = bf16[8,96,256]{2,1,0:T(8,128)(2,1)S(1)} async-done(((bf16[8,96,256]{2,1,0:T(8,128)(2,1)}), bf16[8,96,256]{2,1,0:T(8,128)(2,1)S(1)}, u32[]{:S(2)}, u32[]{:S(2)}) %all-to-all-start.2) | async-done | bytes 393248 | tf_op jit(solution)/shard_map/all_to_all | solution.py:45
  100.5 10.0 %all-to-all-start.3 = ((bf16[32,32,384]{2,1,0:T(8,128)(2,1)}), bf16[32,32,384]{2,1,0:T(8,128)(2,1)}, u32[]{:S(2)}, u32[]{:S(2)}) async-start(bf16[32,32,384]{2,1,0:T(8,128)(2,1)} %bitcast.10), calls=%async_computation.3 | async-start | bytes 1572864 | tf_op jit(solution)/shard_map/all_to_all | solution.py:286
  110.5 2.8 collective-permute-start.25
  113.3 0.6 collective-permute-start.7
  114.0 15.7 %collective-permute-done.25 = bf16[768,256]{1,0:T(8,128)(2,1)S(1)} collective-permute-done((bf16[768,256]{1,0:T(8,128)(2,1)S(1)}, bf16[768,256]{1,0:T(8,128)(2,1)S(1)}, u32[]{:S(2)}, u32[]{:S(2)}) %collective-permute-start.25) | collective-permute-done | bytes 393248 | tf_op jit(solution)/shard_map/ppermute | solution.py:53
  129.7 3.3 %collective-permute-start.5 = (bf16[64,3072]{1,0:T(8,128)(2,1)S(1)}, bf16[64,3072]{1,0:T(8,128)(2,1)}, u32[]{:S(2)}, u32[]{:S(2)}) collective-permute-start(bf16[64,3072]{1,0:T(8,128)(2,1)S(1)} %slice.85), channel_id=1, source_target_pairs={{0,48},{16,0},{32,16},{48,32},{1,49},{17,1},{33,17},{49,33},{2,50}... | collective-permute-start | bytes 1179656 | tf_op jit(solution)/shard_map/ppermute | solution.py:53
  133.0 1.4 collective-permute-start.8
  134.5 2.7 collective-permute-start.27
  137.2 1.9 slice.86
  139.1 1.9 slice.87
  141.0 0.6 collective-permute-start.13
  141.6 2.4 collective-permute-start.14
  144.0 1.7 collective-permute-start.9
  145.7 0.6 collective-permute-start.10
  146.4 0.6 fusion.20
  156.7 0.6 gather_fusion
  157.3 0.6 gather_fusion.1
  162.8 1.1 pad_maximum_fusion.3
  163.8 2.6 pad_maximum_fusion
  166.5 1.0 copy-done.3
  167.5 12.4 %shard_map.155.refs_0_ = bf16[2,4,128,256]{3,2,1,0:T(8,128)(2,1)S(1)} custom-call(s32[1]{0:T(128)} %bitcast.12.ints_ref, bf16[128,3072]{1,0:T(8,128)(2,1)S(1)} %bitcast.66, bf16[128,3072]{1,0:T(8,128)(2,1)S(1)} %collective-permute-done.2.refs_1_, bf16[128,3072]{1,0:T(8,128)(2,1)S(1)} %collective-permute-done.3.refs_2_, bf16[64,3072]{1,0:T(8,128)(2,1)S(1)} %copy-done.3, ...), custom_call_target="tpu_custom_call" | custom-call | tf_op jit(solution)/shard_map/pallas_call | solution.py:182
  180.1 1.1 dynamic-slice_bitcast_fusion.1
  181.3 0.9 collective-permute-start.28
  182.2 3.1 %collective-permute-start.16 = (bf16[2,4,128,256]{3,2,1,0:T(8,128)(2,1)S(1)}, bf16[2,4,128,256]{3,2,1,0:T(8,128)(2,1)S(1)}, u32[]{:S(2)}, u32[]{:S(2)}) collective-permute-start(bf16[2,4,128,256]{3,2,1,0:T(8,128)(2,1)S(1)} %shard_map.155.refs_0_), channel_id=1, source_target_pairs={{0,48},{16,0},{32,16},{48,32},{1,49},{17,1},{33,17},{49,33},{2,50}... | collective-permute-start | bytes 1572872 | tf_op jit(solution)/shard_map/ppermute | solution.py:53
  185.3 1.1 dynamic-slice_bitcast_fusion.4
  186.4 0.7 collective-permute-start.19
  187.1 8.1 %collective-permute-done.15.refs_1_ = bf16[2,4,128,256]{3,2,1,0:T(8,128)(2,1)S(1)} collective-permute-done((bf16[2,4,128,256]{3,2,1,0:T(8,128)(2,1)S(1)}, bf16[2,4,128,256]{3,2,1,0:T(8,128)(2,1)S(1)}, u32[]{:S(2)}, u32[]{:S(2)}) %collective-permute-start.15) | collective-permute-done | bytes 524320 | tf_op jit(solution)/shard_map/ppermute | solution.py:53
  195.3 1.3 collective-permute-done.16.refs_2_
  196.6 3.5 %collective-permute-start.18 = (bf16[4,128,256]{2,1,0:T(8,128)(2,1)S(1)}, bf16[4,128,256]{2,1,0:T(8,128)(2,1)S(1)}, u32[]{:S(2)}, u32[]{:S(2)}) collective-permute-start(bf16[4,128,256]{2,1,0:T(8,128)(2,1)S(1)} %slice_bitcast_fusion), channel_id=1, source_target_pairs={{0,48},{16,0},{32,16},{48,32},{1,49},{17,1},{33,17},{49,33},{2,50}... | collective-permute-start | bytes 786440 | tf_op jit(solution)/shard_map/ppermute | solution.py:53
  200.1 1.1 collective-permute-start.20
  201.4 1.8 collective-permute-done.17.refs_3_
  203.2 2.0 collective-permute-start.22
  205.2 1.4 collective-permute-start.23
  206.8 1.2 pad_maximum_fusion.1
  208.0 5.7 %shard_map.156 = bf16[8,4,2,16,384]{4,3,2,1,0:T(8,128)(2,1)} custom-call(s32[2]{0:T(128)S(1)} %pad_add_fusion.ints_ref, f32[8]{0:T(128)S(1)} %pad_maximum_fusion.4.floats_ref, bf16[2,4,128,256]{3,2,1,0:T(8,128)(2,1)S(1)} %shard_map.155.refs_0_, bf16[2,4,128,256]{3,2,1,0:T(8,128)(2,1)S(1)} %collective-permute-done.15.refs_1_, ...), custom_call_target="tpu_custom_call" | custom-call | tf_op jit(solution)/shard_map/pallas_call | solution.py:316
  213.8 9.0 %all-to-all-start.4 = ((bf16[64,16,384]{2,1,0:T(8,128)(2,1)}), bf16[64,16,384]{2,1,0:T(8,128)(2,1)S(1)}, u32[]{:S(2)}, u32[]{:S(2)}) async-start(bf16[64,16,384]{2,1,0:T(8,128)(2,1)} %bitcast.44), calls=%async_computation.4 | async-start | bytes 1572864 | tf_op jit(solution)/shard_map/all_to_all | solution.py:332
  223.1 0.4 and_convert_fusion.lower_ref
  223.6 21.4 %all-to-all-done.4 = bf16[64,16,384]{2,1,0:T(8,128)(2,1)S(1)} async-done(((bf16[64,16,384]{2,1,0:T(8,128)(2,1)}), bf16[64,16,384]{2,1,0:T(8,128)(2,1)S(1)}, u32[]{:S(2)}, u32[]{:S(2)}) %all-to-all-start.4) | async-done | bytes 786464 | tf_op jit(solution)/shard_map/all_to_all | solution.py:332
  244.9 1.6 shard_map.157
  246.5 8.9 %all-to-all-start.5 = ((bf16[32,16,768]{2,1,0:T(8,128)(2,1)}), bf16[32,16,768]{2,1,0:T(8,128)(2,1)S(1)}, u32[]{:S(2)}, u32[]{:S(2)}) async-start(bf16[32,16,768]{2,1,0:T(8,128)(2,1)} %shard_map.157), calls=%async_computation.5 | async-start | bytes 1572864 | tf_op jit(solution)/shard_map/all_to_all | solution.py:339
  255.5 27.8 %all-to-all-done.5 = bf16[32,16,768]{2,1,0:T(8,128)(2,1)S(1)} async-done(((bf16[32,16,768]{2,1,0:T(8,128)(2,1)}), bf16[32,16,768]{2,1,0:T(8,128)(2,1)S(1)}, u32[]{:S(2)}, u32[]{:S(2)}) %all-to-all-start.5) | async-done | bytes 786464 | tf_op jit(solution)/shard_map/all_to_all | solution.py:339
  283.2 2.7 shard_map.158
  (103 shorter events, 1.5 us)
Async XLA Ops:
  14.6 1.4 copy-start
  16.0 7.9 %copy-start.24 = (bf16[96,768]{1,0:T(8,128)(2,1)S(1)}, bf16[96,768]{1,0:T(8,128)(2,1)}, u32[]{:S(2)}) copy-start(bf16[96,768]{1,0:T(8,128)(2,1)} %param.20) | copy-start | bytes 442372
  18.5 22.7 %all-to-all-start = ((bf16[4,32,3072]{2,1,0:T(8,128)(2,1)}), bf16[4,32,3072]{2,1,0:T(8,128)(2,1)S(1)}, u32[]{:S(2)}, u32[]{:S(2)}) async-start(bf16[4,32,3072]{2,1,0:T(8,128)(2,1)} %get-tuple-element.12), calls=%async_computation | async-start | bytes 1572864 | tf_op jit(solution)/shard_map/all_to_all | solution.py:277
  23.9 33.9 %copy-start.25 = (bf16[256,96]{0,1:T(8,128)(2,1)S(1)}, bf16[256,96]{0,1:T(8,128)(2,1)}, u32[]{:S(2)}) copy-start(bf16[256,96]{0,1:T(8,128)(2,1)} %param.21) | copy-start | bytes 147460
  23.9 17.2 %collective-permute-start.1 = (bf16[96,768]{1,0:T(8,128)(2,1)S(1)}, bf16[96,768]{1,0:T(8,128)(2,1)S(1)}, u32[]{:S(2)}, u32[]{:S(2)}) collective-permute-start(bf16[96,768]{1,0:T(8,128)(2,1)S(1)} %copy-done.24), channel_id=1, source_target_pairs={{0,0},{1,1},{2,16},{3,17},{4,32},{5,33},{6,48},{7,49},{8,8},{9,9},... | collective-permute-start | bytes 442376 | tf_op jit(solution)/shard_map/ppermute | solution.py:274
  42.2 40.9 %all-to-all-start.1 = ((bf16[8,96,768]{2,1,0:T(8,128)(2,1)}), bf16[8,96,768]{2,1,0:T(8,128)(2,1)}, u32[]{:S(2)}, u32[]{:S(2)}) async-start(bf16[8,96,768]{2,1,0:T(8,128)(2,1)} %broadcast_in_dim.38), calls=%async_computation.1 | async-start | bytes 2359296 | tf_op jit(solution)/shard_map/all_to_all | solution.py:45
  54.2 40.9 %collective-permute-start.2 = (bf16[128,3072]{1,0:T(8,128)(2,1)S(1)}, bf16[128,3072]{1,0:T(8,128)(2,1)S(1)}, u32[]{:S(2)}, u32[]{:S(2)}) collective-permute-start(bf16[128,3072]{1,0:T(8,128)(2,1)S(1)} %bitcast.63), channel_id=1, source_target_pairs={{0,16},{16,32},{32,48},{48,0},{1,17},{17,33},{33,49},{49,1},{2,18}... | collective-permute-start | bytes 2359304 | tf_op jit(solution)/shard_map/ppermute | solution.py:53
  57.8 0.7 collective-permute-start
  83.9 16.6 %all-to-all-start.2 = ((bf16[8,96,256]{2,1,0:T(8,128)(2,1)}), bf16[8,96,256]{2,1,0:T(8,128)(2,1)S(1)}, u32[]{:S(2)}, u32[]{:S(2)}) async-start(bf16[8,96,256]{2,1,0:T(8,128)(2,1)} %broadcast_in_dim.39), calls=%async_computation.2 | async-start | bytes 786432 | tf_op jit(solution)/shard_map/all_to_all | solution.py:45
  87.4 23.1 %collective-permute-start.3 = (bf16[128,3072]{1,0:T(8,128)(2,1)S(1)}, bf16[128,3072]{1,0:T(8,128)(2,1)S(1)}, u32[]{:S(2)}, u32[]{:S(2)}) collective-permute-start(bf16[128,3072]{1,0:T(8,128)(2,1)S(1)} %bitcast.64), channel_id=1, source_target_pairs={{0,48},{16,0},{32,16},{48,32},{1,49},{17,1},{33,17},{49,33},{2,50}... | collective-permute-start | bytes 2359304 | tf_op jit(solution)/shard_map/ppermute | solution.py:53
  90.0 23.3 %collective-permute-start.6 = (bf16[128,3072]{1,0:T(8,128)(2,1)S(1)}, bf16[128,3072]{1,0:T(8,128)(2,1)}, u32[]{:S(2)}, u32[]{:S(2)}) collective-permute-start(bf16[128,3072]{1,0:T(8,128)(2,1)S(1)} %bitcast.65), channel_id=1, source_target_pairs={{0,1},{1,0},{2,3},{3,2},{4,5},{5,4},{6,7},{7,6},{8,9},{9,8},{10,11... | collective-permute-start | bytes 2359304 | tf_op jit(solution)/shard_map/ppermute | solution.py:49
  92.3 42.1 %collective-permute-start.11 = (bf16[768,768]{1,0:T(8,128)(2,1)}, bf16[768,768]{1,0:T(8,128)(2,1)}, u32[]{:S(2)}, u32[]{:S(2)}) collective-permute-start(bf16[768,768]{1,0:T(8,128)(2,1)} %bitcast.8.refs_10_), channel_id=1, source_target_pairs={{0,64},{64,128},{128,192},{192,0},{1,65},{65,129},{129,193},{193,1... | collective-permute-start | bytes 3538952 | tf_op jit(solution)/shard_map/ppermute | solution.py:53
  93.6 43.5 %collective-permute-start.12 = (bf16[768,768]{1,0:T(8,128)(2,1)}, bf16[768,768]{1,0:T(8,128)(2,1)}, u32[]{:S(2)}, u32[]{:S(2)}) collective-permute-start(bf16[768,768]{1,0:T(8,128)(2,1)} %bitcast.8.refs_10_), channel_id=1, source_target_pairs={{0,192},{64,0},{128,64},{192,128},{1,193},{65,1},{129,65},{193,129... | collective-permute-start | bytes 3538952 | tf_op jit(solution)/shard_map/ppermute | solution.py:53
  95.1 18.8 %collective-permute-start.4 = (bf16[64,3072]{1,0:T(8,128)(2,1)S(1)}, bf16[64,3072]{1,0:T(8,128)(2,1)S(1)}, u32[]{:S(2)}, u32[]{:S(2)}) collective-permute-start(bf16[64,3072]{1,0:T(8,128)(2,1)S(1)} %slice.84), channel_id=1, source_target_pairs={{0,16},{16,32},{32,48},{48,0},{1,17},{17,33},{33,49},{49,1},{2,18}... | collective-permute-start | bytes 1179656 | tf_op jit(solution)/shard_map/ppermute | solution.py:53
  100.5 40.5 %copy-start.10 = (bf16[8,96,256]{2,1,0:T(8,128)(2,1)}, bf16[8,96,256]{2,1,0:T(8,128)(2,1)S(1)}, u32[]{:S(2)}) copy-start(bf16[8,96,256]{2,1,0:T(8,128)(2,1)S(1)} %all-to-all-done.2) | copy-start | bytes 1179652
  100.5 65.9 %all-to-all-start.3 = ((bf16[32,32,384]{2,1,0:T(8,128)(2,1)}), bf16[32,32,384]{2,1,0:T(8,128)(2,1)}, u32[]{:S(2)}, u32[]{:S(2)}) async-start(bf16[32,32,384]{2,1,0:T(8,128)(2,1)} %bitcast.10), calls=%async_computation.3 | async-start | bytes 1572864 | tf_op jit(solution)/shard_map/all_to_all | solution.py:286
  110.5 19.2 %collective-permute-start.25 = (bf16[768,256]{1,0:T(8,128)(2,1)S(1)}, bf16[768,256]{1,0:T(8,128)(2,1)S(1)}, u32[]{:S(2)}, u32[]{:S(2)}) collective-permute-start(bf16[768,256]{1,0:T(8,128)(2,1)S(1)} %bitcast.73), channel_id=1, source_target_pairs={{0,192},{64,0},{128,64},{192,128},{1,193},{65,1},{129,65},{193,129... | collective-permute-start | bytes 1179656 | tf_op jit(solution)/shard_map/ppermute | solution.py:53
  113.3 28.3 %collective-permute-start.7 = (bf16[128,3072]{1,0:T(8,128)(2,1)S(1)}, bf16[128,3072]{1,0:T(8,128)(2,1)S(1)}, u32[]{:S(2)}, u32[]{:S(2)}) collective-permute-start(bf16[128,3072]{1,0:T(8,128)(2,1)S(1)} %collective-permute-done.2.refs_1_), channel_id=1, source_target_pairs={{0,1},{1,0},{2,3},{3,2},{4,5},{5,4},{6,7},{7,6},{8,9},{9,8},{10,11... | collective-permute-start | bytes 2359304 | tf_op jit(solution)/shard_map/ppermute | solution.py:49
  113.9 30.1 %copy-start.2 = (bf16[64,3072]{1,0:T(8,128)(2,1)}, bf16[64,3072]{1,0:T(8,128)(2,1)S(1)}, u32[]{:S(2)}) copy-start(bf16[64,3072]{1,0:T(8,128)(2,1)S(1)} %collective-permute-done.4.refs_3_) | copy-start | bytes 1179652
  113.9 19.1 %collective-permute-start.24 = (bf16[768,256]{1,0:T(8,128)(2,1)S(1)}, bf16[768,256]{1,0:T(8,128)(2,1)S(1)}, u32[]{:S(2)}, u32[]{:S(2)}) collective-permute-start(bf16[768,256]{1,0:T(8,128)(2,1)S(1)} %bitcast.74), channel_id=1, source_target_pairs={{0,64},{64,128},{128,192},{192,0},{1,65},{65,129},{129,193},{193,1... | collective-permute-start | bytes 1179656 | tf_op jit(solution)/shard_map/ppermute | solution.py:53
  114.0 32.5 %copy-start.19 = (s32[4]{0:T(128)S(1)}, s32[4]{0:T(128)}, u32[]{:S(2)}) copy-start(s32[4]{0:T(128)} %constant.98.clone) | copy-start | bytes 52
  114.0 42.7 %copy-start.8 = (s32[33]{0:T(128)S(1)}, s32[33]{0:T(128)}, u32[]{:S(2)}) copy-start(s32[33]{0:T(128)} %param.17) | copy-start | bytes 400
  129.7 4.7 %copy-start.11 = (bf16[768,256]{1,0:T(8,128)(2,1)}, bf16[768,256]{1,0:T(8,128)(2,1)S(1)}, u32[]{:S(2)}) copy-start(bf16[768,256]{1,0:T(8,128)(2,1)S(1)} %collective-permute-done.25) | copy-start | bytes 1179652
  129.7 11.4 %collective-permute-start.5 = (bf16[64,3072]{1,0:T(8,128)(2,1)S(1)}, bf16[64,3072]{1,0:T(8,128)(2,1)}, u32[]{:S(2)}, u32[]{:S(2)}) collective-permute-start(bf16[64,3072]{1,0:T(8,128)(2,1)S(1)} %slice.85), channel_id=1, source_target_pairs={{0,48},{16,0},{32,16},{48,32},{1,49},{17,1},{33,17},{49,33},{2,50}... | collective-permute-start | bytes 1179656 | tf_op jit(solution)/shard_map/ppermute | solution.py:53
  133.0 1.4 copy-start.12
  133.0 33.4 %collective-permute-start.8 = (bf16[128,3072]{1,0:T(8,128)(2,1)S(1)}, bf16[128,3072]{1,0:T(8,128)(2,1)}, u32[]{:S(2)}, u32[]{:S(2)}) collective-permute-start(bf16[128,3072]{1,0:T(8,128)(2,1)S(1)} %collective-permute-done.3.refs_2_), channel_id=1, source_target_pairs={{0,1},{1,0},{2,3},{3,2},{4,5},{5,4},{6,7},{7,6},{8,9},{9,8},{10,11... | collective-permute-start | bytes 2359304 | tf_op jit(solution)/shard_map/ppermute | solution.py:49
  134.5 9.6 %collective-permute-start.27 = (bf16[384,256]{1,0:T(8,128)(2,1)S(1)}, bf16[384,256]{1,0:T(8,128)(2,1)S(1)}, u32[]{:S(2)}, u32[]{:S(2)}) collective-permute-start(bf16[384,256]{1,0:T(8,128)(2,1)S(1)} %slice.91), channel_id=1, source_target_pairs={{0,192},{64,0},{128,64},{192,128},{1,193},{65,1},{129,65},{193,129... | collective-permute-start | bytes 589832 | tf_op jit(solution)/shard_map/ppermute | solution.py:53
  137.2 8.5 %collective-permute-start.26 = (bf16[384,256]{1,0:T(8,128)(2,1)S(1)}, bf16[384,256]{1,0:T(8,128)(2,1)S(1)}, u32[]{:S(2)}, u32[]{:S(2)}) collective-permute-start(bf16[384,256]{1,0:T(8,128)(2,1)S(1)} %slice.90), channel_id=1, source_target_pairs={{0,64},{64,128},{128,192},{192,0},{1,65},{65,129},{129,193},{193,1... | collective-permute-start | bytes 589832 | tf_op jit(solution)/shard_map/ppermute | solution.py:53
  141.0 25.4 %collective-permute-start.13 = (bf16[384,768]{1,0:T(8,128)(2,1)}, bf16[384,768]{1,0:T(8,128)(2,1)S(1)}, u32[]{:S(2)}, u32[]{:S(2)}) collective-permute-start(bf16[384,768]{1,0:T(8,128)(2,1)} %slice.86), channel_id=1, source_target_pairs={{0,64},{64,128},{128,192},{192,0},{1,65},{65,129},{129,193},{193,1... | collective-permute-start | bytes 1769480 | tf_op jit(solution)/shard_map/ppermute | solution.py:53
  141.6 4.1 %copy-start.13 = (bf16[128,3072]{1,0:T(8,128)(2,1)}, bf16[128,3072]{1,0:T(8,128)(2,1)S(1)}, u32[]{:S(2)}) copy-start(bf16[128,3072]{1,0:T(8,128)(2,1)S(1)} %collective-permute-done.7.refs_6_) | copy-start | bytes 2359300
  141.6 24.8 %collective-permute-start.14 = (bf16[384,768]{1,0:T(8,128)(2,1)}, bf16[384,768]{1,0:T(8,128)(2,1)}, u32[]{:S(2)}, u32[]{:S(2)}) collective-permute-start(bf16[384,768]{1,0:T(8,128)(2,1)} %slice.87), channel_id=1, source_target_pairs={{0,192},{64,0},{128,64},{192,128},{1,193},{65,1},{129,65},{193,129... | collective-permute-start | bytes 1769480 | tf_op jit(solution)/shard_map/ppermute | solution.py:53
  144.0 1.7 copy-start.16
  144.0 22.4 %collective-permute-start.9 = (bf16[64,3072]{1,0:T(8,128)(2,1)S(1)}, bf16[64,3072]{1,0:T(8,128)(2,1)}, u32[]{:S(2)}, u32[]{:S(2)}) collective-permute-start(bf16[64,3072]{1,0:T(8,128)(2,1)S(1)} %collective-permute-done.4.refs_3_), channel_id=1, source_target_pairs={{0,1},{1,0},{2,3},{3,2},{4,5},{5,4},{6,7},{7,6},{8,9},{9,8},{10,11... | collective-permute-start | bytes 1179656 | tf_op jit(solution)/shard_map/ppermute | solution.py:49
  145.7 0.7 copy-start.17
  145.7 20.7 %collective-permute-start.10 = (bf16[64,3072]{1,0:T(8,128)(2,1)}, bf16[64,3072]{1,0:T(8,128)(2,1)}, u32[]{:S(2)}, u32[]{:S(2)}) collective-permute-start(bf16[64,3072]{1,0:T(8,128)(2,1)} %collective-permute-done.5.refs_4_), channel_id=1, source_target_pairs={{0,1},{1,0},{2,3},{3,2},{4,5},{5,4},{6,7},{7,6},{8,9},{9,8},{10,11... | collective-permute-start | bytes 1179656 | tf_op jit(solution)/shard_map/ppermute | solution.py:49
  163.8 2.6 copy-start.6
  163.8 2.6 copy-start.7
  166.5 1.0 copy-start.3
  167.5 12.6 %copy-start.9 = (bf16[4,4,2,96,256]{4,3,2,1,0:T(8,128)(2,1)S(1)}, bf16[4,4,2,96,256]{4,3,2,1,0:T(8,128)(2,1)}, u32[]{:S(2)}) copy-start(bf16[4,4,2,96,256]{4,3,2,1,0:T(8,128)(2,1)} %pad_maximum_fusion) | copy-start | bytes 4718596
  179.8 15.4 %collective-permute-start.15 = (bf16[2,4,128,256]{3,2,1,0:T(8,128)(2,1)S(1)}, bf16[2,4,128,256]{3,2,1,0:T(8,128)(2,1)S(1)}, u32[]{:S(2)}, u32[]{:S(2)}) collective-permute-start(bf16[2,4,128,256]{3,2,1,0:T(8,128)(2,1)S(1)} %shard_map.155.refs_0_), channel_id=1, source_target_pairs={{0,16},{16,32},{32,48},{48,0},{1,17},{17,33},{33,49},{49,1},{2,18}... | collective-permute-start | bytes 1572872 | tf_op jit(solution)/shard_map/ppermute | solution.py:53
  181.3 26.8 %copy-start.5 = (bf16[128,128]{1,0:T(8,128)(2,1)S(1)}, bf16[128,128]{1,0:T(8,128)(2,1)}, u32[]{:S(2)}) copy-start(bf16[128,128]{1,0:T(8,128)(2,1)} %constant.99.clone.refs_14_) | copy-start | bytes 98308
  181.3 20.0 %collective-permute-start.28 = (bf16[4,384,256]{2,1,0:T(8,128)(2,1)S(1)}, bf16[4,384,256]{2,1,0:T(8,128)(2,1)S(1)}, u32[]{:S(2)}, u32[]{:S(2)}) collective-permute-start(bf16[4,384,256]{2,1,0:T(8,128)(2,1)S(1)} %bitcast.79), channel_id=1, source_target_pairs={{0,1},{1,0},{2,3},{3,2},{4,5},{5,4},{6,7},{7,6},{8,9},{9,8},{10,11... | collective-permute-start | bytes 2359304 | tf_op jit(solution)/shard_map/ppermute | solution.py:49
  182.2 14.4 %collective-permute-start.16 = (bf16[2,4,128,256]{3,2,1,0:T(8,128)(2,1)S(1)}, bf16[2,4,128,256]{3,2,1,0:T(8,128)(2,1)S(1)}, u32[]{:S(2)}, u32[]{:S(2)}) collective-permute-start(bf16[2,4,128,256]{3,2,1,0:T(8,128)(2,1)S(1)} %shard_map.155.refs_0_), channel_id=1, source_target_pairs={{0,48},{16,0},{32,16},{48,32},{1,49},{17,1},{33,17},{49,33},{2,50}... | collective-permute-start | bytes 1572872 | tf_op jit(solution)/shard_map/ppermute | solution.py:53
  186.4 21.6 %collective-permute-start.19 = (bf16[2,4,128,256]{3,2,1,0:T(8,128)(2,1)S(1)}, bf16[2,4,128,256]{3,2,1,0:T(8,128)(2,1)S(1)}, u32[]{:S(2)}, u32[]{:S(2)}) collective-permute-start(bf16[2,4,128,256]{3,2,1,0:T(8,128)(2,1)S(1)} %shard_map.155.refs_0_), channel_id=1, source_target_pairs={{0,1},{1,0},{2,3},{3,2},{4,5},{5,4},{6,7},{7,6},{8,9},{9,8},{10,11... | collective-permute-start | bytes 1572872 | tf_op jit(solution)/shard_map/ppermute | solution.py:49
  195.2 8.0 %collective-permute-start.17 = (bf16[4,128,256]{2,1,0:T(8,128)(2,1)S(1)}, bf16[4,128,256]{2,1,0:T(8,128)(2,1)S(1)}, u32[]{:S(2)}, u32[]{:S(2)}) collective-permute-start(bf16[4,128,256]{2,1,0:T(8,128)(2,1)S(1)} %slice_bitcast_fusion.1), channel_id=1, source_target_pairs={{0,16},{16,32},{32,48},{48,0},{1,17},{17,33},{33,49},{49,1},{2,18}... | collective-permute-start | bytes 786440 | tf_op jit(solution)/shard_map/ppermute | solution.py:53
  196.6 8.6 %collective-permute-start.18 = (bf16[4,128,256]{2,1,0:T(8,128)(2,1)S(1)}, bf16[4,128,256]{2,1,0:T(8,128)(2,1)S(1)}, u32[]{:S(2)}, u32[]{:S(2)}) collective-permute-start(bf16[4,128,256]{2,1,0:T(8,128)(2,1)S(1)} %slice_bitcast_fusion), channel_id=1, source_target_pairs={{0,48},{16,0},{32,16},{48,32},{1,49},{17,1},{33,17},{49,33},{2,50}... | collective-permute-start | bytes 786440 | tf_op jit(solution)/shard_map/ppermute | solution.py:53
  200.1 7.9 %collective-permute-start.20 = (bf16[2,4,128,256]{3,2,1,0:T(8,128)(2,1)S(1)}, bf16[2,4,128,256]{3,2,1,0:T(8,128)(2,1)}, u32[]{:S(2)}, u32[]{:S(2)}) collective-permute-start(bf16[2,4,128,256]{3,2,1,0:T(8,128)(2,1)S(1)} %collective-permute-done.15.refs_1_), channel_id=1, source_target_pairs={{0,1},{1,0},{2,3},{3,2},{4,5},{5,4},{6,7},{7,6},{8,9},{9,8},{10,11... | collective-permute-start | bytes 1572872 | tf_op jit(solution)/shard_map/ppermute | solution.py:49
  201.2 5.4 %copy-start.14 = (bf16[4,384,256]{2,1,0:T(8,128)(2,1)}, bf16[4,384,256]{2,1,0:T(8,128)(2,1)S(1)}, u32[]{:S(2)}) copy-start(bf16[4,384,256]{2,1,0:T(8,128)(2,1)S(1)} %collective-permute-done.28.refs_11_) | copy-start | bytes 2359300
  201.3 6.7 %collective-permute-start.21 = (bf16[2,4,128,256]{3,2,1,0:T(8,128)(2,1)S(1)}, bf16[2,4,128,256]{3,2,1,0:T(8,128)(2,1)}, u32[]{:S(2)}, u32[]{:S(2)}) collective-permute-start(bf16[2,4,128,256]{3,2,1,0:T(8,128)(2,1)S(1)} %collective-permute-done.16.refs_2_), channel_id=1, source_target_pairs={{0,1},{1,0},{2,3},{3,2},{4,5},{5,4},{6,7},{7,6},{8,9},{9,8},{10,11... | collective-permute-start | bytes 1572872 | tf_op jit(solution)/shard_map/ppermute | solution.py:49
  203.2 4.8 %collective-permute-start.22 = (bf16[4,128,256]{2,1,0:T(8,128)(2,1)S(1)}, bf16[4,128,256]{2,1,0:T(8,128)(2,1)}, u32[]{:S(2)}, u32[]{:S(2)}) collective-permute-start(bf16[4,128,256]{2,1,0:T(8,128)(2,1)S(1)} %collective-permute-done.17.refs_3_), channel_id=1, source_target_pairs={{0,1},{1,0},{2,3},{3,2},{4,5},{5,4},{6,7},{7,6},{8,9},{9,8},{10,11... | collective-permute-start | bytes 786440 | tf_op jit(solution)/shard_map/ppermute | solution.py:49
  205.2 2.8 collective-permute-start.23
  213.8 9.0 %copy-start.23 = (s32[4]{0:T(128)S(1)}, s32[4]{0:T(128)}, u32[]{:S(2)}) copy-start(s32[4]{0:T(128)} %param.18) | copy-start | bytes 52
  213.8 9.3 %copy-start.18 = (s32[512]{0:T(512)S(1)}, s32[512]{0:T(512)}, u32[]{:S(2)}) copy-start(s32[512]{0:T(512)} %constant.104.clone) | copy-start | bytes 6148
  213.8 9.3 %copy-start.20 = (s32[512]{0:T(512)S(1)}, s32[512]{0:T(512)}, u32[]{:S(2)}) copy-start(s32[512]{0:T(512)} %constant.103.clone) | copy-start | bytes 6148
  213.8 9.3 %copy-start.21 = (s32[512]{0:T(512)S(1)}, s32[512]{0:T(512)}, u32[]{:S(2)}) copy-start(s32[512]{0:T(512)} %constant.107) | copy-start | bytes 6148
  213.8 9.3 %copy-start.22 = (s32[512]{0:T(512)S(1)}, s32[512]{0:T(512)}, u32[]{:S(2)}) copy-start(s32[512]{0:T(512)} %constant.102.clone) | copy-start | bytes 6148
  213.8 9.3 %copy-start.15 = (pred[512,512]{1,0:T(32,128)(4,1)S(1)}, pred[512,512]{1,0:T(32,128)(4,1)}, u32[]{:S(2)}) copy-start(pred[512,512]{1,0:T(32,128)(4,1)} %constant.105.clone) | copy-start | bytes 786436
  213.8 31.1 %all-to-all-start.4 = ((bf16[64,16,384]{2,1,0:T(8,128)(2,1)}), bf16[64,16,384]{2,1,0:T(8,128)(2,1)S(1)}, u32[]{:S(2)}, u32[]{:S(2)}) async-start(bf16[64,16,384]{2,1,0:T(8,128)(2,1)} %bitcast.44), calls=%async_computation.4 | async-start | bytes 1572864 | tf_op jit(solution)/shard_map/all_to_all | solution.py:332
  244.9 38.3 %copy-start.1 = (f32[1,4,32,3072]{3,2,1,0:T(8,128)S(1)}, f32[1,4,32,3072]{3,2,1,0:T(8,128)}, u32[]{:S(2)}) copy-start(f32[1,4,32,3072]{3,2,1,0:T(8,128)} %cur_ref.1) | copy-start | bytes 4718596
  244.9 38.3 %copy-start.4 = (bf16[128,128]{1,0:T(8,128)(2,1)S(1)}, bf16[128,128]{1,0:T(8,128)(2,1)}, u32[]{:S(2)}) copy-start(bf16[128,128]{1,0:T(8,128)(2,1)} %constant.100.clone.perm_ref) | copy-start | bytes 98308
  246.5 36.7 %all-to-all-start.5 = ((bf16[32,16,768]{2,1,0:T(8,128)(2,1)}), bf16[32,16,768]{2,1,0:T(8,128)(2,1)S(1)}, u32[]{:S(2)}, u32[]{:S(2)}) async-start(bf16[32,16,768]{2,1,0:T(8,128)(2,1)} %shard_map.157), calls=%async_computation.5 | async-start | bytes 1572864 | tf_op jit(solution)/shard_map/all_to_all | solution.py:339

commit v3 on v2

v3 whole, which is shorter than its diff:
```python
import math

import jax
import jax.numpy as jnp
import numpy as np
from jax import lax
from jax.experimental import pallas as pl
from jax.experimental.pallas import tpu as pltpu
from jax.sharding import Mesh, PartitionSpec as P

eps = 1e-06
AXES = ("y", "x", "h", "z", "c")
NY, NX, NH, NZ, NC = 4, 4, 2, 4, 2
D = 3072
SEQS = 4
ROWS = 32
HEAD = 128
COLS = D // (NX * NC)
TS = 4
WIDE = D // NY
TOKENS = NZ * ROWS
AWAY = (0, 3, 1, 2)
BF = jnp.bfloat16
F32 = jnp.float32
VMEM_LIMIT = 48 * 1024 * 1024
SMEM = pl.BlockSpec(memory_space=pltpu.SMEM)
VMEM = pl.BlockSpec(memory_space=pltpu.VMEM)


def flat(y, x, h, z, c):
    return (((y * NX + x) * NH + h) * NZ + z) * NC + c


def every():
    for y in range(NY):
        for x in range(NX):
            for h in range(NH):
                for z in range(NZ):
                    for c in range(NC):
                        yield y, x, h, z, c


TO_HEADS = [(flat(y, x, h, z, c), flat(y, z, h, x, c)) for y, x, h, z, c in every()]
TO_COLUMNS = [
    (flat(y, x, h, z, c), flat((x % 2) * 2 + c, y, h, z, x // 2)) for y, x, h, z, c in every()
]


def spread(v, axes, parts):
    copies = jnp.broadcast_to(v[None], (parts,) + v.shape)
    return lax.all_to_all(copies, axes, 0, 0)


def other_core(v):
    return lax.ppermute(v, "c", [(0, 1), (1, 0)])


def shift(v, axis, size, away):
    return lax.ppermute(v, axis, [(i, (i + away) % size) for i in range(size)])


def ring(v, axis, size, first, second):
    before = shift(v, axis, size, 1)
    after_ = shift(v, axis, size, -1)
    far = (shift(first(before), axis, size, 1), shift(second(after_), axis, size, -1))
    return (v, before, after_) + far


def ring_rows(v, axis, size):
    n = v.shape[0] // 2
    return ring(v, axis, size, lambda b: b[:n], lambda b: b[n:])


def after(v, other):
    return lax.optimization_barrier((v, other))[0]


def call(kernel, out_shape, specs, **rest):
    return pl.pallas_call(
        kernel,
        out_shape=out_shape,
        in_specs=specs,
        compiler_params=pltpu.CompilerParams(vmem_limit_bytes=VMEM_LIMIT),
        **rest,
    )


def dot(a, b):
    return lax.dot_general(a, b, (((1,), (0,)), ((), ())), preferred_element_type=F32)


def dot_t(a, b):
    return lax.dot_general(a, b, (((1,), (1,)), ((), ())), preferred_element_type=F32)


def step_index(y, x, h):
    return (y * NX + x) * NH + h


def my_step():
    return step_index(lax.axis_index("y"), lax.axis_index("x"), lax.axis_index("h"))


def enter_kernel(steps_ref, cur_ref, mod_ref, hidden_ref, state_ref):
    now = steps_ref[my_step()]
    shift_row = mod_ref[0, pl.ds(now, 1), :]
    scale_row = 1.0 + mod_ref[1, pl.ds(now, 1), :]
    for s in range(SEQS):
        values = cur_ref[0, s]
        mean = jnp.mean(values, axis=-1, keepdims=True)
        centered = values - mean
        variance = jnp.mean(centered * centered, axis=-1, keepdims=True)
        normal = centered * lax.rsqrt(variance + eps)
        hidden_ref[s] = (normal * scale_row + shift_row).astype(BF)
        for x in range(NX):
            for c in range(NC):
                at = (x * NC + c) * COLS
                state_ref[x, s, c] = values[:, at : at + COLS].astype(BF)


def lower_kernel(offset_ref, out_ref):
    shape = (512, 512)
    row = lax.broadcasted_iota(jnp.int32, shape, 0)
    col = lax.broadcasted_iota(jnp.int32, shape, 1)
    bits = lambda v, at, n: (v >> at) & ((1 << n) - 1)
    k, s, t = row >> 4, bits(row, 2, 2), bits(row, 0, 2)
    y, h, s2 = col >> 7, bits(col, 6, 1), bits(col, 4, 2)
    x = (bits(col, 2, 2) + lax.axis_index("x")) & (NX - 1)
    j = step_index(y, x, h)
    start = jnp.full(shape, offset_ref[0], jnp.int32)
    for index in range(1, SEQS):
        start = jnp.where(s == index, offset_ref[index], start)
    same = (s == s2) & (t == bits(col, 0, 2))
    late = (k >= start) & (j >= start) & (j <= k)
    alone = (k < start) & (j == k)
    out_ref[...] = jnp.where(same & (late | alone), 1.0, 0.0).astype(BF)


def rms(values, gain):
    scale = lax.rsqrt(jnp.mean(values * values, axis=-1, keepdims=True) + eps)
    return (values * scale * gain).astype(BF)


def fill_tokens(tokens_ref, pieces):
    half = TOKENS // 2
    for side in range(2):
        mine = pieces[5 * side : 5 * side + 5]
        for place in range(3):
            tokens_ref[side * TS + place] = mine[place][...]
        tokens_ref[side * TS + 3, :half] = mine[3][...]
        tokens_ref[side * TS + 3, half:] = mine[4][...]


def product(tokens_ref, weight, start):
    depth = weight.shape[0]
    columns = pl.ds(pl.multiple_of(start, HEAD), depth)
    return dot(tokens_ref[:, :, columns].reshape(2 * TS * TOKENS, depth), weight[...])


def qkv_kernel(*refs):
    weights, (qkv_ref, tokens_ref) = refs[10:13], refs[13:]
    fill_tokens(tokens_ref, refs[:10])
    y = lax.axis_index("y")
    for place, weight in enumerate(weights):
        term = product(tokens_ref, weight, lax.rem(y + AWAY[place], NY) * WIDE)
        if place == 0:
            qkv_ref[...] = term
        else:
            qkv_ref[...] += term


def attend_kernel(*refs):
    weights = refs[10:12]
    partial_ref, qg_ref, kg_ref, att_ref, tokens_ref, qkv_ref = refs[12:]
    fill_tokens(tokens_ref, refs[:10])
    start = lax.rem(lax.axis_index("y") + 2, NY) * WIDE
    qkv_ref[...] = partial_ref[...] + product(tokens_ref, weights[0], start)
    qkv_ref[...] += product(tokens_ref, weights[1], start + WIDE // 2)

    def part(index, column):
        here = slice(column * HEAD, (column + 1) * HEAD)
        first, second = index * TOKENS, (TS + index) * TOKENS
        return jnp.concatenate(
            [qkv_ref[first : first + TOKENS, here], qkv_ref[second : second + TOKENS, here]], 0
        )

    for index in range(TS):
        for head in range(2):
            queries = rms(part(index, 3 * head), qg_ref[...])
            keys = rms(part(index, 3 * head + 1), kg_ref[...])
            values = part(index, 3 * head + 2).astype(BF)
            scores = dot_t(queries, keys) * (1.0 / math.sqrt(HEAD))
            scores = jnp.exp(scores - jnp.max(scores, axis=-1, keepdims=True))
            share = scores / jnp.sum(scores, axis=-1, keepdims=True)
            result = dot(share.astype(BF), values).astype(BF)
            at = head * HEAD
            att_ref[0, index, :, at : at + HEAD] = result[:TOKENS]
            att_ref[1, index, :, at : at + HEAD] = result[TOKENS:]


def project_kernel(steps_ref, offset_ref, mod_ref, *refs):
    att, sib, blocks = refs[0:5], refs[5:10], refs[10:15]
    state_ref, perm_ref, out_ref, weight_ref = refs[15:]
    y, x, h, z, core = (lax.axis_index(a) for a in AXES)
    plans = mod_ref.shape[1]

    for place, block in enumerate(blocks):
        source = lax.rem(y + AWAY[min(place, 3)], NY)
        into = lax.rem(source, 2)
        down = pl.multiple_of((source >> 1) * (COLS // 2), 16)
        zs = {3: (0, 1), 4: (2, 3)}.get(place, range(NZ))
        for at, zz in enumerate(zs):
            rows = COLS // 2
            weight_ref[into, zz, pl.ds(down, rows)] = block[at * rows : (at + 1) * rows]

    def piece(pieces, place, half):
        if place < 3:
            return pieces[place][half].reshape(TS * TOKENS, 2 * HEAD)
        return pieces[3 + half][...].reshape(TS * TOKENS, 2 * HEAD)

    column = pl.multiple_of((x * NC + core) * COLS, HEAD)
    for half in range(2):
        totals = [None] * TS
        for place, away in enumerate(AWAY):
            group = lax.rem(x + away, NX)
            term = dot_t(piece(att, place, half), weight_ref[core, group])
            term += dot_t(piece(sib, place, 1 - half), weight_ref[1 - core, group])
            for j in range(TS):
                at = AWAY.index((j - away) % NX) * TOKENS
                rows = term[at : at + TOKENS]
                totals[j] = rows if totals[j] is None else totals[j] + rows
        token_core = core if half == 0 else 1 - core
        values = []
        for j in range(TS):
            there = lax.rem(x + j, NX)
            k = step_index(y, there, h)
            now = steps_ref[k]
            size = (now - steps_ref[k + 1]).astype(F32) / plans
            first = jnp.where(k == offset_ref[z], 1.0, 0.0)
            gate = mod_ref[2, pl.ds(now, 1), pl.ds(column, COLS)]
            state = state_ref[there, :, token_core].reshape(TOKENS, COLS).astype(F32)
            increment = size * (state + gate * totals[j])
            values.append((increment + first * state).astype(BF).reshape(NZ, ROWS, COLS))
        for zz in range(NZ):
            stacked = jnp.concatenate([v[zz] for v in values], 0)
            moved = dot(perm_ref[...], stacked).astype(BF)
            out_ref[:, zz, token_core] = moved.reshape(NY * NH, TS * 4, COLS)


def prefix_kernel(lower_ref, terms_ref, out_ref):
    for c in range(NC):
        terms = terms_ref[:, c].reshape(NY * NH * SEQS * 16, COLS)
        total = dot(lower_ref[...], terms).astype(BF)
        out_ref[:, :, c * COLS : (c + 1) * COLS] = total.reshape(32, 16, COLS)


def leave_kernel(offset_ref, got_ref, cur_ref, perm_ref, out_ref):
    got = got_ref[:, 0].reshape(NY * NH * 16, 2 * COLS)
    total = dot(perm_ref[...], got).reshape(SEQS, ROWS, 2 * COLS)
    mine = my_step()
    for s in range(SEQS):
        out_ref[0, s] = total[s] + jnp.where(mine < offset_ref[s], cur_ref[0, s], 0.0)


def row_orders():
    out = np.zeros((128, 128), np.float32)
    for part in range(8):
        for a in range(4):
            for t in range(4):
                out[part * 16 + a * 4 + t, a * 32 + part * 4 + t] = 1
    return jnp.asarray(out, BF), jnp.asarray(out.T, BF)


def shape(*dims, kind=BF):
    return jax.ShapeDtypeStruct(dims, kind)


def body(trajectory, timesteps, offset, mod_table, w_qkv, w_out, query_gain, k_gain):
    planes = mod_table.transpose(1, 0, 2)
    wq = lax.ppermute(w_qkv, AXES, TO_HEADS)
    wo = lax.ppermute(w_out.T, AXES, TO_COLUMNS)
    hidden, state = call(
        enter_kernel,
        (shape(SEQS, ROWS, D), shape(NX, SEQS, NC, ROWS, COLS)),
        [SMEM, VMEM, VMEM],
        out_specs=(VMEM, VMEM),
    )(timesteps, trajectory, planes)
    lower = call(lower_kernel, shape(512, 512), [SMEM], out_specs=VMEM)(offset)

    tokens = lax.all_to_all(hidden, "z", 0, 0)
    wq = spread(after(wq, tokens), ("z", "h"), NZ * NH).reshape(WIDE, 6 * HEAD)
    weights = ring_rows(wq, "y", NY)
    tokens = ring_rows(tokens.reshape(TOKENS, D), "x", NX)
    others = tuple(other_core(v) for v in tokens)

    wo = spread(after(wo, wq), ("z", "h"), NZ * NH).reshape(NZ * NH * 96, 2 * HEAD)
    state = lax.all_to_all(
        after(state, (wo, tokens[3], tokens[4])).reshape(NX * SEQS * NC, ROWS, COLS), ("x", "z", "c"), 0, 0
    ).reshape(NX, NZ, NC, ROWS, COLS)
    columns = ring_rows(wo, "y", NY)

    scratch = [pltpu.VMEM((2 * TS, TOKENS, D), BF)]
    partial = call(
        qkv_kernel,
        shape(2 * TS * TOKENS, 6 * HEAD, kind=F32),
        [VMEM] * 13,
        out_specs=VMEM,
        scratch_shapes=scratch,
    )(*tokens, *others, *weights[:3])
    attended = call(
        attend_kernel,
        shape(2, TS, TOKENS, 2 * HEAD),
        [VMEM] * 15,
        out_specs=VMEM,
        scratch_shapes=scratch + [pltpu.VMEM((2 * TS * TOKENS, 6 * HEAD), F32)],
    )(*tokens, *others, *weights[3:], partial, query_gain[None], k_gain[None])

    attended = ring(after(attended, state), "x", NX, lambda b: b[0], lambda b: b[1])
    sibling = tuple(other_core(v) for v in attended)

    outward, back = row_orders()
    terms = call(
        project_kernel,
        shape(NY * NH, NZ, NC, TS * 4, COLS),
        [SMEM, SMEM] + [VMEM] * 18,
        out_specs=VMEM,
        scratch_shapes=[pltpu.VMEM((NC, NZ, COLS, 2 * HEAD), BF)],
    )(timesteps, offset, planes, *attended, *sibling, *columns, state, outward)
    terms = lax.all_to_all(terms.reshape(64, TS * 4, COLS), ("y", "h", "z", "c"), 0, 0)
    sums = call(prefix_kernel, shape(32, 16, 2 * COLS), [VMEM, VMEM], out_specs=VMEM)(
        lower, terms.reshape(32, NC, 16, COLS)
    )
    got = lax.all_to_all(sums, ("y", "x", "h"), 0, 0)
    return call(
        leave_kernel,
        shape(1, SEQS, ROWS, D, kind=F32),
        [
            SMEM,
            pl.BlockSpec((NY, 1, NH, 16, 2 * COLS), lambda i: (0, i, 0, 0, 0)),
            pl.BlockSpec((1, SEQS, ROWS, 2 * COLS), lambda i: (0, 0, 0, i)),
            pl.BlockSpec((128, 128), lambda i: (0, 0)),
        ],
        grid=(NX,),
        out_specs=pl.BlockSpec((1, SEQS, ROWS, 2 * COLS), lambda i: (0, 0, 0, i)),
    )(offset, got.reshape(NY, NX, NH, 16, 2 * COLS), trajectory, back)


def solution(mesh):
    fine = Mesh(mesh.devices.reshape(NY, NX, NH, NZ, NC), AXES)
    steps, places = ("y", "x", "h"), ("z", "c")
    return jax.shard_map(
        body,
        mesh=fine,
        in_specs=(
            P(steps, None, places, None),
            P(),
            P(),
            P(),
            P(steps, places),
            P(places, steps),
            P(),
            P(),
        ),
        out_specs=P(steps, None, places, None),
        check_vma=False,
    )
```

time: 287 us -> 240 us (0.84)
  waiting for transfers between devices: 119 us -> 81.5 us
  blocking collectives: 0 us -> 34.9 us
  between operations: 24.4 us -> 0.3 us
  starting transfers between devices: 94.1 us -> 82.8 us
  other arithmetic: 6.27 us -> 0 us
  local copies, waits for them, and re-layouts: 17.1 us -> 10.9 us
  Pallas kernels: 24.9 us -> 28.6 us
    all_to_all x0 -> x1, blocking collectives: none -> 34.9 us  [body(): got = lax.all_to_all(sums, ('y', 'x', 'h'), 0, 0)]
    all_to_all x2 -> x1, waiting for transfers between devices: 27.8 us -> 0.01 us  [body(): lax.all_to_all(after(state, (wo, tokens[3], tokens[4])).reshape(NX * SEQS...]
    all_to_all x2, waiting for transfers between devices: 28.9 us -> 4.2 us  [spread(): return lax.all_to_all(copies, axes, 0, 0)]
    ppermute x2, waiting for transfers between devices: 14.2 us -> 29.9 us  [the longest x1 15.6 us: body(): wo = lax.ppermute(w_out.T, AXES, TO_COLUMNS)]
    all_to_all x2 -> x1, starting transfers between devices: 18.9 us -> 9.22 us  [body(): lax.all_to_all(after(state, (wo, tokens[3], tokens[4])).reshape(NX * SEQS...]
    ppermute x2, starting transfers between devices: 3.61 us -> 8.42 us  [the longest x1 5.47 us: body(): wo = lax.ppermute(w_out.T, AXES, TO_COLUMNS)]
    dynamic_slice x4 -> x0, local copies, waits for them, and re-layouts: 4.38 us -> none  [the longest x1 1.52 us: body(): lax.dynamic_index_in_dim(timesteps, index, 0, keepdims=False)]
    ppermute x16, starting transfers between devices: 28.8 us -> 24.5 us  [shift(): return lax.ppermute(v, axis, [(i, (i + away) % size) for i in range(size)])]
  transfers between devices with their start and end apart: 35 -> 33, of which waited for: 9 -> 12; matrix products, arithmetic and copies ran while one was open for 5% -> 1% of each run, Pallas kernels for 0% -> 7%
where the time goes in v3:
time: 240 us; the launch traced here: 239 us
  starting transfers between devices  82.8 us (34%)
  waiting for transfers between devices  81.5 us (34%)
  blocking collectives  34.9 us (15%)
  Pallas kernels  28.6 us (12%)
  local copies, waits for them, and re-layouts  10.9 us (5%)
    all_to_all x1, blocking collectives, body(): got = lax.all_to_all(sums, ('y', 'x', 'h'), 0, 0)  34.9 us
    ppermute x16, starting transfers between devices, shift(): return lax.ppermute(v, axis, [(i, (i + away) % size) for i in range(size)])  24.5 us
    ppermute x16, waiting for transfers between devices, shift(): return lax.ppermute(v, axis, [(i, (i + away) % size) for i in range(size)])  23.7 us
    all_to_all x1, waiting for transfers between devices, body(): lax.all_to_all(terms.reshape(64, TS * 4, COLS), ('y', 'h', 'z', 'c'), 0, 0)  21 us
    all_to_all x2, starting transfers between devices, spread(): return lax.all_to_all(copies, axes, 0, 0)  16 us
    ppermute x1, waiting for transfers between devices, body(): wo = lax.ppermute(w_out.T, AXES, TO_COLUMNS)  15.6 us
    ppermute x1, waiting for transfers between devices, body(): wq = lax.ppermute(w_qkv, AXES, TO_HEADS)  14.2 us
    ppermute x10, starting transfers between devices, other_core(): return lax.ppermute(v, 'c', [(0, 1), (1, 0)])  11.6 us
  transfers between devices with their start and end apart: 33, of which 12 were waited for; matrix products, arithmetic and copies ran while one was open for 1% of the time, Pallas kernels for 7%

profile of v3, /device:TPU:33, one launch (start us, length us, event | category | flops | bytes accessed | tf_op | source)
XLA Modules:
  0.0 238.9 jit_solution(7809009364303105383)
XLA Ops:
  0.0 1.7 copy-done
  1.8 1.4 copy-done.1
  3.2 0.7 copy-done.11
  3.8 2.1 shard_map.101
  5.9 0.9 copy-done.7
  6.8 5.6 %all-to-all-start = ((bf16[4,32,3072]{2,1,0:T(8,128)(2,1)}), bf16[4,32,3072]{2,1,0:T(8,128)(2,1)S(1)}, u32[]{:S(2)}, u32[]{:S(2)}) async-start(bf16[4,32,3072]{2,1,0:T(8,128)(2,1)} %get-tuple-element.11), calls=%async_computation | async-start | bytes 1572864 | tf_op jit(solution)/shard_map/all_to_all | solution.py:290
  12.4 3.0 %collective-permute-start.9 = (bf16[96,768]{1,0:T(8,128)(2,1)S(1)}, bf16[96,768]{1,0:T(8,128)(2,1)S(1)}, u32[]{:S(2)}, u32[]{:S(2)}) collective-permute-start(bf16[96,768]{1,0:T(8,128)(2,1)S(1)} %copy-done.16), channel_id=1, source_target_pairs={{0,0},{1,1},{2,16},{3,17},{4,32},{5,33},{6,48},{7,49},{8,8},{9,9},... | collective-permute-start | bytes 442376 | tf_op jit(solution)/shard_map/ppermute | solution.py:280
  15.4 14.2 %collective-permute-done.9 = bf16[96,768]{1,0:T(8,128)(2,1)S(1)} collective-permute-done((bf16[96,768]{1,0:T(8,128)(2,1)S(1)}, bf16[96,768]{1,0:T(8,128)(2,1)S(1)}, u32[]{:S(2)}, u32[]{:S(2)}) %collective-permute-start.9) | collective-permute-done | bytes 147488 | tf_op jit(solution)/shard_map/ppermute | solution.py:280
  29.6 1.1 broadcast_in_dim.8
  30.7 12.0 %all-to-all-start.1 = ((bf16[8,96,768]{2,1,0:T(8,128)(2,1)}), bf16[8,96,768]{2,1,0:T(8,128)(2,1)}, u32[]{:S(2)}, u32[]{:S(2)}) async-start(bf16[8,96,768]{2,1,0:T(8,128)(2,1)} %broadcast_in_dim.8), calls=%async_computation.1 | async-start | bytes 2359296 | tf_op jit(solution)/shard_map/all_to_all | solution.py:51
  42.7 3.7 %collective-permute-start = (bf16[128,3072]{1,0:T(8,128)(2,1)S(1)}, bf16[128,3072]{1,0:T(8,128)(2,1)S(1)}, u32[]{:S(2)}, u32[]{:S(2)}) collective-permute-start(bf16[128,3072]{1,0:T(8,128)(2,1)S(1)} %bitcast.18), channel_id=1, source_target_pairs={{0,16},{16,32},{32,48},{48,0},{1,17},{17,33},{33,49},{49,1},{2,18}... | collective-permute-start | bytes 2359304 | tf_op jit(solution)/shard_map/ppermute | solution.py:59
  46.4 5.5 %collective-permute-start.14 = (bf16[96,256]{1,0:T(8,128)(2,1)S(1)}, bf16[96,256]{1,0:T(8,128)(2,1)S(1)}, u32[]{:S(2)}, u32[]{:S(2)}) collective-permute-start(bf16[96,256]{1,0:T(8,128)(2,1)S(1)} %bitcast.29), channel_id=1, source_target_pairs={{0,0},{1,64},{2,2},{3,66},{4,4},{5,68},{6,6},{7,70},{8,8},{9,72},{... | collective-permute-start | bytes 147464 | tf_op jit(solution)/shard_map/ppermute | solution.py:281
  51.8 15.6 %collective-permute-done.14 = bf16[96,256]{1,0:T(8,128)(2,1)S(1)} collective-permute-done((bf16[96,256]{1,0:T(8,128)(2,1)S(1)}, bf16[96,256]{1,0:T(8,128)(2,1)S(1)}, u32[]{:S(2)}, u32[]{:S(2)}) %collective-permute-start.14) | collective-permute-done | bytes 49184 | tf_op jit(solution)/shard_map/ppermute | solution.py:281
  67.5 4.2 %all-to-all-done.1 = bf16[8,96,768]{2,1,0:T(8,128)(2,1)} async-done(((bf16[8,96,768]{2,1,0:T(8,128)(2,1)}), bf16[8,96,768]{2,1,0:T(8,128)(2,1)}, u32[]{:S(2)}, u32[]{:S(2)}) %all-to-all-start.1) | async-done | bytes 1179680 | tf_op jit(solution)/shard_map/all_to_all | solution.py:51
  71.7 0.8 broadcast_in_dim.21
  72.4 4.1 %all-to-all-start.2 = ((bf16[8,96,256]{2,1,0:T(8,128)(2,1)}), bf16[8,96,256]{2,1,0:T(8,128)(2,1)}, u32[]{:S(2)}, u32[]{:S(2)}) async-start(bf16[8,96,256]{2,1,0:T(8,128)(2,1)} %broadcast_in_dim.21), calls=%async_computation.2 | async-start | bytes 786432 | tf_op jit(solution)/shard_map/all_to_all | solution.py:51
  76.5 1.4 collective-permute-start.10
  77.9 3.7 %collective-permute-start.2 = (bf16[64,3072]{1,0:T(8,128)(2,1)S(1)}, bf16[64,3072]{1,0:T(8,128)(2,1)S(1)}, u32[]{:S(2)}, u32[]{:S(2)}) collective-permute-start(bf16[64,3072]{1,0:T(8,128)(2,1)S(1)} %slice.32), channel_id=1, source_target_pairs={{0,16},{16,32},{32,48},{48,0},{1,17},{17,33},{33,49},{49,1},{2,18}... | collective-permute-start | bytes 1179656 | tf_op jit(solution)/shard_map/ppermute | solution.py:59
  81.6 0.1 collective-permute-start.3
  81.7 1.5 collective-permute-start.12
  83.3 4.8 %collective-permute-done.2.refs_3_ = bf16[64,3072]{1,0:T(8,128)(2,1)S(1)} collective-permute-done((bf16[64,3072]{1,0:T(8,128)(2,1)S(1)}, bf16[64,3072]{1,0:T(8,128)(2,1)S(1)}, u32[]{:S(2)}, u32[]{:S(2)}) %collective-permute-start.2) | collective-permute-done | bytes 393248 | tf_op jit(solution)/shard_map/ppermute | solution.py:59
  88.0 2.1 collective-permute-done.3.refs_4_
  90.2 9.2 %all-to-all-start.3 = ((bf16[32,32,384]{2,1,0:T(8,128)(2,1)}), bf16[32,32,384]{2,1,0:T(8,128)(2,1)}, u32[]{:S(2)}, u32[]{:S(2)}) async-start(bf16[32,32,384]{2,1,0:T(8,128)(2,1)} %bitcast.25), calls=%async_computation.3 | async-start | bytes 1572864 | tf_op jit(solution)/shard_map/all_to_all | solution.py:297
  99.4 0.4 collective-permute-start.4
  99.9 0.1 collective-permute-start.7
  100.0 0.4 collective-permute-start.5
  100.4 3.6 %collective-permute-done.10.refs_11_ = bf16[768,768]{1,0:T(8,128)(2,1)} collective-permute-done((bf16[768,768]{1,0:T(8,128)(2,1)}, bf16[768,768]{1,0:T(8,128)(2,1)}, u32[]{:S(2)}, u32[]{:S(2)}) %collective-permute-start.10) | collective-permute-done | bytes 1179680 | tf_op jit(solution)/shard_map/ppermute | solution.py:59
  104.0 2.5 %collective-permute-start.6 = (bf16[128,3072]{1,0:T(8,128)(2,1)S(1)}, bf16[128,3072]{1,0:T(8,128)(2,1)S(1)}, u32[]{:S(2)}, u32[]{:S(2)}) collective-permute-start(bf16[128,3072]{1,0:T(8,128)(2,1)S(1)} %collective-permute-done.1.refs_2_), channel_id=1, source_target_pairs={{0,1},{1,0},{2,3},{3,2},{4,5},{5,4},{6,7},{7,6},{8,9},{9,8},{10,11... | collective-permute-start | bytes 2359304 | tf_op jit(solution)/shard_map/ppermute | solution.py:55
  106.5 1.1 slice.34
  107.7 1.0 collective-permute-start.11
  108.6 1.1 slice.35
  109.7 0.0 copy-start.13
  109.7 0.0 copy-start.14
  109.8 1.9 collective-permute-start.13
  111.6 3.3 %collective-permute-start.8 = (bf16[64,3072]{1,0:T(8,128)(2,1)S(1)}, bf16[64,3072]{1,0:T(8,128)(2,1)S(1)}, u32[]{:S(2)}, u32[]{:S(2)}) collective-permute-start(bf16[64,3072]{1,0:T(8,128)(2,1)S(1)} %collective-permute-done.3.refs_4_), channel_id=1, source_target_pairs={{0,1},{1,0},{2,3},{3,2},{4,5},{5,4},{6,7},{7,6},{8,9},{9,8},{10,11... | collective-permute-start | bytes 1179656 | tf_op jit(solution)/shard_map/ppermute | solution.py:55
  115.0 1.3 collective-permute-done.8.refs_9_
  116.4 0.9 copy-done.15
  117.3 8.1 %shard_map.102.refs_12_ = f32[1024,768]{1,0:T(8,128)} custom-call(bf16[128,3072]{1,0:T(8,128)(2,1)S(1)} %bitcast.21, bf16[128,3072]{1,0:T(8,128)(2,1)S(1)} %collective-permute-done.refs_1_, bf16[128,3072]{1,0:T(8,128)(2,1)S(1)} %collective-permute-done.1.refs_2_, bf16[64,3072]{1,0:T(8,128)(2,1)S(1)} %collective-permute-done.2.refs_3_, ...), custom_call_target="tpu_custom_call" | custom-call | tf_op jit(solution)/shard_map/pallas_call | solution.py:303
  125.4 1.0 copy-done.6
  126.4 7.7 %shard_map.103.refs_0_ = bf16[2,4,128,256]{3,2,1,0:T(8,128)(2,1)S(1)} custom-call(bf16[128,3072]{1,0:T(8,128)(2,1)S(1)} %bitcast.22, bf16[128,3072]{1,0:T(8,128)(2,1)S(1)} %collective-permute-done.refs_1_, bf16[128,3072]{1,0:T(8,128)(2,1)S(1)} %collective-permute-done.1.refs_2_, bf16[64,3072]{1,0:T(8,128)(2,1)S(1)} %collective-permute-done.2.refs_3_, ...), custom_call_target="tpu_custom_call" | custom-call | tf_op jit(solution)/shard_map/pallas_call | solution.py:310
  134.2 0.0 copy-start.9
  134.2 1.8 collective-permute-start.15
  136.0 3.4 %collective-permute-start.25 = (bf16[768,256]{1,0:T(8,128)(2,1)}, bf16[768,256]{1,0:T(8,128)(2,1)S(1)}, u32[]{:S(2)}, u32[]{:S(2)}) collective-permute-start(bf16[768,256]{1,0:T(8,128)(2,1)} %bitcast.6.refs_10_), channel_id=1, source_target_pairs={{0,192},{64,0},{128,64},{192,128},{1,193},{65,1},{129,65},{193,129... | collective-permute-start | bytes 1179656 | tf_op jit(solution)/shard_map/ppermute | solution.py:59
  139.4 0.2 collective-permute-start.16
  139.6 7.4 %collective-permute-done.24.refs_11_ = bf16[768,256]{1,0:T(8,128)(2,1)S(1)} collective-permute-done((bf16[768,256]{1,0:T(8,128)(2,1)}, bf16[768,256]{1,0:T(8,128)(2,1)S(1)}, u32[]{:S(2)}, u32[]{:S(2)}) %collective-permute-start.24) | collective-permute-done | bytes 393248 | tf_op jit(solution)/shard_map/ppermute | solution.py:59
  147.1 0.1 collective-permute-start.26
  147.2 2.9 %collective-permute-start.27 = (bf16[384,256]{1,0:T(8,128)(2,1)S(1)}, bf16[384,256]{1,0:T(8,128)(2,1)S(1)}, u32[]{:S(2)}, u32[]{:S(2)}) collective-permute-start(bf16[384,256]{1,0:T(8,128)(2,1)S(1)} %slice.39), channel_id=1, source_target_pairs={{0,192},{64,0},{128,64},{192,128},{1,193},{65,1},{129,65},{193,129... | collective-permute-start | bytes 589832 | tf_op jit(solution)/shard_map/ppermute | solution.py:59
  150.2 3.2 %collective-permute-start.19 = (bf16[2,4,128,256]{3,2,1,0:T(8,128)(2,1)S(1)}, bf16[2,4,128,256]{3,2,1,0:T(8,128)(2,1)S(1)}, u32[]{:S(2)}, u32[]{:S(2)}) collective-permute-start(bf16[2,4,128,256]{3,2,1,0:T(8,128)(2,1)S(1)} %shard_map.103.refs_0_), channel_id=1, source_target_pairs={{0,1},{1,0},{2,3},{3,2},{4,5},{5,4},{6,7},{7,6},{8,9},{9,8},{10,11... | collective-permute-start | bytes 1572872 | tf_op jit(solution)/shard_map/ppermute | solution.py:55
  153.4 1.4 collective-permute-start.17
  154.8 1.4 collective-permute-start.18
  156.2 0.6 collective-permute-start.20
  156.8 0.1 collective-permute-start.21
  156.9 5.7 %collective-permute-done.17.refs_3_ = bf16[4,128,256]{2,1,0:T(8,128)(2,1)S(1)} collective-permute-done((bf16[4,128,256]{2,1,0:T(8,128)(2,1)S(1)}, bf16[4,128,256]{2,1,0:T(8,128)(2,1)S(1)}, u32[]{:S(2)}, u32[]{:S(2)}) %collective-permute-start.17) | collective-permute-done | bytes 262176 | tf_op jit(solution)/shard_map/ppermute | solution.py:59
  162.6 0.8 collective-permute-start.22
  163.4 0.2 collective-permute-start.23
  163.6 0.9 collective-permute-done.22.refs_8_
  164.5 0.4 collective-permute-done.23.refs_9_
  164.9 6.1 %shard_map.104 = bf16[8,4,2,16,384]{4,3,2,1,0:T(8,128)(2,1)} custom-call(s32[33]{0:T(128)S(1)} %copy-done.12, s32[4]{0:T(128)S(1)} %copy-done.10, f32[3,66,3072]{2,1,0:T(8,128)} %bitcast.16, bf16[2,4,128,256]{3,2,1,0:T(8,128)(2,1)S(1)} %shard_map.103.refs_0_, bf16[2,4,128,256]{3,2,1,0:T(8,128)(2,1)S(1)} %collective-permute-done.15.refs_1_, ...), custom_call_target="tpu_custom_call" | custom-call | tf_op jit(solution)/shard_map/pallas_call | solution.py:322
  171.0 7.4 %all-to-all-start.4 = ((bf16[64,16,384]{2,1,0:T(8,128)(2,1)}), bf16[64,16,384]{2,1,0:T(8,128)(2,1)S(1)}, u32[]{:S(2)}, u32[]{:S(2)}) async-start(bf16[64,16,384]{2,1,0:T(8,128)(2,1)} %bitcast.28), calls=%async_computation.4 | async-start | bytes 1572864 | tf_op jit(solution)/shard_map/all_to_all | solution.py:329
  178.4 1.1 shard_map.100.lower_ref
  179.5 21.0 %all-to-all-done.4 = bf16[64,16,384]{2,1,0:T(8,128)(2,1)S(1)} async-done(((bf16[64,16,384]{2,1,0:T(8,128)(2,1)}), bf16[64,16,384]{2,1,0:T(8,128)(2,1)S(1)}, u32[]{:S(2)}, u32[]{:S(2)}) %all-to-all-start.4) | async-done | bytes 786464 | tf_op jit(solution)/shard_map/all_to_all | solution.py:329
  200.6 0.7 shard_map.105
  201.3 34.9 %all_to_all.30 = bf16[32,16,768]{2,1,0:T(8,128)(2,1)S(1)} all-to-all(bf16[32,16,768]{2,1,0:T(8,128)(2,1)S(1)} %shard_map.105), channel_id=1, replica_groups=mesh['y'=4,'x'=4,'h'=2,'z'=4,'c'=2] {'y','x','h'}, dimensions={0} | all-to-all | bytes 1572864 | tf_op jit(solution)/shard_map/all_to_all | solution.py:333
  236.2 2.7 %shard_map.106 = f32[1,4,32,3072]{3,2,1,0:T(8,128)} custom-call(s32[4]{0:T(128)S(1)} %copy-done.10, bf16[4,4,2,16,768]{4,3,2,1,0:T(8,128)(2,1)S(1)} %bitcast.24, f32[1,4,32,3072]{3,2,1,0:T(8,128)S(1)} %copy-done.2, bf16[128,128]{1,0:T(8,128)(2,1)S(1)} %copy-done.8), custom_call_target="tpu_custom_call" | custom-call | tf_op jit(solution)/shard_map/pallas_call | solution.py:334
  (56 shorter events, 0.2 us)
Async XLA Ops:
  0.0 1.7 copy-start
  1.8 1.4 copy-start.1
  3.2 0.7 copy-start.11
  5.9 0.9 copy-start.7
  6.8 5.6 %copy-start.16 = (bf16[96,768]{1,0:T(8,128)(2,1)S(1)}, bf16[96,768]{1,0:T(8,128)(2,1)}, u32[]{:S(2)}) copy-start(bf16[96,768]{1,0:T(8,128)(2,1)} %param.14) | copy-start | bytes 442372
  6.8 22.8 %all-to-all-start = ((bf16[4,32,3072]{2,1,0:T(8,128)(2,1)}), bf16[4,32,3072]{2,1,0:T(8,128)(2,1)S(1)}, u32[]{:S(2)}, u32[]{:S(2)}) async-start(bf16[4,32,3072]{2,1,0:T(8,128)(2,1)} %get-tuple-element.11), calls=%async_computation | async-start | bytes 1572864 | tf_op jit(solution)/shard_map/all_to_all | solution.py:290
  12.4 33.9 %copy-start.17 = (bf16[256,96]{0,1:T(8,128)(2,1)S(1)}, bf16[256,96]{0,1:T(8,128)(2,1)}, u32[]{:S(2)}) copy-start(bf16[256,96]{0,1:T(8,128)(2,1)} %param.15) | copy-start | bytes 147460
  12.4 17.2 %collective-permute-start.9 = (bf16[96,768]{1,0:T(8,128)(2,1)S(1)}, bf16[96,768]{1,0:T(8,128)(2,1)S(1)}, u32[]{:S(2)}, u32[]{:S(2)}) collective-permute-start(bf16[96,768]{1,0:T(8,128)(2,1)S(1)} %copy-done.16), channel_id=1, source_target_pairs={{0,0},{1,1},{2,16},{3,17},{4,32},{5,33},{6,48},{7,49},{8,8},{9,9},... | collective-permute-start | bytes 442376 | tf_op jit(solution)/shard_map/ppermute | solution.py:280
  30.7 40.9 %all-to-all-start.1 = ((bf16[8,96,768]{2,1,0:T(8,128)(2,1)}), bf16[8,96,768]{2,1,0:T(8,128)(2,1)}, u32[]{:S(2)}, u32[]{:S(2)}) async-start(bf16[8,96,768]{2,1,0:T(8,128)(2,1)} %broadcast_in_dim.8), calls=%async_computation.1 | async-start | bytes 2359296 | tf_op jit(solution)/shard_map/all_to_all | solution.py:51
  42.7 35.2 %collective-permute-start = (bf16[128,3072]{1,0:T(8,128)(2,1)S(1)}, bf16[128,3072]{1,0:T(8,128)(2,1)S(1)}, u32[]{:S(2)}, u32[]{:S(2)}) collective-permute-start(bf16[128,3072]{1,0:T(8,128)(2,1)S(1)} %bitcast.18), channel_id=1, source_target_pairs={{0,16},{16,32},{32,48},{48,0},{1,17},{17,33},{33,49},{49,1},{2,18}... | collective-permute-start | bytes 2359304 | tf_op jit(solution)/shard_map/ppermute | solution.py:59
  46.4 35.2 %collective-permute-start.1 = (bf16[128,3072]{1,0:T(8,128)(2,1)S(1)}, bf16[128,3072]{1,0:T(8,128)(2,1)S(1)}, u32[]{:S(2)}, u32[]{:S(2)}) collective-permute-start(bf16[128,3072]{1,0:T(8,128)(2,1)S(1)} %bitcast.19), channel_id=1, source_target_pairs={{0,48},{16,0},{32,16},{48,32},{1,49},{17,1},{33,17},{49,33},{2,50}... | collective-permute-start | bytes 2359304 | tf_op jit(solution)/shard_map/ppermute | solution.py:59
  46.4 21.1 %collective-permute-start.14 = (bf16[96,256]{1,0:T(8,128)(2,1)S(1)}, bf16[96,256]{1,0:T(8,128)(2,1)S(1)}, u32[]{:S(2)}, u32[]{:S(2)}) collective-permute-start(bf16[96,256]{1,0:T(8,128)(2,1)S(1)} %bitcast.29), channel_id=1, source_target_pairs={{0,0},{1,64},{2,2},{3,66},{4,4},{5,68},{6,6},{7,70},{8,8},{9,72},{... | collective-permute-start | bytes 147464 | tf_op jit(solution)/shard_map/ppermute | solution.py:281
  72.4 17.7 %all-to-all-start.2 = ((bf16[8,96,256]{2,1,0:T(8,128)(2,1)}), bf16[8,96,256]{2,1,0:T(8,128)(2,1)}, u32[]{:S(2)}, u32[]{:S(2)}) async-start(bf16[8,96,256]{2,1,0:T(8,128)(2,1)} %broadcast_in_dim.21), calls=%async_computation.2 | async-start | bytes 786432 | tf_op jit(solution)/shard_map/all_to_all | solution.py:51
  76.5 27.5 %collective-permute-start.10 = (bf16[768,768]{1,0:T(8,128)(2,1)}, bf16[768,768]{1,0:T(8,128)(2,1)}, u32[]{:S(2)}, u32[]{:S(2)}) collective-permute-start(bf16[768,768]{1,0:T(8,128)(2,1)} %bitcast.2.refs_10_), channel_id=1, source_target_pairs={{0,64},{64,128},{128,192},{192,0},{1,65},{65,129},{129,193},{193,1... | collective-permute-start | bytes 3538952 | tf_op jit(solution)/shard_map/ppermute | solution.py:59
  77.9 10.1 %collective-permute-start.2 = (bf16[64,3072]{1,0:T(8,128)(2,1)S(1)}, bf16[64,3072]{1,0:T(8,128)(2,1)S(1)}, u32[]{:S(2)}, u32[]{:S(2)}) collective-permute-start(bf16[64,3072]{1,0:T(8,128)(2,1)S(1)} %slice.32), channel_id=1, source_target_pairs={{0,16},{16,32},{32,48},{48,0},{1,17},{17,33},{33,49},{49,1},{2,18}... | collective-permute-start | bytes 1179656 | tf_op jit(solution)/shard_map/ppermute | solution.py:59
  81.6 8.5 %collective-permute-start.3 = (bf16[64,3072]{1,0:T(8,128)(2,1)S(1)}, bf16[64,3072]{1,0:T(8,128)(2,1)S(1)}, u32[]{:S(2)}, u32[]{:S(2)}) collective-permute-start(bf16[64,3072]{1,0:T(8,128)(2,1)S(1)} %slice.33), channel_id=1, source_target_pairs={{0,48},{16,0},{32,16},{48,32},{1,49},{17,1},{33,17},{49,33},{2,50}... | collective-permute-start | bytes 1179656 | tf_op jit(solution)/shard_map/ppermute | solution.py:59
  81.7 25.9 %collective-permute-start.12 = (bf16[768,768]{1,0:T(8,128)(2,1)}, bf16[768,768]{1,0:T(8,128)(2,1)}, u32[]{:S(2)}, u32[]{:S(2)}) collective-permute-start(bf16[768,768]{1,0:T(8,128)(2,1)} %bitcast.2.refs_10_), channel_id=1, source_target_pairs={{0,192},{64,0},{128,64},{192,128},{1,193},{65,1},{129,65},{193,129... | collective-permute-start | bytes 3538952 | tf_op jit(solution)/shard_map/ppermute | solution.py:59
  90.2 26.2 %copy-start.5 = (bf16[64,3072]{1,0:T(8,128)(2,1)}, bf16[64,3072]{1,0:T(8,128)(2,1)S(1)}, u32[]{:S(2)}) copy-start(bf16[64,3072]{1,0:T(8,128)(2,1)S(1)} %collective-permute-done.3.refs_4_) | copy-start | bytes 1179652
  90.2 44.0 %all-to-all-start.3 = ((bf16[32,32,384]{2,1,0:T(8,128)(2,1)}), bf16[32,32,384]{2,1,0:T(8,128)(2,1)}, u32[]{:S(2)}, u32[]{:S(2)}) async-start(bf16[32,32,384]{2,1,0:T(8,128)(2,1)} %bitcast.25), calls=%async_computation.3 | async-start | bytes 1572864 | tf_op jit(solution)/shard_map/all_to_all | solution.py:297
  99.4 10.3 %collective-permute-start.4 = (bf16[128,3072]{1,0:T(8,128)(2,1)S(1)}, bf16[128,3072]{1,0:T(8,128)(2,1)S(1)}, u32[]{:S(2)}, u32[]{:S(2)}) collective-permute-start(bf16[128,3072]{1,0:T(8,128)(2,1)S(1)} %bitcast.20), channel_id=1, source_target_pairs={{0,1},{1,0},{2,3},{3,2},{4,5},{5,4},{6,7},{7,6},{8,9},{9,8},{10,11... | collective-permute-start | bytes 2359304 | tf_op jit(solution)/shard_map/ppermute | solution.py:55
  99.9 11.8 %collective-permute-start.7 = (bf16[64,3072]{1,0:T(8,128)(2,1)S(1)}, bf16[64,3072]{1,0:T(8,128)(2,1)S(1)}, u32[]{:S(2)}, u32[]{:S(2)}) collective-permute-start(bf16[64,3072]{1,0:T(8,128)(2,1)S(1)} %collective-permute-done.2.refs_3_), channel_id=1, source_target_pairs={{0,1},{1,0},{2,3},{3,2},{4,5},{5,4},{6,7},{7,6},{8,9},{9,8},{10,11... | collective-permute-start | bytes 1179656 | tf_op jit(solution)/shard_map/ppermute | solution.py:55
  100.0 16.3 %collective-permute-start.5 = (bf16[128,3072]{1,0:T(8,128)(2,1)S(1)}, bf16[128,3072]{1,0:T(8,128)(2,1)S(1)}, u32[]{:S(2)}, u32[]{:S(2)}) collective-permute-start(bf16[128,3072]{1,0:T(8,128)(2,1)S(1)} %collective-permute-done.refs_1_), channel_id=1, source_target_pairs={{0,1},{1,0},{2,3},{3,2},{4,5},{5,4},{6,7},{7,6},{8,9},{9,8},{10,11... | collective-permute-start | bytes 2359304 | tf_op jit(solution)/shard_map/ppermute | solution.py:55
  104.0 12.3 %collective-permute-start.6 = (bf16[128,3072]{1,0:T(8,128)(2,1)S(1)}, bf16[128,3072]{1,0:T(8,128)(2,1)S(1)}, u32[]{:S(2)}, u32[]{:S(2)}) collective-permute-start(bf16[128,3072]{1,0:T(8,128)(2,1)S(1)} %collective-permute-done.1.refs_2_), channel_id=1, source_target_pairs={{0,1},{1,0},{2,3},{3,2},{4,5},{5,4},{6,7},{7,6},{8,9},{9,8},{10,11... | collective-permute-start | bytes 2359304 | tf_op jit(solution)/shard_map/ppermute | solution.py:55
  107.7 17.7 %collective-permute-start.11 = (bf16[384,768]{1,0:T(8,128)(2,1)S(1)}, bf16[384,768]{1,0:T(8,128)(2,1)S(1)}, u32[]{:S(2)}, u32[]{:S(2)}) collective-permute-start(bf16[384,768]{1,0:T(8,128)(2,1)S(1)} %slice.34), channel_id=1, source_target_pairs={{0,64},{64,128},{128,192},{192,0},{1,65},{65,129},{129,193},{193,1... | collective-permute-start | bytes 1769480 | tf_op jit(solution)/shard_map/ppermute | solution.py:59
  109.7 15.7 %copy-start.13 = (f32[128]{0:T(128)S(1)}, f32[128]{0:T(128)}, u32[]{:S(2)}) copy-start(f32[128]{0:T(128)} %param.16) | copy-start | bytes 1540
  109.7 15.7 %copy-start.14 = (f32[128]{0:T(128)S(1)}, f32[128]{0:T(128)}, u32[]{:S(2)}) copy-start(f32[128]{0:T(128)} %param.17) | copy-start | bytes 1540
  109.8 15.6 %copy-start.3 = (bf16[128,3072]{1,0:T(8,128)(2,1)}, bf16[128,3072]{1,0:T(8,128)(2,1)S(1)}, u32[]{:S(2)}) copy-start(bf16[128,3072]{1,0:T(8,128)(2,1)S(1)} %collective-permute-done.4.refs_5_) | copy-start | bytes 2359300
  109.8 15.6 %collective-permute-start.13 = (bf16[384,768]{1,0:T(8,128)(2,1)S(1)}, bf16[384,768]{1,0:T(8,128)(2,1)S(1)}, u32[]{:S(2)}, u32[]{:S(2)}) collective-permute-start(bf16[384,768]{1,0:T(8,128)(2,1)S(1)} %slice.35), channel_id=1, source_target_pairs={{0,192},{64,0},{128,64},{192,128},{1,193},{65,1},{129,65},{193,129... | collective-permute-start | bytes 1769480 | tf_op jit(solution)/shard_map/ppermute | solution.py:59
  111.6 4.7 %collective-permute-start.8 = (bf16[64,3072]{1,0:T(8,128)(2,1)S(1)}, bf16[64,3072]{1,0:T(8,128)(2,1)S(1)}, u32[]{:S(2)}, u32[]{:S(2)}) collective-permute-start(bf16[64,3072]{1,0:T(8,128)(2,1)S(1)} %collective-permute-done.3.refs_4_), channel_id=1, source_target_pairs={{0,1},{1,0},{2,3},{3,2},{4,5},{5,4},{6,7},{7,6},{8,9},{9,8},{10,11... | collective-permute-start | bytes 1179656 | tf_op jit(solution)/shard_map/ppermute | solution.py:55
  116.3 9.0 %copy-start.4 = (bf16[128,3072]{1,0:T(8,128)(2,1)}, bf16[128,3072]{1,0:T(8,128)(2,1)S(1)}, u32[]{:S(2)}) copy-start(bf16[128,3072]{1,0:T(8,128)(2,1)S(1)} %collective-permute-done.5.refs_6_) | copy-start | bytes 2359300
  116.3 0.9 copy-start.15
  125.4 1.0 copy-start.6
  134.2 30.8 %copy-start.9 = (bf16[128,128]{1,0:T(8,128)(2,1)S(1)}, bf16[128,128]{1,0:T(8,128)(2,1)}, u32[]{:S(2)}) copy-start(bf16[128,128]{1,0:T(8,128)(2,1)} %constant.4.clone.refs_16_) | copy-start | bytes 98308
  134.2 30.8 %copy-start.10 = (s32[4]{0:T(128)S(1)}, s32[4]{0:T(128)}, u32[]{:S(2)}) copy-start(s32[4]{0:T(128)} %offset_ref.5) | copy-start | bytes 52
  134.2 30.8 %copy-start.12 = (s32[33]{0:T(128)S(1)}, s32[33]{0:T(128)}, u32[]{:S(2)}) copy-start(s32[33]{0:T(128)} %steps_ref.3) | copy-start | bytes 400
  134.2 19.1 %collective-permute-start.15 = (bf16[2,4,128,256]{3,2,1,0:T(8,128)(2,1)S(1)}, bf16[2,4,128,256]{3,2,1,0:T(8,128)(2,1)S(1)}, u32[]{:S(2)}, u32[]{:S(2)}) collective-permute-start(bf16[2,4,128,256]{3,2,1,0:T(8,128)(2,1)S(1)} %shard_map.103.refs_0_), channel_id=1, source_target_pairs={{0,16},{16,32},{32,48},{48,0},{1,17},{17,33},{33,49},{49,1},{2,18}... | collective-permute-start | bytes 1572872 | tf_op jit(solution)/shard_map/ppermute | solution.py:59
  136.0 11.1 %collective-permute-start.24 = (bf16[768,256]{1,0:T(8,128)(2,1)}, bf16[768,256]{1,0:T(8,128)(2,1)S(1)}, u32[]{:S(2)}, u32[]{:S(2)}) collective-permute-start(bf16[768,256]{1,0:T(8,128)(2,1)} %bitcast.6.refs_10_), channel_id=1, source_target_pairs={{0,64},{64,128},{128,192},{192,0},{1,65},{65,129},{129,193},{193,1... | collective-permute-start | bytes 1179656 | tf_op jit(solution)/shard_map/ppermute | solution.py:59
  136.0 11.2 %collective-permute-start.25 = (bf16[768,256]{1,0:T(8,128)(2,1)}, bf16[768,256]{1,0:T(8,128)(2,1)S(1)}, u32[]{:S(2)}, u32[]{:S(2)}) collective-permute-start(bf16[768,256]{1,0:T(8,128)(2,1)} %bitcast.6.refs_10_), channel_id=1, source_target_pairs={{0,192},{64,0},{128,64},{192,128},{1,193},{65,1},{129,65},{193,129... | collective-permute-start | bytes 1179656 | tf_op jit(solution)/shard_map/ppermute | solution.py:59
  139.4 15.4 %collective-permute-start.16 = (bf16[2,4,128,256]{3,2,1,0:T(8,128)(2,1)S(1)}, bf16[2,4,128,256]{3,2,1,0:T(8,128)(2,1)S(1)}, u32[]{:S(2)}, u32[]{:S(2)}) collective-permute-start(bf16[2,4,128,256]{3,2,1,0:T(8,128)(2,1)S(1)} %shard_map.103.refs_0_), channel_id=1, source_target_pairs={{0,48},{16,0},{32,16},{48,32},{1,49},{17,1},{33,17},{49,33},{2,50}... | collective-permute-start | bytes 1572872 | tf_op jit(solution)/shard_map/ppermute | solution.py:59
  147.1 9.1 %collective-permute-start.26 = (bf16[384,256]{1,0:T(8,128)(2,1)S(1)}, bf16[384,256]{1,0:T(8,128)(2,1)S(1)}, u32[]{:S(2)}, u32[]{:S(2)}) collective-permute-start(bf16[384,256]{1,0:T(8,128)(2,1)S(1)} %slice.38), channel_id=1, source_target_pairs={{0,64},{64,128},{128,192},{192,0},{1,65},{65,129},{129,193},{193,1... | collective-permute-start | bytes 589832 | tf_op jit(solution)/shard_map/ppermute | solution.py:59
  147.2 9.6 %collective-permute-start.27 = (bf16[384,256]{1,0:T(8,128)(2,1)S(1)}, bf16[384,256]{1,0:T(8,128)(2,1)S(1)}, u32[]{:S(2)}, u32[]{:S(2)}) collective-permute-start(bf16[384,256]{1,0:T(8,128)(2,1)S(1)} %slice.39), channel_id=1, source_target_pairs={{0,192},{64,0},{128,64},{192,128},{1,193},{65,1},{129,65},{193,129... | collective-permute-start | bytes 589832 | tf_op jit(solution)/shard_map/ppermute | solution.py:59
  150.2 13.4 %collective-permute-start.19 = (bf16[2,4,128,256]{3,2,1,0:T(8,128)(2,1)S(1)}, bf16[2,4,128,256]{3,2,1,0:T(8,128)(2,1)S(1)}, u32[]{:S(2)}, u32[]{:S(2)}) collective-permute-start(bf16[2,4,128,256]{3,2,1,0:T(8,128)(2,1)S(1)} %shard_map.103.refs_0_), channel_id=1, source_target_pairs={{0,1},{1,0},{2,3},{3,2},{4,5},{5,4},{6,7},{7,6},{8,9},{9,8},{10,11... | collective-permute-start | bytes 1572872 | tf_op jit(solution)/shard_map/ppermute | solution.py:55
  153.4 9.2 %collective-permute-start.17 = (bf16[4,128,256]{2,1,0:T(8,128)(2,1)S(1)}, bf16[4,128,256]{2,1,0:T(8,128)(2,1)S(1)}, u32[]{:S(2)}, u32[]{:S(2)}) collective-permute-start(bf16[4,128,256]{2,1,0:T(8,128)(2,1)S(1)} %slice_bitcast_fusion.1), channel_id=1, source_target_pairs={{0,16},{16,32},{32,48},{48,0},{1,17},{17,33},{33,49},{49,1},{2,18}... | collective-permute-start | bytes 786440 | tf_op jit(solution)/shard_map/ppermute | solution.py:59
  154.8 8.6 %collective-permute-start.18 = (bf16[4,128,256]{2,1,0:T(8,128)(2,1)S(1)}, bf16[4,128,256]{2,1,0:T(8,128)(2,1)S(1)}, u32[]{:S(2)}, u32[]{:S(2)}) collective-permute-start(bf16[4,128,256]{2,1,0:T(8,128)(2,1)S(1)} %slice_bitcast_fusion), channel_id=1, source_target_pairs={{0,48},{16,0},{32,16},{48,32},{1,49},{17,1},{33,17},{49,33},{2,50}... | collective-permute-start | bytes 786440 | tf_op jit(solution)/shard_map/ppermute | solution.py:59
  156.2 8.7 %collective-permute-start.20 = (bf16[2,4,128,256]{3,2,1,0:T(8,128)(2,1)S(1)}, bf16[2,4,128,256]{3,2,1,0:T(8,128)(2,1)S(1)}, u32[]{:S(2)}, u32[]{:S(2)}) collective-permute-start(bf16[2,4,128,256]{3,2,1,0:T(8,128)(2,1)S(1)} %collective-permute-done.15.refs_1_), channel_id=1, source_target_pairs={{0,1},{1,0},{2,3},{3,2},{4,5},{5,4},{6,7},{7,6},{8,9},{9,8},{10,11... | collective-permute-start | bytes 1572872 | tf_op jit(solution)/shard_map/ppermute | solution.py:55
  156.8 8.1 %collective-permute-start.21 = (bf16[2,4,128,256]{3,2,1,0:T(8,128)(2,1)S(1)}, bf16[2,4,128,256]{3,2,1,0:T(8,128)(2,1)S(1)}, u32[]{:S(2)}, u32[]{:S(2)}) collective-permute-start(bf16[2,4,128,256]{3,2,1,0:T(8,128)(2,1)S(1)} %collective-permute-done.16.refs_2_), channel_id=1, source_target_pairs={{0,1},{1,0},{2,3},{3,2},{4,5},{5,4},{6,7},{7,6},{8,9},{9,8},{10,11... | collective-permute-start | bytes 1572872 | tf_op jit(solution)/shard_map/ppermute | solution.py:55
  162.6 1.9 collective-permute-start.22
  163.4 1.5 collective-permute-start.23
  171.0 29.6 %all-to-all-start.4 = ((bf16[64,16,384]{2,1,0:T(8,128)(2,1)}), bf16[64,16,384]{2,1,0:T(8,128)(2,1)S(1)}, u32[]{:S(2)}, u32[]{:S(2)}) async-start(bf16[64,16,384]{2,1,0:T(8,128)(2,1)} %bitcast.28), calls=%async_computation.4 | async-start | bytes 1572864 | tf_op jit(solution)/shard_map/all_to_all | solution.py:329
  200.6 35.6 %copy-start.2 = (f32[1,4,32,3072]{3,2,1,0:T(8,128)S(1)}, f32[1,4,32,3072]{3,2,1,0:T(8,128)}, u32[]{:S(2)}) copy-start(f32[1,4,32,3072]{3,2,1,0:T(8,128)} %cur_ref.3) | copy-start | bytes 4718596
  200.6 35.6 %copy-start.8 = (bf16[128,128]{1,0:T(8,128)(2,1)S(1)}, bf16[128,128]{1,0:T(8,128)(2,1)}, u32[]{:S(2)}) copy-start(bf16[128,128]{1,0:T(8,128)(2,1)} %constant.5.clone.perm_ref) | copy-start | bytes 98308

commit v4 on v3

--- a/solution.py
+++ b/solution.py
@@ -22,9 +22,9 @@
 AWAY = (0, 3, 1, 2)
 BF = jnp.bfloat16
 F32 = jnp.float32
-VMEM_LIMIT = 48 * 1024 * 1024
 SMEM = pl.BlockSpec(memory_space=pltpu.SMEM)
 VMEM = pl.BlockSpec(memory_space=pltpu.VMEM)
+HBM = pl.BlockSpec(memory_space=pltpu.HBM)
 
 
 def flat(y, x, h, z, c):
@@ -75,12 +75,12 @@
     return lax.optimization_barrier((v, other))[0]
 
 
-def call(kernel, out_shape, specs, **rest):
+def call(kernel, out_shape, specs, mib=48, **rest):
     return pl.pallas_call(
         kernel,
         out_shape=out_shape,
         in_specs=specs,
-        compiler_params=pltpu.CompilerParams(vmem_limit_bytes=VMEM_LIMIT),
+        compiler_params=pltpu.CompilerParams(vmem_limit_bytes=mib * 1024 * 1024),
         **rest,
     )
 
@@ -101,21 +101,30 @@
     return step_index(lax.axis_index("y"), lax.axis_index("x"), lax.axis_index("h"))
 
 
-def enter_kernel(steps_ref, cur_ref, mod_ref, hidden_ref, state_ref):
+def enter_kernel(steps_ref, cur_hbm, mod_hbm, hidden_ref, state_ref, cur_ref, mod_ref, sems):
+    plane = pltpu.make_async_copy(mod_hbm.at[0:2], mod_ref, sems.at[SEQS])
+    loads = [
+        pltpu.make_async_copy(cur_hbm.at[0, s], cur_ref.at[s], sems.at[s]) for s in range(SEQS)
+    ]
+    for copy in loads + [plane]:
+        copy.start()
     now = steps_ref[my_step()]
-    shift_row = mod_ref[0, pl.ds(now, 1), :]
-    scale_row = 1.0 + mod_ref[1, pl.ds(now, 1), :]
     for s in range(SEQS):
-        values = cur_ref[0, s]
+        loads[s].wait()
+        values = cur_ref[s]
         mean = jnp.mean(values, axis=-1, keepdims=True)
         centered = values - mean
         variance = jnp.mean(centered * centered, axis=-1, keepdims=True)
-        normal = centered * lax.rsqrt(variance + eps)
-        hidden_ref[s] = (normal * scale_row + shift_row).astype(BF)
+        cur_ref[s] = centered * lax.rsqrt(variance + eps)
         for x in range(NX):
             for c in range(NC):
                 at = (x * NC + c) * COLS
                 state_ref[x, s, c] = values[:, at : at + COLS].astype(BF)
+    plane.wait()
+    shift_row = mod_ref[0, pl.ds(now, 1), :]
+    scale_row = 1.0 + mod_ref[1, pl.ds(now, 1), :]
+    for s in range(SEQS):
+        hidden_ref[s] = (cur_ref[s] * scale_row + shift_row).astype(BF)
 
 
 def lower_kernel(offset_ref, out_ref):
@@ -282,8 +291,14 @@
     hidden, state = call(
         enter_kernel,
         (shape(SEQS, ROWS, D), shape(NX, SEQS, NC, ROWS, COLS)),
-        [SMEM, VMEM, VMEM],
+        [SMEM, HBM, HBM],
+        mib=58,
         out_specs=(VMEM, VMEM),
+        scratch_shapes=[
+            pltpu.VMEM((SEQS, ROWS, D), F32),
+            pltpu.VMEM((2,) + planes.shape[1:], F32),
+            pltpu.SemaphoreType.DMA((SEQS + 1,)),
+        ],
     )(timesteps, trajectory, planes)
     lower = call(lower_kernel, shape(512, 512), [SMEM], out_specs=VMEM)(offset)
 

time: 240 us -> 237 us (0.988)
  local copies, waits for them, and re-layouts: 10.9 us -> 6.15 us
    unnamed x36 -> x28, local copies, waits for them, and re-layouts: 6.68 us -> 1.96 us
where the time goes in v4:
time: 237 us; the launch traced here: 236 us
  starting transfers between devices  82.8 us (35%)
  waiting for transfers between devices  81.5 us (34%)
  blocking collectives  34.9 us (15%)
  Pallas kernels  30.3 us (13%)
  local copies, waits for them, and re-layouts  6.15 us (3%)
    all_to_all x1, blocking collectives, body(): got = lax.all_to_all(sums, ('y', 'x', 'h'), 0, 0)  34.9 us
    ppermute x16, starting transfers between devices, shift(): return lax.ppermute(v, axis, [(i, (i + away) % size) for i in range(size)])  24.5 us
    ppermute x16, waiting for transfers between devices, shift(): return lax.ppermute(v, axis, [(i, (i + away) % size) for i in range(size)])  23.7 us
    all_to_all x1, waiting for transfers between devices, body(): lax.all_to_all(terms.reshape(64, TS * 4, COLS), ('y', 'h', 'z', 'c'), 0, 0)  21 us
    all_to_all x2, starting transfers between devices, spread(): return lax.all_to_all(copies, axes, 0, 0)  16 us
    ppermute x1, waiting for transfers between devices, body(): wo = lax.ppermute(w_out.T, AXES, TO_COLUMNS)  15.6 us
    ppermute x1, waiting for transfers between devices, body(): wq = lax.ppermute(w_qkv, AXES, TO_HEADS)  14.2 us
    ppermute x10, starting transfers between devices, other_core(): return lax.ppermute(v, 'c', [(0, 1), (1, 0)])  11.7 us
  transfers between devices with their start and end apart: 33, of which 12 were waited for; matrix products, arithmetic and copies ran while one was open for 1% of the time, Pallas kernels for 7%

profile of v4, /device:TPU:33, one launch (start us, length us, event | category | flops | bytes accessed | tf_op | source)
XLA Modules:
  0.0 236.0 jit_solution(3983535970549545146)
XLA Ops:
  0.0 3.8 %shard_map.101 = (bf16[4,32,3072]{2,1,0:T(8,128)(2,1)}, bf16[4,4,2,32,384]{4,3,2,1,0:T(8,128)(2,1)}) custom-call(s32[33]{0:T(128)} %steps_ref.3, f32[1,4,32,3072]{3,2,1,0:T(8,128)} %cur_ref.1, f32[3,66,3072]{2,1,0:T(8,128)} %bitcast.25), custom_call_target="tpu_custom_call" | custom-call | tf_op jit(solution)/shard_map/pallas_call | solution.py:291
  3.9 0.0 copy-start.12
  3.9 5.6 %all-to-all-start = ((bf16[4,32,3072]{2,1,0:T(8,128)(2,1)}), bf16[4,32,3072]{2,1,0:T(8,128)(2,1)S(1)}, u32[]{:S(2)}, u32[]{:S(2)}) async-start(bf16[4,32,3072]{2,1,0:T(8,128)(2,1)} %get-tuple-element.11), calls=%async_computation | async-start | bytes 1572864 | tf_op jit(solution)/shard_map/all_to_all | solution.py:305
  9.5 3.0 %collective-permute-start.9 = (bf16[96,768]{1,0:T(8,128)(2,1)S(1)}, bf16[96,768]{1,0:T(8,128)(2,1)S(1)}, u32[]{:S(2)}, u32[]{:S(2)}) collective-permute-start(bf16[96,768]{1,0:T(8,128)(2,1)S(1)} %copy-done.12), channel_id=1, source_target_pairs={{0,0},{1,1},{2,16},{3,17},{4,32},{5,33},{6,48},{7,49},{8,8},{9,9},... | collective-permute-start | bytes 442376 | tf_op jit(solution)/shard_map/ppermute | solution.py:289
  12.4 14.2 %collective-permute-done.9 = bf16[96,768]{1,0:T(8,128)(2,1)S(1)} collective-permute-done((bf16[96,768]{1,0:T(8,128)(2,1)S(1)}, bf16[96,768]{1,0:T(8,128)(2,1)S(1)}, u32[]{:S(2)}, u32[]{:S(2)}) %collective-permute-start.9) | collective-permute-done | bytes 147488 | tf_op jit(solution)/shard_map/ppermute | solution.py:289
  26.7 1.1 broadcast_in_dim.8
  27.8 12.0 %all-to-all-start.1 = ((bf16[8,96,768]{2,1,0:T(8,128)(2,1)}), bf16[8,96,768]{2,1,0:T(8,128)(2,1)}, u32[]{:S(2)}, u32[]{:S(2)}) async-start(bf16[8,96,768]{2,1,0:T(8,128)(2,1)} %broadcast_in_dim.8), calls=%async_computation.1 | async-start | bytes 2359296 | tf_op jit(solution)/shard_map/all_to_all | solution.py:51
  39.7 3.7 %collective-permute-start = (bf16[128,3072]{1,0:T(8,128)(2,1)S(1)}, bf16[128,3072]{1,0:T(8,128)(2,1)S(1)}, u32[]{:S(2)}, u32[]{:S(2)}) collective-permute-start(bf16[128,3072]{1,0:T(8,128)(2,1)S(1)} %bitcast.16), channel_id=1, source_target_pairs={{0,16},{16,32},{32,48},{48,0},{1,17},{17,33},{33,49},{49,1},{2,18}... | collective-permute-start | bytes 2359304 | tf_op jit(solution)/shard_map/ppermute | solution.py:59
  43.4 5.5 %collective-permute-start.14 = (bf16[96,256]{1,0:T(8,128)(2,1)S(1)}, bf16[96,256]{1,0:T(8,128)(2,1)S(1)}, u32[]{:S(2)}, u32[]{:S(2)}) collective-permute-start(bf16[96,256]{1,0:T(8,128)(2,1)S(1)} %bitcast.29), channel_id=1, source_target_pairs={{0,0},{1,64},{2,2},{3,66},{4,4},{5,68},{6,6},{7,70},{8,8},{9,72},{... | collective-permute-start | bytes 147464 | tf_op jit(solution)/shard_map/ppermute | solution.py:290
  48.9 15.6 %collective-permute-done.14 = bf16[96,256]{1,0:T(8,128)(2,1)S(1)} collective-permute-done((bf16[96,256]{1,0:T(8,128)(2,1)S(1)}, bf16[96,256]{1,0:T(8,128)(2,1)S(1)}, u32[]{:S(2)}, u32[]{:S(2)}) %collective-permute-start.14) | collective-permute-done | bytes 49184 | tf_op jit(solution)/shard_map/ppermute | solution.py:290
  64.5 4.2 %all-to-all-done.1 = bf16[8,96,768]{2,1,0:T(8,128)(2,1)} async-done(((bf16[8,96,768]{2,1,0:T(8,128)(2,1)}), bf16[8,96,768]{2,1,0:T(8,128)(2,1)}, u32[]{:S(2)}, u32[]{:S(2)}) %all-to-all-start.1) | async-done | bytes 1179680 | tf_op jit(solution)/shard_map/all_to_all | solution.py:51
  68.7 0.8 broadcast_in_dim.21
  69.5 4.0 %all-to-all-start.2 = ((bf16[8,96,256]{2,1,0:T(8,128)(2,1)}), bf16[8,96,256]{2,1,0:T(8,128)(2,1)}, u32[]{:S(2)}, u32[]{:S(2)}) async-start(bf16[8,96,256]{2,1,0:T(8,128)(2,1)} %broadcast_in_dim.21), calls=%async_computation.2 | async-start | bytes 786432 | tf_op jit(solution)/shard_map/all_to_all | solution.py:51
  73.5 1.4 collective-permute-start.10
  74.9 3.7 %collective-permute-start.2 = (bf16[64,3072]{1,0:T(8,128)(2,1)S(1)}, bf16[64,3072]{1,0:T(8,128)(2,1)S(1)}, u32[]{:S(2)}, u32[]{:S(2)}) collective-permute-start(bf16[64,3072]{1,0:T(8,128)(2,1)S(1)} %slice.32), channel_id=1, source_target_pairs={{0,16},{16,32},{32,48},{48,0},{1,17},{17,33},{33,49},{49,1},{2,18}... | collective-permute-start | bytes 1179656 | tf_op jit(solution)/shard_map/ppermute | solution.py:59
  78.7 0.1 collective-permute-start.3
  78.8 1.5 collective-permute-start.12
  80.3 4.8 %collective-permute-done.2.refs_3_ = bf16[64,3072]{1,0:T(8,128)(2,1)S(1)} collective-permute-done((bf16[64,3072]{1,0:T(8,128)(2,1)S(1)}, bf16[64,3072]{1,0:T(8,128)(2,1)S(1)}, u32[]{:S(2)}, u32[]{:S(2)}) %collective-permute-start.2) | collective-permute-done | bytes 393248 | tf_op jit(solution)/shard_map/ppermute | solution.py:59
  85.1 2.1 collective-permute-done.3.refs_4_
  87.2 9.2 %all-to-all-start.3 = ((bf16[32,32,384]{2,1,0:T(8,128)(2,1)}), bf16[32,32,384]{2,1,0:T(8,128)(2,1)}, u32[]{:S(2)}, u32[]{:S(2)}) async-start(bf16[32,32,384]{2,1,0:T(8,128)(2,1)} %bitcast.28), calls=%async_computation.3 | async-start | bytes 1572864 | tf_op jit(solution)/shard_map/all_to_all | solution.py:312
  96.4 0.4 collective-permute-start.4
  96.9 0.1 collective-permute-start.7
  97.0 0.4 collective-permute-start.5
  97.4 3.6 %collective-permute-done.10.refs_11_ = bf16[768,768]{1,0:T(8,128)(2,1)} collective-permute-done((bf16[768,768]{1,0:T(8,128)(2,1)}, bf16[768,768]{1,0:T(8,128)(2,1)}, u32[]{:S(2)}, u32[]{:S(2)}) %collective-permute-start.10) | collective-permute-done | bytes 1179680 | tf_op jit(solution)/shard_map/ppermute | solution.py:59
  101.0 2.5 %collective-permute-start.6 = (bf16[128,3072]{1,0:T(8,128)(2,1)S(1)}, bf16[128,3072]{1,0:T(8,128)(2,1)S(1)}, u32[]{:S(2)}, u32[]{:S(2)}) collective-permute-start(bf16[128,3072]{1,0:T(8,128)(2,1)S(1)} %collective-permute-done.1.refs_2_), channel_id=1, source_target_pairs={{0,1},{1,0},{2,3},{3,2},{4,5},{5,4},{6,7},{7,6},{8,9},{9,8},{10,11... | collective-permute-start | bytes 2359304 | tf_op jit(solution)/shard_map/ppermute | solution.py:55
  103.6 1.1 slice.34
  104.7 1.0 collective-permute-start.11
  105.7 1.1 slice.35
  106.8 0.0 copy-start.9
  106.8 0.0 copy-start.10
  106.8 0.0 copy-start.1
  106.8 1.8 collective-permute-start.13
  108.7 3.4 %collective-permute-start.8 = (bf16[64,3072]{1,0:T(8,128)(2,1)S(1)}, bf16[64,3072]{1,0:T(8,128)(2,1)S(1)}, u32[]{:S(2)}, u32[]{:S(2)}) collective-permute-start(bf16[64,3072]{1,0:T(8,128)(2,1)S(1)} %collective-permute-done.3.refs_4_), channel_id=1, source_target_pairs={{0,1},{1,0},{2,3},{3,2},{4,5},{5,4},{6,7},{7,6},{8,9},{9,8},{10,11... | collective-permute-start | bytes 1179656 | tf_op jit(solution)/shard_map/ppermute | solution.py:55
  112.0 1.3 collective-permute-done.8.refs_9_
  113.4 0.9 copy-done.11
  114.3 8.1 %shard_map.102.refs_12_ = f32[1024,768]{1,0:T(8,128)} custom-call(bf16[128,3072]{1,0:T(8,128)(2,1)S(1)} %bitcast.19, bf16[128,3072]{1,0:T(8,128)(2,1)S(1)} %collective-permute-done.refs_1_, bf16[128,3072]{1,0:T(8,128)(2,1)S(1)} %collective-permute-done.1.refs_2_, bf16[64,3072]{1,0:T(8,128)(2,1)S(1)} %collective-permute-done.2.refs_3_, ...), custom_call_target="tpu_custom_call" | custom-call | tf_op jit(solution)/shard_map/pallas_call | solution.py:318
  122.4 1.0 copy-done.4
  123.4 7.7 %shard_map.103.refs_0_ = bf16[2,4,128,256]{3,2,1,0:T(8,128)(2,1)S(1)} custom-call(bf16[128,3072]{1,0:T(8,128)(2,1)S(1)} %bitcast.20, bf16[128,3072]{1,0:T(8,128)(2,1)S(1)} %collective-permute-done.refs_1_, bf16[128,3072]{1,0:T(8,128)(2,1)S(1)} %collective-permute-done.1.refs_2_, bf16[64,3072]{1,0:T(8,128)(2,1)S(1)} %collective-permute-done.2.refs_3_, ...), custom_call_target="tpu_custom_call" | custom-call | tf_op jit(solution)/shard_map/pallas_call | solution.py:325
  131.2 0.0 copy-start.6
  131.2 0.0 copy-start.7
  131.2 0.0 copy-start.8
  131.2 1.8 collective-permute-start.15
  133.0 3.4 %collective-permute-start.25 = (bf16[768,256]{1,0:T(8,128)(2,1)}, bf16[768,256]{1,0:T(8,128)(2,1)S(1)}, u32[]{:S(2)}, u32[]{:S(2)}) collective-permute-start(bf16[768,256]{1,0:T(8,128)(2,1)} %bitcast.6.refs_10_), channel_id=1, source_target_pairs={{0,192},{64,0},{128,64},{192,128},{1,193},{65,1},{129,65},{193,129... | collective-permute-start | bytes 1179656 | tf_op jit(solution)/shard_map/ppermute | solution.py:59
  136.4 0.2 collective-permute-start.16
  136.6 7.5 %collective-permute-done.24.refs_11_ = bf16[768,256]{1,0:T(8,128)(2,1)S(1)} collective-permute-done((bf16[768,256]{1,0:T(8,128)(2,1)}, bf16[768,256]{1,0:T(8,128)(2,1)S(1)}, u32[]{:S(2)}, u32[]{:S(2)}) %collective-permute-start.24) | collective-permute-done | bytes 393248 | tf_op jit(solution)/shard_map/ppermute | solution.py:59
  144.1 0.1 collective-permute-start.26
  144.2 2.9 %collective-permute-start.27 = (bf16[384,256]{1,0:T(8,128)(2,1)S(1)}, bf16[384,256]{1,0:T(8,128)(2,1)S(1)}, u32[]{:S(2)}, u32[]{:S(2)}) collective-permute-start(bf16[384,256]{1,0:T(8,128)(2,1)S(1)} %slice.39), channel_id=1, source_target_pairs={{0,192},{64,0},{128,64},{192,128},{1,193},{65,1},{129,65},{193,129... | collective-permute-start | bytes 589832 | tf_op jit(solution)/shard_map/ppermute | solution.py:59
  147.2 3.2 %collective-permute-start.19 = (bf16[2,4,128,256]{3,2,1,0:T(8,128)(2,1)S(1)}, bf16[2,4,128,256]{3,2,1,0:T(8,128)(2,1)S(1)}, u32[]{:S(2)}, u32[]{:S(2)}) collective-permute-start(bf16[2,4,128,256]{3,2,1,0:T(8,128)(2,1)S(1)} %shard_map.103.refs_0_), channel_id=1, source_target_pairs={{0,1},{1,0},{2,3},{3,2},{4,5},{5,4},{6,7},{7,6},{8,9},{9,8},{10,11... | collective-permute-start | bytes 1572872 | tf_op jit(solution)/shard_map/ppermute | solution.py:55
  150.4 1.4 collective-permute-start.17
  151.8 1.4 collective-permute-start.18
  153.3 0.6 collective-permute-start.20
  153.8 0.1 collective-permute-start.21
  153.9 5.7 %collective-permute-done.17.refs_3_ = bf16[4,128,256]{2,1,0:T(8,128)(2,1)S(1)} collective-permute-done((bf16[4,128,256]{2,1,0:T(8,128)(2,1)S(1)}, bf16[4,128,256]{2,1,0:T(8,128)(2,1)S(1)}, u32[]{:S(2)}, u32[]{:S(2)}) %collective-permute-start.17) | collective-permute-done | bytes 262176 | tf_op jit(solution)/shard_map/ppermute | solution.py:59
  159.6 0.8 collective-permute-start.22
  160.4 0.2 collective-permute-start.23
  160.6 1.0 collective-permute-done.22.refs_8_
  161.6 0.4 collective-permute-done.23.refs_9_
  162.0 6.1 %shard_map.104 = bf16[8,4,2,16,384]{4,3,2,1,0:T(8,128)(2,1)} custom-call(s32[33]{0:T(128)S(1)} %copy-done.8, s32[4]{0:T(128)S(1)} %copy-done.7, f32[3,66,3072]{2,1,0:T(8,128)} %bitcast.26, bf16[2,4,128,256]{3,2,1,0:T(8,128)(2,1)S(1)} %shard_map.103.refs_0_, bf16[2,4,128,256]{3,2,1,0:T(8,128)(2,1)S(1)} %collective-permute-done.15.refs_1_, ...), custom_call_target="tpu_custom_call" | custom-call | tf_op jit(solution)/shard_map/pallas_call | solution.py:337
  168.0 7.4 %all-to-all-start.4 = ((bf16[64,16,384]{2,1,0:T(8,128)(2,1)}), bf16[64,16,384]{2,1,0:T(8,128)(2,1)S(1)}, u32[]{:S(2)}, u32[]{:S(2)}) async-start(bf16[64,16,384]{2,1,0:T(8,128)(2,1)} %bitcast.27), calls=%async_computation.4 | async-start | bytes 1572864 | tf_op jit(solution)/shard_map/all_to_all | solution.py:344
  175.5 1.1 shard_map.100.lower_ref
  176.6 21.0 %all-to-all-done.4 = bf16[64,16,384]{2,1,0:T(8,128)(2,1)S(1)} async-done(((bf16[64,16,384]{2,1,0:T(8,128)(2,1)}), bf16[64,16,384]{2,1,0:T(8,128)(2,1)S(1)}, u32[]{:S(2)}, u32[]{:S(2)}) %all-to-all-start.4) | async-done | bytes 786464 | tf_op jit(solution)/shard_map/all_to_all | solution.py:344
  197.6 0.7 shard_map.105
  198.3 34.9 %all_to_all.30 = bf16[32,16,768]{2,1,0:T(8,128)(2,1)S(1)} all-to-all(bf16[32,16,768]{2,1,0:T(8,128)(2,1)S(1)} %shard_map.105), channel_id=1, replica_groups=mesh['y'=4,'x'=4,'h'=2,'z'=4,'c'=2] {'y','x','h'}, dimensions={0} | all-to-all | bytes 1572864 | tf_op jit(solution)/shard_map/all_to_all | solution.py:348
  233.2 2.7 %shard_map.106 = f32[1,4,32,3072]{3,2,1,0:T(8,128)} custom-call(s32[4]{0:T(128)S(1)} %copy-done.7, bf16[4,4,2,16,768]{4,3,2,1,0:T(8,128)(2,1)S(1)} %bitcast.22, f32[1,4,32,3072]{3,2,1,0:T(8,128)S(1)} %copy-done, bf16[128,128]{1,0:T(8,128)(2,1)S(1)} %copy-done.5), custom_call_target="tpu_custom_call" | custom-call | tf_op jit(solution)/shard_map/pallas_call | solution.py:349
  (48 shorter events, 0.2 us)
Async XLA Ops:
  3.9 5.6 %copy-start.12 = (bf16[96,768]{1,0:T(8,128)(2,1)S(1)}, bf16[96,768]{1,0:T(8,128)(2,1)}, u32[]{:S(2)}) copy-start(bf16[96,768]{1,0:T(8,128)(2,1)} %param.14) | copy-start | bytes 442372
  3.9 22.8 %all-to-all-start = ((bf16[4,32,3072]{2,1,0:T(8,128)(2,1)}), bf16[4,32,3072]{2,1,0:T(8,128)(2,1)S(1)}, u32[]{:S(2)}, u32[]{:S(2)}) async-start(bf16[4,32,3072]{2,1,0:T(8,128)(2,1)} %get-tuple-element.11), calls=%async_computation | async-start | bytes 1572864 | tf_op jit(solution)/shard_map/all_to_all | solution.py:305
  9.5 33.9 %copy-start.13 = (bf16[256,96]{0,1:T(8,128)(2,1)S(1)}, bf16[256,96]{0,1:T(8,128)(2,1)}, u32[]{:S(2)}) copy-start(bf16[256,96]{0,1:T(8,128)(2,1)} %param.15) | copy-start | bytes 147460
  9.5 17.2 %collective-permute-start.9 = (bf16[96,768]{1,0:T(8,128)(2,1)S(1)}, bf16[96,768]{1,0:T(8,128)(2,1)S(1)}, u32[]{:S(2)}, u32[]{:S(2)}) collective-permute-start(bf16[96,768]{1,0:T(8,128)(2,1)S(1)} %copy-done.12), channel_id=1, source_target_pairs={{0,0},{1,1},{2,16},{3,17},{4,32},{5,33},{6,48},{7,49},{8,8},{9,9},... | collective-permute-start | bytes 442376 | tf_op jit(solution)/shard_map/ppermute | solution.py:289
  27.8 40.9 %all-to-all-start.1 = ((bf16[8,96,768]{2,1,0:T(8,128)(2,1)}), bf16[8,96,768]{2,1,0:T(8,128)(2,1)}, u32[]{:S(2)}, u32[]{:S(2)}) async-start(bf16[8,96,768]{2,1,0:T(8,128)(2,1)} %broadcast_in_dim.8), calls=%async_computation.1 | async-start | bytes 2359296 | tf_op jit(solution)/shard_map/all_to_all | solution.py:51
  39.7 35.2 %collective-permute-start = (bf16[128,3072]{1,0:T(8,128)(2,1)S(1)}, bf16[128,3072]{1,0:T(8,128)(2,1)S(1)}, u32[]{:S(2)}, u32[]{:S(2)}) collective-permute-start(bf16[128,3072]{1,0:T(8,128)(2,1)S(1)} %bitcast.16), channel_id=1, source_target_pairs={{0,16},{16,32},{32,48},{48,0},{1,17},{17,33},{33,49},{49,1},{2,18}... | collective-permute-start | bytes 2359304 | tf_op jit(solution)/shard_map/ppermute | solution.py:59
  43.4 35.3 %collective-permute-start.1 = (bf16[128,3072]{1,0:T(8,128)(2,1)S(1)}, bf16[128,3072]{1,0:T(8,128)(2,1)S(1)}, u32[]{:S(2)}, u32[]{:S(2)}) collective-permute-start(bf16[128,3072]{1,0:T(8,128)(2,1)S(1)} %bitcast.17), channel_id=1, source_target_pairs={{0,48},{16,0},{32,16},{48,32},{1,49},{17,1},{33,17},{49,33},{2,50}... | collective-permute-start | bytes 2359304 | tf_op jit(solution)/shard_map/ppermute | solution.py:59
  43.4 21.1 %collective-permute-start.14 = (bf16[96,256]{1,0:T(8,128)(2,1)S(1)}, bf16[96,256]{1,0:T(8,128)(2,1)S(1)}, u32[]{:S(2)}, u32[]{:S(2)}) collective-permute-start(bf16[96,256]{1,0:T(8,128)(2,1)S(1)} %bitcast.29), channel_id=1, source_target_pairs={{0,0},{1,64},{2,2},{3,66},{4,4},{5,68},{6,6},{7,70},{8,8},{9,72},{... | collective-permute-start | bytes 147464 | tf_op jit(solution)/shard_map/ppermute | solution.py:290
  69.5 17.8 %all-to-all-start.2 = ((bf16[8,96,256]{2,1,0:T(8,128)(2,1)}), bf16[8,96,256]{2,1,0:T(8,128)(2,1)}, u32[]{:S(2)}, u32[]{:S(2)}) async-start(bf16[8,96,256]{2,1,0:T(8,128)(2,1)} %broadcast_in_dim.21), calls=%async_computation.2 | async-start | bytes 786432 | tf_op jit(solution)/shard_map/all_to_all | solution.py:51
  73.5 27.5 %collective-permute-start.10 = (bf16[768,768]{1,0:T(8,128)(2,1)}, bf16[768,768]{1,0:T(8,128)(2,1)}, u32[]{:S(2)}, u32[]{:S(2)}) collective-permute-start(bf16[768,768]{1,0:T(8,128)(2,1)} %bitcast.2.refs_10_), channel_id=1, source_target_pairs={{0,64},{64,128},{128,192},{192,0},{1,65},{65,129},{129,193},{193,1... | collective-permute-start | bytes 3538952 | tf_op jit(solution)/shard_map/ppermute | solution.py:59
  74.9 10.2 %collective-permute-start.2 = (bf16[64,3072]{1,0:T(8,128)(2,1)S(1)}, bf16[64,3072]{1,0:T(8,128)(2,1)S(1)}, u32[]{:S(2)}, u32[]{:S(2)}) collective-permute-start(bf16[64,3072]{1,0:T(8,128)(2,1)S(1)} %slice.32), channel_id=1, source_target_pairs={{0,16},{16,32},{32,48},{48,0},{1,17},{17,33},{33,49},{49,1},{2,18}... | collective-permute-start | bytes 1179656 | tf_op jit(solution)/shard_map/ppermute | solution.py:59
  78.7 8.5 %collective-permute-start.3 = (bf16[64,3072]{1,0:T(8,128)(2,1)S(1)}, bf16[64,3072]{1,0:T(8,128)(2,1)S(1)}, u32[]{:S(2)}, u32[]{:S(2)}) collective-permute-start(bf16[64,3072]{1,0:T(8,128)(2,1)S(1)} %slice.33), channel_id=1, source_target_pairs={{0,48},{16,0},{32,16},{48,32},{1,49},{17,1},{33,17},{49,33},{2,50}... | collective-permute-start | bytes 1179656 | tf_op jit(solution)/shard_map/ppermute | solution.py:59
  78.8 25.9 %collective-permute-start.12 = (bf16[768,768]{1,0:T(8,128)(2,1)}, bf16[768,768]{1,0:T(8,128)(2,1)}, u32[]{:S(2)}, u32[]{:S(2)}) collective-permute-start(bf16[768,768]{1,0:T(8,128)(2,1)} %bitcast.2.refs_10_), channel_id=1, source_target_pairs={{0,192},{64,0},{128,64},{192,128},{1,193},{65,1},{129,65},{193,129... | collective-permute-start | bytes 3538952 | tf_op jit(solution)/shard_map/ppermute | solution.py:59
  87.2 26.2 %copy-start.3 = (bf16[64,3072]{1,0:T(8,128)(2,1)}, bf16[64,3072]{1,0:T(8,128)(2,1)S(1)}, u32[]{:S(2)}) copy-start(bf16[64,3072]{1,0:T(8,128)(2,1)S(1)} %collective-permute-done.3.refs_4_) | copy-start | bytes 1179652
  87.2 44.0 %all-to-all-start.3 = ((bf16[32,32,384]{2,1,0:T(8,128)(2,1)}), bf16[32,32,384]{2,1,0:T(8,128)(2,1)}, u32[]{:S(2)}, u32[]{:S(2)}) async-start(bf16[32,32,384]{2,1,0:T(8,128)(2,1)} %bitcast.28), calls=%async_computation.3 | async-start | bytes 1572864 | tf_op jit(solution)/shard_map/all_to_all | solution.py:312
  96.4 10.4 %collective-permute-start.4 = (bf16[128,3072]{1,0:T(8,128)(2,1)S(1)}, bf16[128,3072]{1,0:T(8,128)(2,1)S(1)}, u32[]{:S(2)}, u32[]{:S(2)}) collective-permute-start(bf16[128,3072]{1,0:T(8,128)(2,1)S(1)} %bitcast.18), channel_id=1, source_target_pairs={{0,1},{1,0},{2,3},{3,2},{4,5},{5,4},{6,7},{7,6},{8,9},{9,8},{10,11... | collective-permute-start | bytes 2359304 | tf_op jit(solution)/shard_map/ppermute | solution.py:55
  96.9 11.8 %collective-permute-start.7 = (bf16[64,3072]{1,0:T(8,128)(2,1)S(1)}, bf16[64,3072]{1,0:T(8,128)(2,1)S(1)}, u32[]{:S(2)}, u32[]{:S(2)}) collective-permute-start(bf16[64,3072]{1,0:T(8,128)(2,1)S(1)} %collective-permute-done.2.refs_3_), channel_id=1, source_target_pairs={{0,1},{1,0},{2,3},{3,2},{4,5},{5,4},{6,7},{7,6},{8,9},{9,8},{10,11... | collective-permute-start | bytes 1179656 | tf_op jit(solution)/shard_map/ppermute | solution.py:55
  97.0 16.3 %collective-permute-start.5 = (bf16[128,3072]{1,0:T(8,128)(2,1)S(1)}, bf16[128,3072]{1,0:T(8,128)(2,1)S(1)}, u32[]{:S(2)}, u32[]{:S(2)}) collective-permute-start(bf16[128,3072]{1,0:T(8,128)(2,1)S(1)} %collective-permute-done.refs_1_), channel_id=1, source_target_pairs={{0,1},{1,0},{2,3},{3,2},{4,5},{5,4},{6,7},{7,6},{8,9},{9,8},{10,11... | collective-permute-start | bytes 2359304 | tf_op jit(solution)/shard_map/ppermute | solution.py:55
  101.0 12.4 %collective-permute-start.6 = (bf16[128,3072]{1,0:T(8,128)(2,1)S(1)}, bf16[128,3072]{1,0:T(8,128)(2,1)S(1)}, u32[]{:S(2)}, u32[]{:S(2)}) collective-permute-start(bf16[128,3072]{1,0:T(8,128)(2,1)S(1)} %collective-permute-done.1.refs_2_), channel_id=1, source_target_pairs={{0,1},{1,0},{2,3},{3,2},{4,5},{5,4},{6,7},{7,6},{8,9},{9,8},{10,11... | collective-permute-start | bytes 2359304 | tf_op jit(solution)/shard_map/ppermute | solution.py:55
  104.7 17.7 %collective-permute-start.11 = (bf16[384,768]{1,0:T(8,128)(2,1)S(1)}, bf16[384,768]{1,0:T(8,128)(2,1)S(1)}, u32[]{:S(2)}, u32[]{:S(2)}) collective-permute-start(bf16[384,768]{1,0:T(8,128)(2,1)S(1)} %slice.34), channel_id=1, source_target_pairs={{0,64},{64,128},{128,192},{192,0},{1,65},{65,129},{129,193},{193,1... | collective-permute-start | bytes 1769480 | tf_op jit(solution)/shard_map/ppermute | solution.py:59
  106.8 15.6 %copy-start.9 = (f32[128]{0:T(128)S(1)}, f32[128]{0:T(128)}, u32[]{:S(2)}) copy-start(f32[128]{0:T(128)} %param.16) | copy-start | bytes 1540
  106.8 15.6 %copy-start.10 = (f32[128]{0:T(128)S(1)}, f32[128]{0:T(128)}, u32[]{:S(2)}) copy-start(f32[128]{0:T(128)} %param.17) | copy-start | bytes 1540
  106.8 15.6 %copy-start.1 = (bf16[128,3072]{1,0:T(8,128)(2,1)}, bf16[128,3072]{1,0:T(8,128)(2,1)S(1)}, u32[]{:S(2)}) copy-start(bf16[128,3072]{1,0:T(8,128)(2,1)S(1)} %collective-permute-done.4.refs_5_) | copy-start | bytes 2359300
  106.8 15.6 %collective-permute-start.13 = (bf16[384,768]{1,0:T(8,128)(2,1)S(1)}, bf16[384,768]{1,0:T(8,128)(2,1)S(1)}, u32[]{:S(2)}, u32[]{:S(2)}) collective-permute-start(bf16[384,768]{1,0:T(8,128)(2,1)S(1)} %slice.35), channel_id=1, source_target_pairs={{0,192},{64,0},{128,64},{192,128},{1,193},{65,1},{129,65},{193,129... | collective-permute-start | bytes 1769480 | tf_op jit(solution)/shard_map/ppermute | solution.py:59
  108.7 4.7 %collective-permute-start.8 = (bf16[64,3072]{1,0:T(8,128)(2,1)S(1)}, bf16[64,3072]{1,0:T(8,128)(2,1)S(1)}, u32[]{:S(2)}, u32[]{:S(2)}) collective-permute-start(bf16[64,3072]{1,0:T(8,128)(2,1)S(1)} %collective-permute-done.3.refs_4_), channel_id=1, source_target_pairs={{0,1},{1,0},{2,3},{3,2},{4,5},{5,4},{6,7},{7,6},{8,9},{9,8},{10,11... | collective-permute-start | bytes 1179656 | tf_op jit(solution)/shard_map/ppermute | solution.py:55
  113.4 9.0 %copy-start.2 = (bf16[128,3072]{1,0:T(8,128)(2,1)}, bf16[128,3072]{1,0:T(8,128)(2,1)S(1)}, u32[]{:S(2)}) copy-start(bf16[128,3072]{1,0:T(8,128)(2,1)S(1)} %collective-permute-done.5.refs_6_) | copy-start | bytes 2359300
  113.4 0.9 copy-start.11
  122.4 1.0 copy-start.4
  131.2 30.8 %copy-start.6 = (bf16[128,128]{1,0:T(8,128)(2,1)S(1)}, bf16[128,128]{1,0:T(8,128)(2,1)}, u32[]{:S(2)}) copy-start(bf16[128,128]{1,0:T(8,128)(2,1)} %constant.4.clone.refs_16_) | copy-start | bytes 98308
  131.2 30.8 %copy-start.7 = (s32[4]{0:T(128)S(1)}, s32[4]{0:T(128)}, u32[]{:S(2)}) copy-start(s32[4]{0:T(128)} %offset_ref.5) | copy-start | bytes 52
  131.2 30.8 %copy-start.8 = (s32[33]{0:T(128)S(1)}, s32[33]{0:T(128)}, u32[]{:S(2)}) copy-start(s32[33]{0:T(128)} %steps_ref.3) | copy-start | bytes 400
  131.2 19.2 %collective-permute-start.15 = (bf16[2,4,128,256]{3,2,1,0:T(8,128)(2,1)S(1)}, bf16[2,4,128,256]{3,2,1,0:T(8,128)(2,1)S(1)}, u32[]{:S(2)}, u32[]{:S(2)}) collective-permute-start(bf16[2,4,128,256]{3,2,1,0:T(8,128)(2,1)S(1)} %shard_map.103.refs_0_), channel_id=1, source_target_pairs={{0,16},{16,32},{32,48},{48,0},{1,17},{17,33},{33,49},{49,1},{2,18}... | collective-permute-start | bytes 1572872 | tf_op jit(solution)/shard_map/ppermute | solution.py:59
  133.0 11.1 %collective-permute-start.24 = (bf16[768,256]{1,0:T(8,128)(2,1)}, bf16[768,256]{1,0:T(8,128)(2,1)S(1)}, u32[]{:S(2)}, u32[]{:S(2)}) collective-permute-start(bf16[768,256]{1,0:T(8,128)(2,1)} %bitcast.6.refs_10_), channel_id=1, source_target_pairs={{0,64},{64,128},{128,192},{192,0},{1,65},{65,129},{129,193},{193,1... | collective-permute-start | bytes 1179656 | tf_op jit(solution)/shard_map/ppermute | solution.py:59
  133.0 11.2 %collective-permute-start.25 = (bf16[768,256]{1,0:T(8,128)(2,1)}, bf16[768,256]{1,0:T(8,128)(2,1)S(1)}, u32[]{:S(2)}, u32[]{:S(2)}) collective-permute-start(bf16[768,256]{1,0:T(8,128)(2,1)} %bitcast.6.refs_10_), channel_id=1, source_target_pairs={{0,192},{64,0},{128,64},{192,128},{1,193},{65,1},{129,65},{193,129... | collective-permute-start | bytes 1179656 | tf_op jit(solution)/shard_map/ppermute | solution.py:59
  136.4 15.3 %collective-permute-start.16 = (bf16[2,4,128,256]{3,2,1,0:T(8,128)(2,1)S(1)}, bf16[2,4,128,256]{3,2,1,0:T(8,128)(2,1)S(1)}, u32[]{:S(2)}, u32[]{:S(2)}) collective-permute-start(bf16[2,4,128,256]{3,2,1,0:T(8,128)(2,1)S(1)} %shard_map.103.refs_0_), channel_id=1, source_target_pairs={{0,48},{16,0},{32,16},{48,32},{1,49},{17,1},{33,17},{49,33},{2,50}... | collective-permute-start | bytes 1572872 | tf_op jit(solution)/shard_map/ppermute | solution.py:59
  144.1 9.1 %collective-permute-start.26 = (bf16[384,256]{1,0:T(8,128)(2,1)S(1)}, bf16[384,256]{1,0:T(8,128)(2,1)S(1)}, u32[]{:S(2)}, u32[]{:S(2)}) collective-permute-start(bf16[384,256]{1,0:T(8,128)(2,1)S(1)} %slice.38), channel_id=1, source_target_pairs={{0,64},{64,128},{128,192},{192,0},{1,65},{65,129},{129,193},{193,1... | collective-permute-start | bytes 589832 | tf_op jit(solution)/shard_map/ppermute | solution.py:59
  144.2 9.6 %collective-permute-start.27 = (bf16[384,256]{1,0:T(8,128)(2,1)S(1)}, bf16[384,256]{1,0:T(8,128)(2,1)S(1)}, u32[]{:S(2)}, u32[]{:S(2)}) collective-permute-start(bf16[384,256]{1,0:T(8,128)(2,1)S(1)} %slice.39), channel_id=1, source_target_pairs={{0,192},{64,0},{128,64},{192,128},{1,193},{65,1},{129,65},{193,129... | collective-permute-start | bytes 589832 | tf_op jit(solution)/shard_map/ppermute | solution.py:59
  147.2 13.4 %collective-permute-start.19 = (bf16[2,4,128,256]{3,2,1,0:T(8,128)(2,1)S(1)}, bf16[2,4,128,256]{3,2,1,0:T(8,128)(2,1)S(1)}, u32[]{:S(2)}, u32[]{:S(2)}) collective-permute-start(bf16[2,4,128,256]{3,2,1,0:T(8,128)(2,1)S(1)} %shard_map.103.refs_0_), channel_id=1, source_target_pairs={{0,1},{1,0},{2,3},{3,2},{4,5},{5,4},{6,7},{7,6},{8,9},{9,8},{10,11... | collective-permute-start | bytes 1572872 | tf_op jit(solution)/shard_map/ppermute | solution.py:55
  150.4 9.2 %collective-permute-start.17 = (bf16[4,128,256]{2,1,0:T(8,128)(2,1)S(1)}, bf16[4,128,256]{2,1,0:T(8,128)(2,1)S(1)}, u32[]{:S(2)}, u32[]{:S(2)}) collective-permute-start(bf16[4,128,256]{2,1,0:T(8,128)(2,1)S(1)} %slice_bitcast_fusion.1), channel_id=1, source_target_pairs={{0,16},{16,32},{32,48},{48,0},{1,17},{17,33},{33,49},{49,1},{2,18}... | collective-permute-start | bytes 786440 | tf_op jit(solution)/shard_map/ppermute | solution.py:59
  151.8 8.6 %collective-permute-start.18 = (bf16[4,128,256]{2,1,0:T(8,128)(2,1)S(1)}, bf16[4,128,256]{2,1,0:T(8,128)(2,1)S(1)}, u32[]{:S(2)}, u32[]{:S(2)}) collective-permute-start(bf16[4,128,256]{2,1,0:T(8,128)(2,1)S(1)} %slice_bitcast_fusion), channel_id=1, source_target_pairs={{0,48},{16,0},{32,16},{48,32},{1,49},{17,1},{33,17},{49,33},{2,50}... | collective-permute-start | bytes 786440 | tf_op jit(solution)/shard_map/ppermute | solution.py:59
  153.3 8.7 %collective-permute-start.20 = (bf16[2,4,128,256]{3,2,1,0:T(8,128)(2,1)S(1)}, bf16[2,4,128,256]{3,2,1,0:T(8,128)(2,1)S(1)}, u32[]{:S(2)}, u32[]{:S(2)}) collective-permute-start(bf16[2,4,128,256]{3,2,1,0:T(8,128)(2,1)S(1)} %collective-permute-done.15.refs_1_), channel_id=1, source_target_pairs={{0,1},{1,0},{2,3},{3,2},{4,5},{5,4},{6,7},{7,6},{8,9},{9,8},{10,11... | collective-permute-start | bytes 1572872 | tf_op jit(solution)/shard_map/ppermute | solution.py:55
  153.8 8.1 %collective-permute-start.21 = (bf16[2,4,128,256]{3,2,1,0:T(8,128)(2,1)S(1)}, bf16[2,4,128,256]{3,2,1,0:T(8,128)(2,1)S(1)}, u32[]{:S(2)}, u32[]{:S(2)}) collective-permute-start(bf16[2,4,128,256]{3,2,1,0:T(8,128)(2,1)S(1)} %collective-permute-done.16.refs_2_), channel_id=1, source_target_pairs={{0,1},{1,0},{2,3},{3,2},{4,5},{5,4},{6,7},{7,6},{8,9},{9,8},{10,11... | collective-permute-start | bytes 1572872 | tf_op jit(solution)/shard_map/ppermute | solution.py:55
  159.6 1.9 collective-permute-start.22
  160.4 1.5 collective-permute-start.23
  168.0 29.6 %all-to-all-start.4 = ((bf16[64,16,384]{2,1,0:T(8,128)(2,1)}), bf16[64,16,384]{2,1,0:T(8,128)(2,1)S(1)}, u32[]{:S(2)}, u32[]{:S(2)}) async-start(bf16[64,16,384]{2,1,0:T(8,128)(2,1)} %bitcast.27), calls=%async_computation.4 | async-start | bytes 1572864 | tf_op jit(solution)/shard_map/all_to_all | solution.py:344
  197.6 35.6 %copy-start = (f32[1,4,32,3072]{3,2,1,0:T(8,128)S(1)}, f32[1,4,32,3072]{3,2,1,0:T(8,128)}, u32[]{:S(2)}) copy-start(f32[1,4,32,3072]{3,2,1,0:T(8,128)} %cur_ref.1) | copy-start | bytes 4718596
  197.6 35.6 %copy-start.5 = (bf16[128,128]{1,0:T(8,128)(2,1)S(1)}, bf16[128,128]{1,0:T(8,128)(2,1)}, u32[]{:S(2)}) copy-start(bf16[128,128]{1,0:T(8,128)(2,1)} %constant.5.clone.perm_ref) | copy-start | bytes 98308

commit v5 on v4

--- a/solution.py
+++ b/solution.py
@@ -179,12 +179,20 @@
 
 
 def attend_kernel(*refs):
-    weights = refs[10:12]
-    partial_ref, qg_ref, kg_ref, att_ref, tokens_ref, qkv_ref = refs[12:]
-    fill_tokens(tokens_ref, refs[:10])
+    mine, others, weights = refs[0:5], refs[5:10], refs[10:12]
+    partial_ref, qg_ref, kg_ref, att_ref, tokens_ref, weight_ref, qkv_ref = refs[12:]
+    half = TOKENS // 2
     start = lax.rem(lax.axis_index("y") + 2, NY) * WIDE
-    qkv_ref[...] = partial_ref[...] + product(tokens_ref, weights[0], start)
-    qkv_ref[...] += product(tokens_ref, weights[1], start + WIDE // 2)
+    columns = pl.ds(pl.multiple_of(start, HEAD), WIDE)
+    for side, pieces in enumerate((mine, others)):
+        for place in range(3):
+            tokens_ref[side * TS + place] = pieces[place][:, columns]
+        tokens_ref[side * TS + 3, :half] = pieces[3][:, columns]
+        tokens_ref[side * TS + 3, half:] = pieces[4][:, columns]
+    weight_ref[: WIDE // 2] = weights[0][...]
+    weight_ref[WIDE // 2 :] = weights[1][...]
+    tokens = tokens_ref[...].reshape(2 * TS * TOKENS, WIDE)
+    qkv_ref[...] = partial_ref[...] + dot(tokens, weight_ref[...])
 
     def part(index, column):
         here = slice(column * HEAD, (column + 1) * HEAD)
@@ -198,9 +206,10 @@
             queries = rms(part(index, 3 * head), qg_ref[...])
             keys = rms(part(index, 3 * head + 1), kg_ref[...])
             values = part(index, 3 * head + 2).astype(BF)
-            scores = dot_t(queries, keys) * (1.0 / math.sqrt(HEAD))
-            scores = jnp.exp(scores - jnp.max(scores, axis=-1, keepdims=True))
-            share = scores / jnp.sum(scores, axis=-1, keepdims=True)
+            scores = dot_t(queries, keys)
+            scores = scores - jnp.max(scores, axis=-1, keepdims=True)
+            scores = jnp.exp2(scores * (math.log2(math.e) / math.sqrt(HEAD)))
+            share = scores * (1.0 / jnp.sum(scores, axis=-1, keepdims=True))
             result = dot(share.astype(BF), values).astype(BF)
             at = head * HEAD
             att_ref[0, index, :, at : at + HEAD] = result[:TOKENS]
@@ -327,7 +336,11 @@
         shape(2, TS, TOKENS, 2 * HEAD),
         [VMEM] * 15,
         out_specs=VMEM,
-        scratch_shapes=scratch + [pltpu.VMEM((2 * TS * TOKENS, 6 * HEAD), F32)],
+        scratch_shapes=[
+            pltpu.VMEM((2 * TS, TOKENS, WIDE), BF),
+            pltpu.VMEM((WIDE, 6 * HEAD), BF),
+            pltpu.VMEM((2 * TS * TOKENS, 6 * HEAD), F32),
+        ],
     )(*tokens, *others, *weights[3:], partial, query_gain[None], k_gain[None])
 
     attended = ring(after(attended, state), "x", NX, lambda b: b[0], lambda b: b[1])

time: 237 us -> 236 us (level)
  no operation moved by 1% of the time
where the time goes in v5:
time: 236 us; the launch traced here: 235 us
  starting transfers between devices  82.8 us (35%)
  waiting for transfers between devices  81.5 us (35%)
  blocking collectives  34.9 us (15%)
  Pallas kernels  29.1 us (12%)
  local copies, waits for them, and re-layouts  6.15 us (3%)
    all_to_all x1, blocking collectives, body(): got = lax.all_to_all(sums, ('y', 'x', 'h'), 0, 0)  34.9 us
    ppermute x16, starting transfers between devices, shift(): return lax.ppermute(v, axis, [(i, (i + away) % size) for i in range(size)])  24.5 us
    ppermute x16, waiting for transfers between devices, shift(): return lax.ppermute(v, axis, [(i, (i + away) % size) for i in range(size)])  23.7 us
    all_to_all x1, waiting for transfers between devices, body(): lax.all_to_all(terms.reshape(64, TS * 4, COLS), ('y', 'h', 'z', 'c'), 0, 0)  21 us
    all_to_all x2, starting transfers between devices, spread(): return lax.all_to_all(copies, axes, 0, 0)  16 us
    ppermute x1, waiting for transfers between devices, body(): wo = lax.ppermute(w_out.T, AXES, TO_COLUMNS)  15.6 us
    ppermute x1, waiting for transfers between devices, body(): wq = lax.ppermute(w_qkv, AXES, TO_HEADS)  14.2 us
    ppermute x10, starting transfers between devices, other_core(): return lax.ppermute(v, 'c', [(0, 1), (1, 0)])  11.7 us
  transfers between devices with their start and end apart: 33, of which 12 were waited for; matrix products, arithmetic and copies ran while one was open for 1% of the time, Pallas kernels for 7%

profile of v5, /device:TPU:33, one launch (start us, length us, event | category | flops | bytes accessed | tf_op | source)
XLA Modules:
  0.0 234.8 jit_solution(12511763907785736623)
XLA Ops:
  0.0 3.8 %shard_map.101 = (bf16[4,32,3072]{2,1,0:T(8,128)(2,1)}, bf16[4,4,2,32,384]{4,3,2,1,0:T(8,128)(2,1)}) custom-call(s32[33]{0:T(128)} %steps_ref.3, f32[1,4,32,3072]{3,2,1,0:T(8,128)} %cur_ref.1, f32[3,66,3072]{2,1,0:T(8,128)} %bitcast.25), custom_call_target="tpu_custom_call" | custom-call | tf_op jit(solution)/shard_map/pallas_call | solution.py:300
  3.9 0.0 copy-start.12
  3.9 5.6 %all-to-all-start = ((bf16[4,32,3072]{2,1,0:T(8,128)(2,1)}), bf16[4,32,3072]{2,1,0:T(8,128)(2,1)S(1)}, u32[]{:S(2)}, u32[]{:S(2)}) async-start(bf16[4,32,3072]{2,1,0:T(8,128)(2,1)} %get-tuple-element.11), calls=%async_computation | async-start | bytes 1572864 | tf_op jit(solution)/shard_map/all_to_all | solution.py:314
  9.5 3.0 %collective-permute-start.9 = (bf16[96,768]{1,0:T(8,128)(2,1)S(1)}, bf16[96,768]{1,0:T(8,128)(2,1)S(1)}, u32[]{:S(2)}, u32[]{:S(2)}) collective-permute-start(bf16[96,768]{1,0:T(8,128)(2,1)S(1)} %copy-done.12), channel_id=1, source_target_pairs={{0,0},{1,1},{2,16},{3,17},{4,32},{5,33},{6,48},{7,49},{8,8},{9,9},... | collective-permute-start | bytes 442376 | tf_op jit(solution)/shard_map/ppermute | solution.py:298
  12.4 14.2 %collective-permute-done.9 = bf16[96,768]{1,0:T(8,128)(2,1)S(1)} collective-permute-done((bf16[96,768]{1,0:T(8,128)(2,1)S(1)}, bf16[96,768]{1,0:T(8,128)(2,1)S(1)}, u32[]{:S(2)}, u32[]{:S(2)}) %collective-permute-start.9) | collective-permute-done | bytes 147488 | tf_op jit(solution)/shard_map/ppermute | solution.py:298
  26.7 1.1 broadcast_in_dim.8
  27.8 12.0 %all-to-all-start.1 = ((bf16[8,96,768]{2,1,0:T(8,128)(2,1)}), bf16[8,96,768]{2,1,0:T(8,128)(2,1)}, u32[]{:S(2)}, u32[]{:S(2)}) async-start(bf16[8,96,768]{2,1,0:T(8,128)(2,1)} %broadcast_in_dim.8), calls=%async_computation.1 | async-start | bytes 2359296 | tf_op jit(solution)/shard_map/all_to_all | solution.py:51
  39.7 3.7 %collective-permute-start = (bf16[128,3072]{1,0:T(8,128)(2,1)S(1)}, bf16[128,3072]{1,0:T(8,128)(2,1)S(1)}, u32[]{:S(2)}, u32[]{:S(2)}) collective-permute-start(bf16[128,3072]{1,0:T(8,128)(2,1)S(1)} %bitcast.16), channel_id=1, source_target_pairs={{0,16},{16,32},{32,48},{48,0},{1,17},{17,33},{33,49},{49,1},{2,18}... | collective-permute-start | bytes 2359304 | tf_op jit(solution)/shard_map/ppermute | solution.py:59
  43.4 5.5 %collective-permute-start.14 = (bf16[96,256]{1,0:T(8,128)(2,1)S(1)}, bf16[96,256]{1,0:T(8,128)(2,1)S(1)}, u32[]{:S(2)}, u32[]{:S(2)}) collective-permute-start(bf16[96,256]{1,0:T(8,128)(2,1)S(1)} %bitcast.29), channel_id=1, source_target_pairs={{0,0},{1,64},{2,2},{3,66},{4,4},{5,68},{6,6},{7,70},{8,8},{9,72},{... | collective-permute-start | bytes 147464 | tf_op jit(solution)/shard_map/ppermute | solution.py:299
  48.9 15.6 %collective-permute-done.14 = bf16[96,256]{1,0:T(8,128)(2,1)S(1)} collective-permute-done((bf16[96,256]{1,0:T(8,128)(2,1)S(1)}, bf16[96,256]{1,0:T(8,128)(2,1)S(1)}, u32[]{:S(2)}, u32[]{:S(2)}) %collective-permute-start.14) | collective-permute-done | bytes 49184 | tf_op jit(solution)/shard_map/ppermute | solution.py:299
  64.5 4.2 %all-to-all-done.1 = bf16[8,96,768]{2,1,0:T(8,128)(2,1)} async-done(((bf16[8,96,768]{2,1,0:T(8,128)(2,1)}), bf16[8,96,768]{2,1,0:T(8,128)(2,1)}, u32[]{:S(2)}, u32[]{:S(2)}) %all-to-all-start.1) | async-done | bytes 1179680 | tf_op jit(solution)/shard_map/all_to_all | solution.py:51
  68.7 0.8 broadcast_in_dim.21
  69.5 4.0 %all-to-all-start.2 = ((bf16[8,96,256]{2,1,0:T(8,128)(2,1)}), bf16[8,96,256]{2,1,0:T(8,128)(2,1)}, u32[]{:S(2)}, u32[]{:S(2)}) async-start(bf16[8,96,256]{2,1,0:T(8,128)(2,1)} %broadcast_in_dim.21), calls=%async_computation.2 | async-start | bytes 786432 | tf_op jit(solution)/shard_map/all_to_all | solution.py:51
  73.5 1.4 collective-permute-start.10
  74.9 3.7 %collective-permute-start.2 = (bf16[64,3072]{1,0:T(8,128)(2,1)S(1)}, bf16[64,3072]{1,0:T(8,128)(2,1)S(1)}, u32[]{:S(2)}, u32[]{:S(2)}) collective-permute-start(bf16[64,3072]{1,0:T(8,128)(2,1)S(1)} %slice.32), channel_id=1, source_target_pairs={{0,16},{16,32},{32,48},{48,0},{1,17},{17,33},{33,49},{49,1},{2,18}... | collective-permute-start | bytes 1179656 | tf_op jit(solution)/shard_map/ppermute | solution.py:59
  78.7 0.1 collective-permute-start.3
  78.8 1.5 collective-permute-start.12
  80.3 4.8 %collective-permute-done.2.refs_3_ = bf16[64,3072]{1,0:T(8,128)(2,1)S(1)} collective-permute-done((bf16[64,3072]{1,0:T(8,128)(2,1)S(1)}, bf16[64,3072]{1,0:T(8,128)(2,1)S(1)}, u32[]{:S(2)}, u32[]{:S(2)}) %collective-permute-start.2) | collective-permute-done | bytes 393248 | tf_op jit(solution)/shard_map/ppermute | solution.py:59
  85.1 2.1 collective-permute-done.3.refs_4_
  87.2 9.2 %all-to-all-start.3 = ((bf16[32,32,384]{2,1,0:T(8,128)(2,1)}), bf16[32,32,384]{2,1,0:T(8,128)(2,1)}, u32[]{:S(2)}, u32[]{:S(2)}) async-start(bf16[32,32,384]{2,1,0:T(8,128)(2,1)} %bitcast.28), calls=%async_computation.3 | async-start | bytes 1572864 | tf_op jit(solution)/shard_map/all_to_all | solution.py:321
  96.4 0.4 collective-permute-start.4
  96.9 0.1 collective-permute-start.7
  97.0 0.4 collective-permute-start.5
  97.4 3.6 %collective-permute-done.10.refs_11_ = bf16[768,768]{1,0:T(8,128)(2,1)} collective-permute-done((bf16[768,768]{1,0:T(8,128)(2,1)}, bf16[768,768]{1,0:T(8,128)(2,1)}, u32[]{:S(2)}, u32[]{:S(2)}) %collective-permute-start.10) | collective-permute-done | bytes 1179680 | tf_op jit(solution)/shard_map/ppermute | solution.py:59
  101.0 2.5 %collective-permute-start.6 = (bf16[128,3072]{1,0:T(8,128)(2,1)S(1)}, bf16[128,3072]{1,0:T(8,128)(2,1)S(1)}, u32[]{:S(2)}, u32[]{:S(2)}) collective-permute-start(bf16[128,3072]{1,0:T(8,128)(2,1)S(1)} %collective-permute-done.1.refs_2_), channel_id=1, source_target_pairs={{0,1},{1,0},{2,3},{3,2},{4,5},{5,4},{6,7},{7,6},{8,9},{9,8},{10,11... | collective-permute-start | bytes 2359304 | tf_op jit(solution)/shard_map/ppermute | solution.py:55
  103.6 1.1 slice.34
  104.7 1.0 collective-permute-start.11
  105.7 1.1 slice.35
  106.8 0.0 copy-start.9
  106.8 0.0 copy-start.10
  106.8 0.0 copy-start.1
  106.8 1.8 collective-permute-start.13
  108.7 3.4 %collective-permute-start.8 = (bf16[64,3072]{1,0:T(8,128)(2,1)S(1)}, bf16[64,3072]{1,0:T(8,128)(2,1)S(1)}, u32[]{:S(2)}, u32[]{:S(2)}) collective-permute-start(bf16[64,3072]{1,0:T(8,128)(2,1)S(1)} %collective-permute-done.3.refs_4_), channel_id=1, source_target_pairs={{0,1},{1,0},{2,3},{3,2},{4,5},{5,4},{6,7},{7,6},{8,9},{9,8},{10,11... | collective-permute-start | bytes 1179656 | tf_op jit(solution)/shard_map/ppermute | solution.py:55
  112.0 1.3 collective-permute-done.8.refs_9_
  113.4 0.9 copy-done.11
  114.3 8.1 %shard_map.102.refs_12_ = f32[1024,768]{1,0:T(8,128)} custom-call(bf16[128,3072]{1,0:T(8,128)(2,1)S(1)} %bitcast.19, bf16[128,3072]{1,0:T(8,128)(2,1)S(1)} %collective-permute-done.refs_1_, bf16[128,3072]{1,0:T(8,128)(2,1)S(1)} %collective-permute-done.1.refs_2_, bf16[64,3072]{1,0:T(8,128)(2,1)S(1)} %collective-permute-done.2.refs_3_, ...), custom_call_target="tpu_custom_call" | custom-call | tf_op jit(solution)/shard_map/pallas_call | solution.py:327
  122.4 1.0 copy-done.4
  123.4 6.6 %shard_map.103.refs_0_ = bf16[2,4,128,256]{3,2,1,0:T(8,128)(2,1)S(1)} custom-call(bf16[128,3072]{1,0:T(8,128)(2,1)S(1)} %bitcast.20, bf16[128,3072]{1,0:T(8,128)(2,1)S(1)} %collective-permute-done.refs_1_, bf16[128,3072]{1,0:T(8,128)(2,1)S(1)} %collective-permute-done.1.refs_2_, bf16[64,3072]{1,0:T(8,128)(2,1)S(1)} %collective-permute-done.2.refs_3_, ...), custom_call_target="tpu_custom_call" | custom-call | tf_op jit(solution)/shard_map/pallas_call | solution.py:334
  130.0 0.0 copy-start.6
  130.0 0.0 copy-start.7
  130.0 0.0 copy-start.8
  130.0 1.8 collective-permute-start.15
  131.9 3.4 %collective-permute-start.25 = (bf16[768,256]{1,0:T(8,128)(2,1)}, bf16[768,256]{1,0:T(8,128)(2,1)S(1)}, u32[]{:S(2)}, u32[]{:S(2)}) collective-permute-start(bf16[768,256]{1,0:T(8,128)(2,1)} %bitcast.6.refs_10_), channel_id=1, source_target_pairs={{0,192},{64,0},{128,64},{192,128},{1,193},{65,1},{129,65},{193,129... | collective-permute-start | bytes 1179656 | tf_op jit(solution)/shard_map/ppermute | solution.py:59
  135.3 0.2 collective-permute-start.16
  135.5 7.5 %collective-permute-done.24.refs_11_ = bf16[768,256]{1,0:T(8,128)(2,1)S(1)} collective-permute-done((bf16[768,256]{1,0:T(8,128)(2,1)}, bf16[768,256]{1,0:T(8,128)(2,1)S(1)}, u32[]{:S(2)}, u32[]{:S(2)}) %collective-permute-start.24) | collective-permute-done | bytes 393248 | tf_op jit(solution)/shard_map/ppermute | solution.py:59
  142.9 0.1 collective-permute-start.26
  143.1 2.7 %collective-permute-start.27 = (bf16[384,256]{1,0:T(8,128)(2,1)S(1)}, bf16[384,256]{1,0:T(8,128)(2,1)S(1)}, u32[]{:S(2)}, u32[]{:S(2)}) collective-permute-start(bf16[384,256]{1,0:T(8,128)(2,1)S(1)} %slice.39), channel_id=1, source_target_pairs={{0,192},{64,0},{128,64},{192,128},{1,193},{65,1},{129,65},{193,129... | collective-permute-start | bytes 589832 | tf_op jit(solution)/shard_map/ppermute | solution.py:59
  145.8 3.2 %collective-permute-start.19 = (bf16[2,4,128,256]{3,2,1,0:T(8,128)(2,1)S(1)}, bf16[2,4,128,256]{3,2,1,0:T(8,128)(2,1)S(1)}, u32[]{:S(2)}, u32[]{:S(2)}) collective-permute-start(bf16[2,4,128,256]{3,2,1,0:T(8,128)(2,1)S(1)} %shard_map.103.refs_0_), channel_id=1, source_target_pairs={{0,1},{1,0},{2,3},{3,2},{4,5},{5,4},{6,7},{7,6},{8,9},{9,8},{10,11... | collective-permute-start | bytes 1572872 | tf_op jit(solution)/shard_map/ppermute | solution.py:55
  149.0 1.6 collective-permute-start.17
  150.6 1.4 collective-permute-start.18
  152.1 0.6 collective-permute-start.20
  152.6 0.1 collective-permute-start.21
  152.7 5.7 %collective-permute-done.17.refs_3_ = bf16[4,128,256]{2,1,0:T(8,128)(2,1)S(1)} collective-permute-done((bf16[4,128,256]{2,1,0:T(8,128)(2,1)S(1)}, bf16[4,128,256]{2,1,0:T(8,128)(2,1)S(1)}, u32[]{:S(2)}, u32[]{:S(2)}) %collective-permute-start.17) | collective-permute-done | bytes 262176 | tf_op jit(solution)/shard_map/ppermute | solution.py:59
  158.4 0.8 collective-permute-start.22
  159.2 0.2 collective-permute-start.23
  159.4 1.0 collective-permute-done.22.refs_8_
  160.4 0.4 collective-permute-done.23.refs_9_
  160.8 6.1 %shard_map.104 = bf16[8,4,2,16,384]{4,3,2,1,0:T(8,128)(2,1)} custom-call(s32[33]{0:T(128)S(1)} %copy-done.8, s32[4]{0:T(128)S(1)} %copy-done.7, f32[3,66,3072]{2,1,0:T(8,128)} %bitcast.26, bf16[2,4,128,256]{3,2,1,0:T(8,128)(2,1)S(1)} %shard_map.103.refs_0_, bf16[2,4,128,256]{3,2,1,0:T(8,128)(2,1)S(1)} %collective-permute-done.15.refs_1_, ...), custom_call_target="tpu_custom_call" | custom-call | tf_op jit(solution)/shard_map/pallas_call | solution.py:350
  166.9 7.4 %all-to-all-start.4 = ((bf16[64,16,384]{2,1,0:T(8,128)(2,1)}), bf16[64,16,384]{2,1,0:T(8,128)(2,1)S(1)}, u32[]{:S(2)}, u32[]{:S(2)}) async-start(bf16[64,16,384]{2,1,0:T(8,128)(2,1)} %bitcast.27), calls=%async_computation.4 | async-start | bytes 1572864 | tf_op jit(solution)/shard_map/all_to_all | solution.py:357
  174.3 1.1 shard_map.100.lower_ref
  175.4 21.0 %all-to-all-done.4 = bf16[64,16,384]{2,1,0:T(8,128)(2,1)S(1)} async-done(((bf16[64,16,384]{2,1,0:T(8,128)(2,1)}), bf16[64,16,384]{2,1,0:T(8,128)(2,1)S(1)}, u32[]{:S(2)}, u32[]{:S(2)}) %all-to-all-start.4) | async-done | bytes 786464 | tf_op jit(solution)/shard_map/all_to_all | solution.py:357
  196.4 0.7 shard_map.105
  197.2 34.9 %all_to_all.30 = bf16[32,16,768]{2,1,0:T(8,128)(2,1)S(1)} all-to-all(bf16[32,16,768]{2,1,0:T(8,128)(2,1)S(1)} %shard_map.105), channel_id=1, replica_groups=mesh['y'=4,'x'=4,'h'=2,'z'=4,'c'=2] {'y','x','h'}, dimensions={0} | all-to-all | bytes 1572864 | tf_op jit(solution)/shard_map/all_to_all | solution.py:361
  232.0 2.7 %shard_map.106 = f32[1,4,32,3072]{3,2,1,0:T(8,128)} custom-call(s32[4]{0:T(128)S(1)} %copy-done.7, bf16[4,4,2,16,768]{4,3,2,1,0:T(8,128)(2,1)S(1)} %bitcast.22, f32[1,4,32,3072]{3,2,1,0:T(8,128)S(1)} %copy-done, bf16[128,128]{1,0:T(8,128)(2,1)S(1)} %copy-done.5), custom_call_target="tpu_custom_call" | custom-call | tf_op jit(solution)/shard_map/pallas_call | solution.py:362
  (48 shorter events, 0.2 us)
Async XLA Ops:
  3.9 5.6 %copy-start.12 = (bf16[96,768]{1,0:T(8,128)(2,1)S(1)}, bf16[96,768]{1,0:T(8,128)(2,1)}, u32[]{:S(2)}) copy-start(bf16[96,768]{1,0:T(8,128)(2,1)} %param.14) | copy-start | bytes 442372
  3.9 22.8 %all-to-all-start = ((bf16[4,32,3072]{2,1,0:T(8,128)(2,1)}), bf16[4,32,3072]{2,1,0:T(8,128)(2,1)S(1)}, u32[]{:S(2)}, u32[]{:S(2)}) async-start(bf16[4,32,3072]{2,1,0:T(8,128)(2,1)} %get-tuple-element.11), calls=%async_computation | async-start | bytes 1572864 | tf_op jit(solution)/shard_map/all_to_all | solution.py:314
  9.5 33.9 %copy-start.13 = (bf16[256,96]{0,1:T(8,128)(2,1)S(1)}, bf16[256,96]{0,1:T(8,128)(2,1)}, u32[]{:S(2)}) copy-start(bf16[256,96]{0,1:T(8,128)(2,1)} %param.15) | copy-start | bytes 147460
  9.5 17.2 %collective-permute-start.9 = (bf16[96,768]{1,0:T(8,128)(2,1)S(1)}, bf16[96,768]{1,0:T(8,128)(2,1)S(1)}, u32[]{:S(2)}, u32[]{:S(2)}) collective-permute-start(bf16[96,768]{1,0:T(8,128)(2,1)S(1)} %copy-done.12), channel_id=1, source_target_pairs={{0,0},{1,1},{2,16},{3,17},{4,32},{5,33},{6,48},{7,49},{8,8},{9,9},... | collective-permute-start | bytes 442376 | tf_op jit(solution)/shard_map/ppermute | solution.py:298
  27.8 40.9 %all-to-all-start.1 = ((bf16[8,96,768]{2,1,0:T(8,128)(2,1)}), bf16[8,96,768]{2,1,0:T(8,128)(2,1)}, u32[]{:S(2)}, u32[]{:S(2)}) async-start(bf16[8,96,768]{2,1,0:T(8,128)(2,1)} %broadcast_in_dim.8), calls=%async_computation.1 | async-start | bytes 2359296 | tf_op jit(solution)/shard_map/all_to_all | solution.py:51
  39.7 35.2 %collective-permute-start = (bf16[128,3072]{1,0:T(8,128)(2,1)S(1)}, bf16[128,3072]{1,0:T(8,128)(2,1)S(1)}, u32[]{:S(2)}, u32[]{:S(2)}) collective-permute-start(bf16[128,3072]{1,0:T(8,128)(2,1)S(1)} %bitcast.16), channel_id=1, source_target_pairs={{0,16},{16,32},{32,48},{48,0},{1,17},{17,33},{33,49},{49,1},{2,18}... | collective-permute-start | bytes 2359304 | tf_op jit(solution)/shard_map/ppermute | solution.py:59
  43.4 35.3 %collective-permute-start.1 = (bf16[128,3072]{1,0:T(8,128)(2,1)S(1)}, bf16[128,3072]{1,0:T(8,128)(2,1)S(1)}, u32[]{:S(2)}, u32[]{:S(2)}) collective-permute-start(bf16[128,3072]{1,0:T(8,128)(2,1)S(1)} %bitcast.17), channel_id=1, source_target_pairs={{0,48},{16,0},{32,16},{48,32},{1,49},{17,1},{33,17},{49,33},{2,50}... | collective-permute-start | bytes 2359304 | tf_op jit(solution)/shard_map/ppermute | solution.py:59
  43.4 21.1 %collective-permute-start.14 = (bf16[96,256]{1,0:T(8,128)(2,1)S(1)}, bf16[96,256]{1,0:T(8,128)(2,1)S(1)}, u32[]{:S(2)}, u32[]{:S(2)}) collective-permute-start(bf16[96,256]{1,0:T(8,128)(2,1)S(1)} %bitcast.29), channel_id=1, source_target_pairs={{0,0},{1,64},{2,2},{3,66},{4,4},{5,68},{6,6},{7,70},{8,8},{9,72},{... | collective-permute-start | bytes 147464 | tf_op jit(solution)/shard_map/ppermute | solution.py:299
  69.5 17.8 %all-to-all-start.2 = ((bf16[8,96,256]{2,1,0:T(8,128)(2,1)}), bf16[8,96,256]{2,1,0:T(8,128)(2,1)}, u32[]{:S(2)}, u32[]{:S(2)}) async-start(bf16[8,96,256]{2,1,0:T(8,128)(2,1)} %broadcast_in_dim.21), calls=%async_computation.2 | async-start | bytes 786432 | tf_op jit(solution)/shard_map/all_to_all | solution.py:51
  73.5 27.5 %collective-permute-start.10 = (bf16[768,768]{1,0:T(8,128)(2,1)}, bf16[768,768]{1,0:T(8,128)(2,1)}, u32[]{:S(2)}, u32[]{:S(2)}) collective-permute-start(bf16[768,768]{1,0:T(8,128)(2,1)} %bitcast.2.refs_10_), channel_id=1, source_target_pairs={{0,64},{64,128},{128,192},{192,0},{1,65},{65,129},{129,193},{193,1... | collective-permute-start | bytes 3538952 | tf_op jit(solution)/shard_map/ppermute | solution.py:59
  74.9 10.2 %collective-permute-start.2 = (bf16[64,3072]{1,0:T(8,128)(2,1)S(1)}, bf16[64,3072]{1,0:T(8,128)(2,1)S(1)}, u32[]{:S(2)}, u32[]{:S(2)}) collective-permute-start(bf16[64,3072]{1,0:T(8,128)(2,1)S(1)} %slice.32), channel_id=1, source_target_pairs={{0,16},{16,32},{32,48},{48,0},{1,17},{17,33},{33,49},{49,1},{2,18}... | collective-permute-start | bytes 1179656 | tf_op jit(solution)/shard_map/ppermute | solution.py:59
  78.7 8.5 %collective-permute-start.3 = (bf16[64,3072]{1,0:T(8,128)(2,1)S(1)}, bf16[64,3072]{1,0:T(8,128)(2,1)S(1)}, u32[]{:S(2)}, u32[]{:S(2)}) collective-permute-start(bf16[64,3072]{1,0:T(8,128)(2,1)S(1)} %slice.33), channel_id=1, source_target_pairs={{0,48},{16,0},{32,16},{48,32},{1,49},{17,1},{33,17},{49,33},{2,50}... | collective-permute-start | bytes 1179656 | tf_op jit(solution)/shard_map/ppermute | solution.py:59
  78.8 25.9 %collective-permute-start.12 = (bf16[768,768]{1,0:T(8,128)(2,1)}, bf16[768,768]{1,0:T(8,128)(2,1)}, u32[]{:S(2)}, u32[]{:S(2)}) collective-permute-start(bf16[768,768]{1,0:T(8,128)(2,1)} %bitcast.2.refs_10_), channel_id=1, source_target_pairs={{0,192},{64,0},{128,64},{192,128},{1,193},{65,1},{129,65},{193,129... | collective-permute-start | bytes 3538952 | tf_op jit(solution)/shard_map/ppermute | solution.py:59
  87.2 26.2 %copy-start.3 = (bf16[64,3072]{1,0:T(8,128)(2,1)}, bf16[64,3072]{1,0:T(8,128)(2,1)S(1)}, u32[]{:S(2)}) copy-start(bf16[64,3072]{1,0:T(8,128)(2,1)S(1)} %collective-permute-done.3.refs_4_) | copy-start | bytes 1179652
  87.2 42.8 %all-to-all-start.3 = ((bf16[32,32,384]{2,1,0:T(8,128)(2,1)}), bf16[32,32,384]{2,1,0:T(8,128)(2,1)}, u32[]{:S(2)}, u32[]{:S(2)}) async-start(bf16[32,32,384]{2,1,0:T(8,128)(2,1)} %bitcast.28), calls=%async_computation.3 | async-start | bytes 1572864 | tf_op jit(solution)/shard_map/all_to_all | solution.py:321
  96.4 10.4 %collective-permute-start.4 = (bf16[128,3072]{1,0:T(8,128)(2,1)S(1)}, bf16[128,3072]{1,0:T(8,128)(2,1)S(1)}, u32[]{:S(2)}, u32[]{:S(2)}) collective-permute-start(bf16[128,3072]{1,0:T(8,128)(2,1)S(1)} %bitcast.18), channel_id=1, source_target_pairs={{0,1},{1,0},{2,3},{3,2},{4,5},{5,4},{6,7},{7,6},{8,9},{9,8},{10,11... | collective-permute-start | bytes 2359304 | tf_op jit(solution)/shard_map/ppermute | solution.py:55
  96.9 11.8 %collective-permute-start.7 = (bf16[64,3072]{1,0:T(8,128)(2,1)S(1)}, bf16[64,3072]{1,0:T(8,128)(2,1)S(1)}, u32[]{:S(2)}, u32[]{:S(2)}) collective-permute-start(bf16[64,3072]{1,0:T(8,128)(2,1)S(1)} %collective-permute-done.2.refs_3_), channel_id=1, source_target_pairs={{0,1},{1,0},{2,3},{3,2},{4,5},{5,4},{6,7},{7,6},{8,9},{9,8},{10,11... | collective-permute-start | bytes 1179656 | tf_op jit(solution)/shard_map/ppermute | solution.py:55
  97.0 16.3 %collective-permute-start.5 = (bf16[128,3072]{1,0:T(8,128)(2,1)S(1)}, bf16[128,3072]{1,0:T(8,128)(2,1)S(1)}, u32[]{:S(2)}, u32[]{:S(2)}) collective-permute-start(bf16[128,3072]{1,0:T(8,128)(2,1)S(1)} %collective-permute-done.refs_1_), channel_id=1, source_target_pairs={{0,1},{1,0},{2,3},{3,2},{4,5},{5,4},{6,7},{7,6},{8,9},{9,8},{10,11... | collective-permute-start | bytes 2359304 | tf_op jit(solution)/shard_map/ppermute | solution.py:55
  101.0 12.4 %collective-permute-start.6 = (bf16[128,3072]{1,0:T(8,128)(2,1)S(1)}, bf16[128,3072]{1,0:T(8,128)(2,1)S(1)}, u32[]{:S(2)}, u32[]{:S(2)}) collective-permute-start(bf16[128,3072]{1,0:T(8,128)(2,1)S(1)} %collective-permute-done.1.refs_2_), channel_id=1, source_target_pairs={{0,1},{1,0},{2,3},{3,2},{4,5},{5,4},{6,7},{7,6},{8,9},{9,8},{10,11... | collective-permute-start | bytes 2359304 | tf_op jit(solution)/shard_map/ppermute | solution.py:55
  104.7 17.7 %collective-permute-start.11 = (bf16[384,768]{1,0:T(8,128)(2,1)S(1)}, bf16[384,768]{1,0:T(8,128)(2,1)S(1)}, u32[]{:S(2)}, u32[]{:S(2)}) collective-permute-start(bf16[384,768]{1,0:T(8,128)(2,1)S(1)} %slice.34), channel_id=1, source_target_pairs={{0,64},{64,128},{128,192},{192,0},{1,65},{65,129},{129,193},{193,1... | collective-permute-start | bytes 1769480 | tf_op jit(solution)/shard_map/ppermute | solution.py:59
  106.8 15.6 %copy-start.9 = (f32[128]{0:T(128)S(1)}, f32[128]{0:T(128)}, u32[]{:S(2)}) copy-start(f32[128]{0:T(128)} %param.16) | copy-start | bytes 1540
  106.8 15.6 %copy-start.10 = (f32[128]{0:T(128)S(1)}, f32[128]{0:T(128)}, u32[]{:S(2)}) copy-start(f32[128]{0:T(128)} %param.17) | copy-start | bytes 1540
  106.8 15.6 %copy-start.1 = (bf16[128,3072]{1,0:T(8,128)(2,1)}, bf16[128,3072]{1,0:T(8,128)(2,1)S(1)}, u32[]{:S(2)}) copy-start(bf16[128,3072]{1,0:T(8,128)(2,1)S(1)} %collective-permute-done.4.refs_5_) | copy-start | bytes 2359300
  106.8 15.6 %collective-permute-start.13 = (bf16[384,768]{1,0:T(8,128)(2,1)S(1)}, bf16[384,768]{1,0:T(8,128)(2,1)S(1)}, u32[]{:S(2)}, u32[]{:S(2)}) collective-permute-start(bf16[384,768]{1,0:T(8,128)(2,1)S(1)} %slice.35), channel_id=1, source_target_pairs={{0,192},{64,0},{128,64},{192,128},{1,193},{65,1},{129,65},{193,129... | collective-permute-start | bytes 1769480 | tf_op jit(solution)/shard_map/ppermute | solution.py:59
  108.7 4.7 %collective-permute-start.8 = (bf16[64,3072]{1,0:T(8,128)(2,1)S(1)}, bf16[64,3072]{1,0:T(8,128)(2,1)S(1)}, u32[]{:S(2)}, u32[]{:S(2)}) collective-permute-start(bf16[64,3072]{1,0:T(8,128)(2,1)S(1)} %collective-permute-done.3.refs_4_), channel_id=1, source_target_pairs={{0,1},{1,0},{2,3},{3,2},{4,5},{5,4},{6,7},{7,6},{8,9},{9,8},{10,11... | collective-permute-start | bytes 1179656 | tf_op jit(solution)/shard_map/ppermute | solution.py:55
  113.4 9.0 %copy-start.2 = (bf16[128,3072]{1,0:T(8,128)(2,1)}, bf16[128,3072]{1,0:T(8,128)(2,1)S(1)}, u32[]{:S(2)}) copy-start(bf16[128,3072]{1,0:T(8,128)(2,1)S(1)} %collective-permute-done.5.refs_6_) | copy-start | bytes 2359300
  113.4 0.9 copy-start.11
  122.4 1.0 copy-start.4
  130.0 30.8 %copy-start.6 = (bf16[128,128]{1,0:T(8,128)(2,1)S(1)}, bf16[128,128]{1,0:T(8,128)(2,1)}, u32[]{:S(2)}) copy-start(bf16[128,128]{1,0:T(8,128)(2,1)} %constant.4.clone.refs_16_) | copy-start | bytes 98308
  130.0 30.8 %copy-start.7 = (s32[4]{0:T(128)S(1)}, s32[4]{0:T(128)}, u32[]{:S(2)}) copy-start(s32[4]{0:T(128)} %offset_ref.5) | copy-start | bytes 52
  130.0 30.8 %copy-start.8 = (s32[33]{0:T(128)S(1)}, s32[33]{0:T(128)}, u32[]{:S(2)}) copy-start(s32[33]{0:T(128)} %steps_ref.3) | copy-start | bytes 400
  130.0 18.9 %collective-permute-start.15 = (bf16[2,4,128,256]{3,2,1,0:T(8,128)(2,1)S(1)}, bf16[2,4,128,256]{3,2,1,0:T(8,128)(2,1)S(1)}, u32[]{:S(2)}, u32[]{:S(2)}) collective-permute-start(bf16[2,4,128,256]{3,2,1,0:T(8,128)(2,1)S(1)} %shard_map.103.refs_0_), channel_id=1, source_target_pairs={{0,16},{16,32},{32,48},{48,0},{1,17},{17,33},{33,49},{49,1},{2,18}... | collective-permute-start | bytes 1572872 | tf_op jit(solution)/shard_map/ppermute | solution.py:59
  131.9 11.1 %collective-permute-start.24 = (bf16[768,256]{1,0:T(8,128)(2,1)}, bf16[768,256]{1,0:T(8,128)(2,1)S(1)}, u32[]{:S(2)}, u32[]{:S(2)}) collective-permute-start(bf16[768,256]{1,0:T(8,128)(2,1)} %bitcast.6.refs_10_), channel_id=1, source_target_pairs={{0,64},{64,128},{128,192},{192,0},{1,65},{65,129},{129,193},{193,1... | collective-permute-start | bytes 1179656 | tf_op jit(solution)/shard_map/ppermute | solution.py:59
  131.9 11.2 %collective-permute-start.25 = (bf16[768,256]{1,0:T(8,128)(2,1)}, bf16[768,256]{1,0:T(8,128)(2,1)S(1)}, u32[]{:S(2)}, u32[]{:S(2)}) collective-permute-start(bf16[768,256]{1,0:T(8,128)(2,1)} %bitcast.6.refs_10_), channel_id=1, source_target_pairs={{0,192},{64,0},{128,64},{192,128},{1,193},{65,1},{129,65},{193,129... | collective-permute-start | bytes 1179656 | tf_op jit(solution)/shard_map/ppermute | solution.py:59
  135.3 15.3 %collective-permute-start.16 = (bf16[2,4,128,256]{3,2,1,0:T(8,128)(2,1)S(1)}, bf16[2,4,128,256]{3,2,1,0:T(8,128)(2,1)S(1)}, u32[]{:S(2)}, u32[]{:S(2)}) collective-permute-start(bf16[2,4,128,256]{3,2,1,0:T(8,128)(2,1)S(1)} %shard_map.103.refs_0_), channel_id=1, source_target_pairs={{0,48},{16,0},{32,16},{48,32},{1,49},{17,1},{33,17},{49,33},{2,50}... | collective-permute-start | bytes 1572872 | tf_op jit(solution)/shard_map/ppermute | solution.py:59
  142.9 9.1 %collective-permute-start.26 = (bf16[384,256]{1,0:T(8,128)(2,1)S(1)}, bf16[384,256]{1,0:T(8,128)(2,1)S(1)}, u32[]{:S(2)}, u32[]{:S(2)}) collective-permute-start(bf16[384,256]{1,0:T(8,128)(2,1)S(1)} %slice.38), channel_id=1, source_target_pairs={{0,64},{64,128},{128,192},{192,0},{1,65},{65,129},{129,193},{193,1... | collective-permute-start | bytes 589832 | tf_op jit(solution)/shard_map/ppermute | solution.py:59
  143.1 9.6 %collective-permute-start.27 = (bf16[384,256]{1,0:T(8,128)(2,1)S(1)}, bf16[384,256]{1,0:T(8,128)(2,1)S(1)}, u32[]{:S(2)}, u32[]{:S(2)}) collective-permute-start(bf16[384,256]{1,0:T(8,128)(2,1)S(1)} %slice.39), channel_id=1, source_target_pairs={{0,192},{64,0},{128,64},{192,128},{1,193},{65,1},{129,65},{193,129... | collective-permute-start | bytes 589832 | tf_op jit(solution)/shard_map/ppermute | solution.py:59
  145.8 13.6 %collective-permute-start.19 = (bf16[2,4,128,256]{3,2,1,0:T(8,128)(2,1)S(1)}, bf16[2,4,128,256]{3,2,1,0:T(8,128)(2,1)S(1)}, u32[]{:S(2)}, u32[]{:S(2)}) collective-permute-start(bf16[2,4,128,256]{3,2,1,0:T(8,128)(2,1)S(1)} %shard_map.103.refs_0_), channel_id=1, source_target_pairs={{0,1},{1,0},{2,3},{3,2},{4,5},{5,4},{6,7},{7,6},{8,9},{9,8},{10,11... | collective-permute-start | bytes 1572872 | tf_op jit(solution)/shard_map/ppermute | solution.py:55
  149.0 9.4 %collective-permute-start.17 = (bf16[4,128,256]{2,1,0:T(8,128)(2,1)S(1)}, bf16[4,128,256]{2,1,0:T(8,128)(2,1)S(1)}, u32[]{:S(2)}, u32[]{:S(2)}) collective-permute-start(bf16[4,128,256]{2,1,0:T(8,128)(2,1)S(1)} %slice_bitcast_fusion.1), channel_id=1, source_target_pairs={{0,16},{16,32},{32,48},{48,0},{1,17},{17,33},{33,49},{49,1},{2,18}... | collective-permute-start | bytes 786440 | tf_op jit(solution)/shard_map/ppermute | solution.py:59
  150.6 8.6 %collective-permute-start.18 = (bf16[4,128,256]{2,1,0:T(8,128)(2,1)S(1)}, bf16[4,128,256]{2,1,0:T(8,128)(2,1)S(1)}, u32[]{:S(2)}, u32[]{:S(2)}) collective-permute-start(bf16[4,128,256]{2,1,0:T(8,128)(2,1)S(1)} %slice_bitcast_fusion), channel_id=1, source_target_pairs={{0,48},{16,0},{32,16},{48,32},{1,49},{17,1},{33,17},{49,33},{2,50}... | collective-permute-start | bytes 786440 | tf_op jit(solution)/shard_map/ppermute | solution.py:59
  152.1 8.7 %collective-permute-start.20 = (bf16[2,4,128,256]{3,2,1,0:T(8,128)(2,1)S(1)}, bf16[2,4,128,256]{3,2,1,0:T(8,128)(2,1)S(1)}, u32[]{:S(2)}, u32[]{:S(2)}) collective-permute-start(bf16[2,4,128,256]{3,2,1,0:T(8,128)(2,1)S(1)} %collective-permute-done.15.refs_1_), channel_id=1, source_target_pairs={{0,1},{1,0},{2,3},{3,2},{4,5},{5,4},{6,7},{7,6},{8,9},{9,8},{10,11... | collective-permute-start | bytes 1572872 | tf_op jit(solution)/shard_map/ppermute | solution.py:55
  152.6 8.1 %collective-permute-start.21 = (bf16[2,4,128,256]{3,2,1,0:T(8,128)(2,1)S(1)}, bf16[2,4,128,256]{3,2,1,0:T(8,128)(2,1)S(1)}, u32[]{:S(2)}, u32[]{:S(2)}) collective-permute-start(bf16[2,4,128,256]{3,2,1,0:T(8,128)(2,1)S(1)} %collective-permute-done.16.refs_2_), channel_id=1, source_target_pairs={{0,1},{1,0},{2,3},{3,2},{4,5},{5,4},{6,7},{7,6},{8,9},{9,8},{10,11... | collective-permute-start | bytes 1572872 | tf_op jit(solution)/shard_map/ppermute | solution.py:55
  158.4 1.9 collective-permute-start.22
  159.2 1.5 collective-permute-start.23
  166.9 29.6 %all-to-all-start.4 = ((bf16[64,16,384]{2,1,0:T(8,128)(2,1)}), bf16[64,16,384]{2,1,0:T(8,128)(2,1)S(1)}, u32[]{:S(2)}, u32[]{:S(2)}) async-start(bf16[64,16,384]{2,1,0:T(8,128)(2,1)} %bitcast.27), calls=%async_computation.4 | async-start | bytes 1572864 | tf_op jit(solution)/shard_map/all_to_all | solution.py:357
  196.4 35.6 %copy-start = (f32[1,4,32,3072]{3,2,1,0:T(8,128)S(1)}, f32[1,4,32,3072]{3,2,1,0:T(8,128)}, u32[]{:S(2)}) copy-start(f32[1,4,32,3072]{3,2,1,0:T(8,128)} %cur_ref.1) | copy-start | bytes 4718596
  196.4 35.6 %copy-start.5 = (bf16[128,128]{1,0:T(8,128)(2,1)S(1)}, bf16[128,128]{1,0:T(8,128)(2,1)}, u32[]{:S(2)}) copy-start(bf16[128,128]{1,0:T(8,128)(2,1)} %constant.5.clone.perm_ref) | copy-start | bytes 98308
